TPU v7x, 128 devices: a whole 4x4x4 slice. The times are simulated.
128 devices in a mesh: blk: 64 (over x, y, z_lo, core), rep: 2 (over z_hi).
Axes of the slice: x: 4, y: 4, z: 4 (z_hi: 2, z_lo: 2; z = z_hi * 2 + z_lo), core: 2. Of those that a mesh axis runs over, the one named last changes fastest.
Arguments:
- query_in: bfloat16 [32768, 1024], P(('blk', 'rep')), may hold values from -12 to 12
- doc_in: bfloat16 [32768, 1024], P(('blk', 'rep')), may hold values from -12 to 12
- cluster: int32 [32768], P(('blk', 'rep')), may hold values from 0 to 127, never falling along the last dimension, each value on 1 to 384 neighbouring positions
- gain: float32 [1024], replicated, may hold values from 0.5 to 1.5
- w_in: bfloat16 [1024, 4096], P(None, 'rep'), may hold values from -0.1875 to 0.1875
- w_out: bfloat16 [4096, 1024], P('rep'), may hold values from -0.09375 to 0.09375
Outputs:
- loss: float32 [], replicated
- grad_down: float32 [4096, 1024], P('rep', 'blk')
- grad_gain: float32 [1024], replicated
- grad_query_in: bfloat16 [32768, 1024], P(('blk', 'rep'))
- grad_doc_in: bfloat16 [32768, 1024], P(('blk', 'rep'))
Inputs may be any that keep to these rules, and one draw needn't show every extreme that they name: Never falls along the pairs; each cluster holds 1 to 384 consecutive pairs, one exactly 384.
All inputs are finite; a program needn't handle non-finite values.
Results may differ from a plain program's by a relative error of at most 0.015.
Values may be sent and summed in bfloat16 or wider, within the bound.
A program may use at most 128 MiB of HBM per device.

v0:
```python
import math

import jax
import jax.numpy as jnp
from jax import lax
from jax.sharding import PartitionSpec as P

BAND = 2


epsilon = 1e-06


def from_behind(x, axis, by):
    devices = lax.axis_size(axis)
    return lax.ppermute(x, axis, [(i, (i + by) % devices) for i in range(devices)])


def shard_scores(query_emb, band_docs, query_cluster, band_cluster, positive):
    inv_root = 1.0 / math.sqrt(query_emb.shape[1])
    scores = (
        lax.dot_general(
            query_emb, band_docs, (((1,), (1,)), ((), ())), preferred_element_type=jnp.float32
        )
        * inv_root
    )
    columns = jnp.arange(band_docs.shape[0], dtype=jnp.int32)[None, :]
    is_positive = columns == positive[:, None]
    allowed = (band_cluster[None, :] != query_cluster[:, None]) | is_positive
    masked = jnp.where(allowed, scores, -jnp.inf)
    row_max = jnp.max(masked, axis=1, keepdims=True)
    log_total = row_max + jnp.log(jnp.sum(jnp.exp(masked - row_max), axis=1, keepdims=True))
    positive_score = jnp.sum(jnp.where(is_positive, scores, 0.0), axis=1)
    loss_part = jnp.sum(log_total[:, 0] - positive_score)
    weights = (jnp.exp(masked - log_total) - is_positive.astype(jnp.float32)).astype(jnp.bfloat16)
    return (weights, loss_part)


def on_device(query_in, doc_in, cluster, gain, w_in, w_out):
    pair_rows = query_in.shape[0]
    feature_count = query_in.shape[1]
    rep_count = lax.axis_size("rep")
    blocks = lax.axis_size("blk")
    shard_rows = pair_rows * rep_count
    inv_root = 1.0 / math.sqrt(feature_count)
    band_span = 2 * BAND + 1
    rows_in = jnp.concatenate([query_in, doc_in], axis=0)
    values = rows_in.astype(jnp.float32)
    inv_rms = lax.rsqrt(jnp.mean(values * values, axis=-1, keepdims=True) + epsilon)
    unit_rows = values * inv_rms
    normed = (unit_rows * gain).astype(jnp.bfloat16)
    inner_full = lax.all_gather(w_in, "rep", axis=1, tiled=True)
    outer_full = lax.all_gather(w_out, "rep", axis=0, tiled=True)
    pre_act = jnp.dot(normed, inner_full, preferred_element_type=jnp.float32)
    hidden = jax.nn.gelu(pre_act, approximate=True).astype(jnp.bfloat16)
    mixed_out = jnp.dot(hidden, outer_full, preferred_element_type=jnp.float32)
    embedded = (values + mixed_out).astype(jnp.bfloat16)
    query_emb = embedded[:pair_rows]
    doc_emb = embedded[pair_rows:]
    offsets = list(range(-BAND, BAND + 1))
    whole_docs, whole_groups = (
        lax.all_gather(doc_emb, "rep", axis=0, tiled=True),
        lax.all_gather(cluster, "rep", axis=0, tiled=True),
    )
    doc_pieces = []
    group_pieces = []
    for offset in offsets:
        if offset == 0:
            moved = (whole_docs, whole_groups)
        else:
            moved = from_behind((whole_docs, whole_groups), "blk", -offset)
        doc_pieces.append(moved[0])
        group_pieces.append(moved[1])
    band_docs = jnp.concatenate(doc_pieces, axis=0)
    band_groups = jnp.concatenate(group_pieces, axis=0)
    positive = (
        BAND * shard_rows
        + lax.axis_index("rep") * pair_rows
        + jnp.arange(pair_rows, dtype=jnp.int32)
    )
    weights, loss_part = shard_scores(query_emb, band_docs, cluster, band_groups, positive)
    query_grad = (
        jnp.dot(weights, band_docs, preferred_element_type=jnp.float32) * inv_root
    ).astype(jnp.bfloat16)
    partial_value = (
        lax.dot_general(
            weights, query_emb, (((0,), (0,)), ((), ())), preferred_element_type=jnp.float32
        )
        * inv_root
    ).astype(jnp.bfloat16)
    partial_blocks = partial_value.reshape(band_span, shard_rows, feature_count)
    summed = jnp.zeros((shard_rows, feature_count), jnp.float32)
    for slot_index, offset in enumerate(offsets):
        moved = partial_blocks[slot_index]
        if offset != 0:
            moved = from_behind(moved, "blk", offset)
        summed = summed + lax.optimization_barrier(moved).astype(jnp.float32)
    summed = lax.psum_scatter(
        summed.astype(jnp.bfloat16), "rep", scatter_dimension=0, tiled=True
    ).astype(jnp.float32)
    doc_grad = summed.astype(jnp.bfloat16)
    upstream = jnp.concatenate([query_grad, doc_grad], axis=0)
    g_act = lax.dot_general(
        upstream, outer_full, (((1,), (1,)), ((), ())), preferred_element_type=jnp.float32
    )
    g_pre = jax.vjp(lambda p: jax.nn.gelu(p, approximate=True), pre_act)[1](g_act)[0].astype(
        jnp.bfloat16
    )
    g_norm = lax.dot_general(
        g_pre, inner_full, (((1,), (1,)), ((), ())), preferred_element_type=jnp.float32
    )
    down_term = lax.dot_general(
        hidden, upstream, (((0,), (0,)), ((), ())), preferred_element_type=jnp.float32
    )
    down_half = lax.psum_scatter(
        down_term.astype(jnp.bfloat16), "rep", scatter_dimension=0, tiled=True
    ).astype(jnp.float32)
    grad_down = lax.psum_scatter(down_half, "blk", scatter_dimension=1, tiled=True)
    gain_term = jnp.sum(g_norm * unit_rows, axis=0)
    d_unit = g_norm * gain
    d_values = inv_rms * (d_unit - unit_rows * jnp.mean(d_unit * unit_rows, axis=-1, keepdims=True))
    grad_rows = (upstream.astype(jnp.float32) + d_values).astype(jnp.bfloat16)
    loss_total, gain_total = lax.psum((loss_part, gain_term), ("blk", "rep"))
    loss = loss_total / (pair_rows * rep_count * blocks)
    return (loss, grad_down, gain_total, grad_rows[:pair_rows], grad_rows[pair_rows:])


def solution(mesh):
    in_specs = (
        P(("blk", "rep"), None),
        P(("blk", "rep"), None),
        P(("blk", "rep")),
        P(),
        P(None, "rep"),
        P("rep", None),
    )
    out_specs = (P(), P("rep", "blk"), P(), P(("blk", "rep"), None), P(("blk", "rep"), None))
    return jax.shard_map(
        on_device, mesh=mesh, in_specs=in_specs, out_specs=out_specs, check_vma=False
    )
```

profile of v0, /device:TPU:0, one launch (start us, length us, event | category | flops | bytes accessed | tf_op | source)
XLA Modules:
  0.0 881.1 jit_solution(6367122560149769879)
XLA Ops:
  9.0 111.3 %all-gather.5.cloned.1.call-done = bf16[1024,4096]{1,0:T(8,128)(2,1)} async-done(((bf16[1024,2048]{1,0:T(8,128)(2,1)}), bf16[1024,4096]{1,0:T(8,128)(2,1)}) %all-gather.5.cloned.1.call-update) | async-done | bytes 8388624 | tf_op jit(solution)/shard_map/all_gather | solution.py:52
  120.4 10.8 %fusion.26 = f32[512,4096]{1,0:T(8,128)} fusion(bf16[1024,4096]{1,0:T(8,128)(2,1)} %all-gather.5.cloned.1.call-done, f32[1024]{0:T(1024)S(1)} %copy-done.7, f32[512]{0:T(512)S(1)} %add_rsqrt_fusion, bf16[256,1024]{1,0:T(8,128)(2,1)S(1)} %copy-done, bf16[256,1024]{1,0:T(8,128)(2,1)S(1)} %copy-done.1), kind=kOutput, calls=%fused_computation.40 | convolution fusion | flops 4298637312 | bytes 17831936 | tf_op jit(solution)/shard_map/dot_general | solution.py:54
  131.2 98.3 %all-gather.7.cloned.1.call-done = bf16[4096,1024]{1,0:T(8,128)(2,1)} async-done(((bf16[2048,1024]{1,0:T(8,128)(2,1)}), bf16[4096,1024]{1,0:T(8,128)(2,1)}) %all-gather.7.cloned.1.call-update) | async-done | bytes 8388624 | tf_op jit(solution)/shard_map/all_gather | solution.py:53
  229.5 10.9 %fusion.23 = bf16[512,1024]{1,0:T(8,128)(2,1)S(1)} fusion(bf16[4096,1024]{1,0:T(8,128)(2,1)} %all-gather.7.cloned.1.call-done, bf16[256,1024]{1,0:T(8,128)(2,1)S(1)} %copy-done, bf16[256,1024]{1,0:T(8,128)(2,1)S(1)} %copy-done.1, f32[512,4096]{1,0:T(8,128)} %fusion.26), kind=kOutput, calls=%fused_computation.35 | convolution fusion | flops 4316987392 | bytes 18874368 | tf_op jit(solution)/shard_map/dot_general | solution.py:56
  242.4 24.8 %all-gather.9.cloned.1.call-done = bf16[512,1024]{1,0:T(8,128)(2,1)} async-done(((bf16[256,1024]{1,0:T(8,128)(2,1)}), bf16[512,1024]{1,0:T(8,128)(2,1)}) %all-gather.9.cloned.1.call-update) | async-done | bytes 1048592 | tf_op jit(solution)/shard_map/all_gather | solution.py:62
  267.8 26.1 %all-gather = s32[2,1,256]{2,1,0:T(1,128)S(1)} all-gather(s32[1,1,256]{2,1,0:T(1,128)S(1)} %bitcast.16), channel_id=1, replica_groups=mesh['blk'=64,'rep'=2] {'rep'}, dimensions={0}, use_global_device_ids=true | all-gather | bytes 3072 | tf_op jit(solution)/shard_map/all_gather | solution.py:63
  294.0 10.2 %collective-permute-start.1 = (s32[512]{0:T(512)S(1)}, s32[512]{0:T(512)S(1)}, u32[]{:S(2)}, u32[]{:S(2)}) collective-permute-start(s32[512]{0:T(512)S(1)} %bitcast.12), channel_id=1, source_target_pairs={{0,2},{2,4},{4,6},{6,8},{8,10},{10,12},{12,14},{14,16},{16,18},{18... | collective-permute-start | bytes 6152 | tf_op jit(solution)/shard_map/ppermute | solution.py:16
  304.2 5.6 collective-permute-start.6
  312.9 32.0 %collective-permute-done.2 = s32[512]{0:T(512)S(1)} collective-permute-done((s32[512]{0:T(512)S(1)}, s32[512]{0:T(512)S(1)}, u32[]{:S(2)}, u32[]{:S(2)}) %collective-permute-start.2) | collective-permute-done | bytes 2080 | tf_op jit(solution)/shard_map/ppermute | solution.py:16
  345.3 3.2 collective-permute-done.3
  351.5 1.9 fusion.24
  355.6 2.2 multiply_convert_fusion
  358.8 4.7 collective-permute-start.8
  363.4 4.8 collective-permute-start.9
  370.0 45.9 %collective-permute-done.8 = bf16[512,1024]{1,0:T(8,128)(2,1)S(1)} collective-permute-done((bf16[512,1024]{1,0:T(8,128)(2,1)S(1)}, bf16[512,1024]{1,0:T(8,128)(2,1)S(1)}, u32[]{:S(2)}, u32[]{:S(2)}) %collective-permute-start.8) | collective-permute-done | bytes 1048608 | tf_op jit(solution)/shard_map/ppermute | solution.py:16
  415.9 2.2 add_convert_fusion
  418.4 5.1 fusion.25
  423.5 31.1 %reduce-scatter.6.cloned.1.call-done = bf16[256,1024]{1,0:T(8,128)(2,1)} async-done(((bf16[512,1024]{1,0:T(8,128)(2,1)}), bf16[256,1024]{1,0:T(8,128)(2,1)}) %reduce-scatter.6.cloned.1.call-update) | async-done | bytes 524304 | tf_op jit(solution)/shard_map/reduce_scatter | solution.py:98
  454.5 10.2 %convolution_convert_fusion = bf16[4096,1024]{1,0:T(8,128)(2,1)} fusion(bf16[256,1024]{1,0:T(8,128)(2,1)} %reduce-scatter.6.cloned.1.call-done, bf16[256,1024]{1,0:T(8,128)(2,1)} %fusion.25, f32[512,4096]{1,0:T(8,128)} %fusion.26), kind=kOutput, calls=%fused_computation.11 | convolution fusion | flops 4320133120 | bytes 17825792 | tf_op jit(solution)/shard_map/dot_general | solution.py:112
  464.8 102.7 %reduce-scatter.8.cloned.1.call-done = bf16[2048,1024]{1,0:T(8,128)(2,1)} async-done(((bf16[4096,1024]{1,0:T(8,128)(2,1)}), bf16[2048,1024]{1,0:T(8,128)(2,1)}) %reduce-scatter.8.cloned.1.call-update) | async-done | bytes 4194320 | tf_op jit(solution)/shard_map/reduce_scatter | solution.py:115
  567.6 7.1 copy.13
  575.7 16.6 %fusion.17 = (f32[512]{0:T(512)S(1)}, f32[1024]{0:T(1024)S(1)}, f32[512,1024]{1,0:T(8,128)S(1)}) fusion(f32[1024]{0:T(1024)S(1)} %copy-done.7, f32[512]{0:T(512)S(1)} %add_rsqrt_fusion, bf16[256,1024]{1,0:T(8,128)(2,1)S(1)} %copy-done, bf16[256,1024]{1,0:T(8,128)(2,1)S(1)} %copy-done.2, bf16[1024,4096]{1,0:T(8,128)(2,1)} %all-gather.5.cloned.1.call-done, ...), kind=kOutput, calls=%fused_computation.29 | convolution fusion | flops 8639216640 | bytes 29372416 | tf_op jit(solution)/shard_map/dot_general | solution.py:109
  592.4 65.3 %all-reduce = (f32[]{:T(128)}, f32[1024]{0:T(1024)}) all-reduce(f32[]{:T(128)} %get-tuple-element.21, f32[1024]{0:T(1024)S(1)} %get-tuple-element.16), channel_id=1, replica_groups=mesh['blk'=64,'rep'=2] {'blk','rep'}, use_global_device_ids=true, to_apply=%region_5.6 | all-reduce | flops 1025 | bytes 8200 | tf_op jit(solution)/shard_map/psum | solution.py:123
  661.2 211.9 %reduce-scatter.10.cloned.1.call-done = f32[16,2048]{1,0:T(8,128)} async-done(((f32[1024,2048]{1,0:T(8,128)}), f32[16,2048]{1,0:T(8,128)}) %reduce-scatter.10.cloned.1.call-update) | async-done | bytes 131088
  (68 shorter events, 20.0 us)
Async XLA Ops:
  7.2 1.6 copy-start.1
  7.2 113.2 %copy-start.7 = (f32[1024]{0:T(1024)S(1)}, f32[1024]{0:T(1024)}, u32[]{:S(2)}) copy-start(f32[1024]{0:T(1024)} %param.9) | copy-start | bytes 12292
  7.2 113.2 %all-gather.5.cloned.1.call-start = ((), (), s32[]{:S(2)}) async-start(), calls=%async_computation.3 | async-start | bytes 12582912 | tf_op jit(solution)/shard_map/all_gather | solution.py:52
  7.9 221.5 %all-gather.7.cloned.1.call-start = ((), (), s32[]{:S(2)}) async-start(), calls=%async_computation.4 | async-start | bytes 12582912 | tf_op jit(solution)/shard_map/all_gather | solution.py:53
  8.7 258.5 %all-gather.9.cloned.1.call-start = ((), (), s32[]{:S(2)}) async-start(), calls=%async_computation.5 | async-start | bytes 1572864 | tf_op jit(solution)/shard_map/all_gather | solution.py:62
  131.2 136.7 %copy-start.8 = (s32[256]{0:T(256)S(1)}, s32[256]{0:T(256)}, u32[]{:S(2)}) copy-start(s32[256]{0:T(256)} %param.8) | copy-start | bytes 3076
  242.3 212.2 %reduce-scatter.6.cloned.1.call-start = ((), (), s32[]{:S(2)}) async-start(), calls=%async_computation.6 | async-start | bytes 1572864 | tf_op jit(solution)/shard_map/reduce_scatter | solution.py:98
  267.2 82.7 %copy-start.3 = (bf16[512,1024]{1,0:T(8,128)(2,1)S(1)}, bf16[512,1024]{1,0:T(8,128)(2,1)}, u32[]{:S(2)}) copy-start(bf16[512,1024]{1,0:T(8,128)(2,1)} %all-gather.9.cloned.1.call-done) | copy-start | bytes 3145732
  267.2 81.3 %collective-permute-start.4 = (bf16[512,1024]{1,0:T(8,128)(2,1)}, bf16[512,1024]{1,0:T(8,128)(2,1)}, u32[]{:S(2)}, u32[]{:S(2)}) collective-permute-start(bf16[512,1024]{1,0:T(8,128)(2,1)} %all-gather.9.cloned.1.call-done), channel_id=1, source_target_pairs={{0,4},{2,6},{4,8},{6,10},{8,12},{10,14},{12,16},{14,18},{16,20},{1... | collective-permute-start | bytes 3145736 | tf_op jit(solution)/shard_map/ppermute | solution.py:16
  267.8 81.9 %collective-permute-start.5 = (bf16[512,1024]{1,0:T(8,128)(2,1)}, bf16[512,1024]{1,0:T(8,128)(2,1)S(1)}, u32[]{:S(2)}, u32[]{:S(2)}) collective-permute-start(bf16[512,1024]{1,0:T(8,128)(2,1)} %all-gather.9.cloned.1.call-done), channel_id=1, source_target_pairs={{0,2},{2,4},{4,6},{6,8},{8,10},{10,12},{12,14},{14,16},{16,18},{18... | collective-permute-start | bytes 3145736 | tf_op jit(solution)/shard_map/ppermute | solution.py:16
  293.9 15.8 %collective-permute-start = (s32[512]{0:T(512)S(1)}, s32[512]{0:T(512)S(1)}, u32[]{:S(2)}, u32[]{:S(2)}) collective-permute-start(s32[512]{0:T(512)S(1)} %bitcast.11), channel_id=1, source_target_pairs={{0,4},{2,6},{4,8},{6,10},{8,12},{10,14},{12,16},{14,18},{16,20},{1... | collective-permute-start | bytes 6152 | tf_op jit(solution)/shard_map/ppermute | solution.py:16
  294.0 17.2 %collective-permute-start.1 = (s32[512]{0:T(512)S(1)}, s32[512]{0:T(512)S(1)}, u32[]{:S(2)}, u32[]{:S(2)}) collective-permute-start(s32[512]{0:T(512)S(1)} %bitcast.12), channel_id=1, source_target_pairs={{0,2},{2,4},{4,6},{6,8},{8,10},{10,12},{12,14},{14,16},{16,18},{18... | collective-permute-start | bytes 6152 | tf_op jit(solution)/shard_map/ppermute | solution.py:16
  304.2 45.8 %collective-permute-start.6 = (bf16[512,1024]{1,0:T(8,128)(2,1)}, bf16[512,1024]{1,0:T(8,128)(2,1)}, u32[]{:S(2)}, u32[]{:S(2)}) collective-permute-start(bf16[512,1024]{1,0:T(8,128)(2,1)} %all-gather.9.cloned.1.call-done), channel_id=1, source_target_pairs={{0,126},{2,0},{4,2},{6,4},{8,6},{10,8},{12,10},{14,12},{16,14},{18... | collective-permute-start | bytes 3145736 | tf_op jit(solution)/shard_map/ppermute | solution.py:16
  309.8 41.6 %collective-permute-start.7 = (bf16[512,1024]{1,0:T(8,128)(2,1)}, bf16[512,1024]{1,0:T(8,128)(2,1)S(1)}, u32[]{:S(2)}, u32[]{:S(2)}) collective-permute-start(bf16[512,1024]{1,0:T(8,128)(2,1)} %all-gather.9.cloned.1.call-done), channel_id=1, source_target_pairs={{0,124},{2,126},{4,0},{6,2},{8,4},{10,6},{12,8},{14,10},{16,12},{1... | collective-permute-start | bytes 3145736 | tf_op jit(solution)/shard_map/ppermute | solution.py:16
  311.1 33.7 %collective-permute-start.2 = (s32[512]{0:T(512)S(1)}, s32[512]{0:T(512)S(1)}, u32[]{:S(2)}, u32[]{:S(2)}) collective-permute-start(s32[512]{0:T(512)S(1)} %bitcast.13), channel_id=1, source_target_pairs={{0,126},{2,0},{4,2},{6,4},{8,6},{10,8},{12,10},{14,12},{16,14},{18... | collective-permute-start | bytes 6152 | tf_op jit(solution)/shard_map/ppermute | solution.py:16
  344.9 3.6 collective-permute-start.3
  349.7 1.7 copy-start.5
  351.4 2.4 copy-start.6
  358.8 57.1 %collective-permute-start.8 = (bf16[512,1024]{1,0:T(8,128)(2,1)S(1)}, bf16[512,1024]{1,0:T(8,128)(2,1)S(1)}, u32[]{:S(2)}, u32[]{:S(2)}) collective-permute-start(bf16[512,1024]{1,0:T(8,128)(2,1)S(1)} %get-tuple-element.23), channel_id=1, source_target_pairs={{0,124},{2,126},{4,0},{6,2},{8,4},{10,6},{12,8},{14,10},{16,12},{1... | collective-permute-start | bytes 3145736 | tf_op jit(solution)/shard_map/ppermute | solution.py:16
  363.4 52.5 %collective-permute-start.9 = (bf16[512,1024]{1,0:T(8,128)(2,1)S(1)}, bf16[512,1024]{1,0:T(8,128)(2,1)S(1)}, u32[]{:S(2)}, u32[]{:S(2)}) collective-permute-start(bf16[512,1024]{1,0:T(8,128)(2,1)S(1)} %get-tuple-element.27), channel_id=1, source_target_pairs={{0,126},{2,0},{4,2},{6,4},{8,6},{10,8},{12,10},{14,12},{16,14},{18... | collective-permute-start | bytes 3145736 | tf_op jit(solution)/shard_map/ppermute | solution.py:16
  368.3 47.6 %collective-permute-start.10 = (bf16[512,1024]{1,0:T(8,128)(2,1)S(1)}, bf16[512,1024]{1,0:T(8,128)(2,1)S(1)}, u32[]{:S(2)}, u32[]{:S(2)}) collective-permute-start(bf16[512,1024]{1,0:T(8,128)(2,1)S(1)} %get-tuple-element.25), channel_id=1, source_target_pairs={{0,2},{2,4},{4,6},{6,8},{8,10},{10,12},{12,14},{14,16},{16,18},{18... | collective-permute-start | bytes 3145736 | tf_op jit(solution)/shard_map/ppermute | solution.py:16
  368.3 47.6 %collective-permute-start.11 = (bf16[512,1024]{1,0:T(8,128)(2,1)S(1)}, bf16[512,1024]{1,0:T(8,128)(2,1)S(1)}, u32[]{:S(2)}, u32[]{:S(2)}) collective-permute-start(bf16[512,1024]{1,0:T(8,128)(2,1)S(1)} %get-tuple-element.24), channel_id=1, source_target_pairs={{0,4},{2,6},{4,8},{6,10},{8,12},{10,14},{12,16},{14,18},{16,20},{1... | collective-permute-start | bytes 3145736 | tf_op jit(solution)/shard_map/ppermute | solution.py:16
  418.1 149.4 %reduce-scatter.8.cloned.1.call-start = ((), (), s32[]{:S(2)}) async-start(), calls=%async_computation.7 | async-start | bytes 12582912 | tf_op jit(solution)/shard_map/reduce_scatter | solution.py:115
  464.8 408.3 %reduce-scatter.10.cloned.1.call-start = ((), (), s32[]{:S(2)}) async-start(), calls=%async_computation.8 | async-start | bytes 8519680
  (3 other events, 3.7 us)
Sparse Core Ops, SparseCore 0:
  9.7 110.6 all-gather.4
  122.0 107.3 all-gather.6
  242.4 24.6 all-gather.8
  418.2 36.2 reduce-scatter.5
  464.9 102.6 reduce-scatter.7
  574.8 298.2 reduce-scatter.9
where the time goes:
time: 882 us; the launch traced here: 881 us
  waiting for transfers between devices  664 us (75%)
  blocking collectives  91.4 us (10%)
  matrix products  57.8 us (7%)
  starting transfers between devices  30.8 us (3%)
  between operations  16.1 us (2%)
  local copies, waits for them, and re-layouts  15.4 us (2%)
    unnamed x7, waiting for transfers between devices  213 us
    all_gather x1, waiting for transfers between devices, on_device(): inner_full = lax.all_gather(w_in, 'rep', axis=1, tiled=True)  111 us
    reduce_scatter x1, waiting for transfers between devices, on_device(): lax.psum_scatter(down_term.astype(jnp.bfloat16), 'rep', scatter_dimension...  103 us
    all_gather x1, waiting for transfers between devices, on_device(): outer_full = lax.all_gather(w_out, 'rep', axis=0, tiled=True)  98.3 us
    ppermute x12, waiting for transfers between devices, from_behind(): lax.ppermute(x, axis, [(i, (i + by) % devices) for i in range(devices)])  82 us
    psum x1, blocking collectives, on_device(): loss_total, gain_total = lax.psum((loss_part, gain_term), ('blk', 'rep'))  65.3 us
    reduce_scatter x1, waiting for transfers between devices, on_device(): lax.psum_scatter(summed.astype(jnp.bfloat16), 'rep', scatter_dimension=0,...  31.1 us
    ppermute x12, starting transfers between devices, from_behind(): lax.ppermute(x, axis, [(i, (i + by) % devices) for i in range(devices)])  30.3 us
  transfers between devices with their start and end apart: 18, of which 10 were waited for; matrix products, arithmetic and copies ran while one was open for 4% of the time, Pallas kernels for 0%

commit v1 on v0

v1 whole, which is shorter than its diff:
```python
import math

import jax
import jax.numpy as jnp
from jax import lax
from jax.experimental import pallas as pl
from jax.experimental.pallas import tpu as pltpu
from jax.sharding import PartitionSpec as P

MESH = pl.DeviceIdType.MESH
MIB = 2**20
NX, NY, NZ, NC = 4, 4, 2, 2
NBLK = NX * NY * NZ * NC
RING = NX
EPSILON = 1e-06
SLOTS = 10
OWN = 4


def coords():
    b = lax.axis_index("blk")
    r = lax.axis_index("rep")
    return b // (NY * NZ * NC), (b // (NZ * NC)) % NY, (b // NC) % NZ, b % NC, r


def device(x, y, zl, c, r):
    return {"blk": ((x * NY + y) * NZ + zl) * NC + c, "rep": r}


def wrap(v, n):
    return lax.rem(v + n, n)


def greet(peers):
    barrier = pltpu.get_barrier_semaphore()
    for peer in peers:
        pl.semaphore_signal(barrier, inc=1, device_id=peer, device_id_type=MESH)
    pl.semaphore_wait(barrier, len(peers))


def remote(src, dst, send, recv, peer):
    return pltpu.make_async_remote_copy(
        src_ref=src,
        dst_ref=dst,
        send_sem=send,
        recv_sem=recv,
        device_id=peer,
        device_id_type=MESH,
    )


WBLK = 256
W_CHUNKS = 8


def weight_view(in_ref, out_ref, block, chunk):
    if chunk < W_CHUNKS // 2:
        rows = in_ref.shape[0] // (W_CHUNKS // 2)
        return in_ref.at[
            pl.ds(chunk * rows, rows), pl.ds(pl.multiple_of(block * WBLK, WBLK), WBLK)
        ]
    rows = WBLK // (W_CHUNKS // 2)
    first = block * WBLK + (chunk - W_CHUNKS // 2) * rows
    return out_ref.at[pl.ds(pl.multiple_of(first, rows), rows)]


def weights_kernel(win, wout, oin, oout, send, recv):
    x, y, zl, c, r = coords()
    cross = device(x, y, 1 - zl, c, 1 - r)
    near = device(x, y, 1 - zl, c, r)
    ahead = device(wrap(x + 1, NX), y, zl, c, r)
    behind = device(wrap(x - 1, NX), y, zl, c, r)
    sibling = device(x, y, zl, 1 - c, r)
    greet([cross, near, ahead, behind, sibling])
    color = lax.rem(x + 2 * zl, 4)

    def block_of(shift):
        return 2 * lax.rem(color + shift, 4) + c

    def copy(flow, block, chunk, peer, source=None):
        src = weight_view(*(source or (oin, oout)), block, chunk)
        dst = weight_view(oin, oout, block, chunk)
        return remote(src, dst, send.at[flow, chunk], recv.at[flow, chunk], peer)

    started = []

    def start(*args):
        op = copy(*args)
        op.start()
        started.append(op)

    for chunk in range(W_CHUNKS):
        start(0, block_of(2), chunk, cross, (win, wout))
    mine = block_of(0)
    for chunk in range(W_CHUNKS):
        copy(0, mine, chunk, cross).wait_recv()
        start(1, mine, chunk, ahead)
        start(2, mine, chunk, behind)
        start(3, mine, chunk, near)
        start(4, mine, chunk, sibling)
        if chunk:
            pass_on(copy, start, block_of, chunk - 1, (behind, ahead, near), sibling)
    pass_on(copy, start, block_of, W_CHUNKS - 1, (behind, ahead, near), sibling)
    for chunk in range(W_CHUNKS):
        for k in range(4):
            other = 2 * lax.rem(color + k, 4) + (1 - c)
            copy(4 + k, other, chunk, sibling).wait_recv()
    for op in started:
        op.wait_send()


def pass_on(copy, start, block_of, chunk, peers, sibling):
    for flow, shift, k in ((1, 3, 3), (2, 1, 1), (3, 2, 2)):
        block = block_of(shift)
        copy(flow, block, chunk, peers[flow - 1]).wait_recv()
        start(4 + k, block, chunk, sibling)


def gather_weights(w_in, w_out):
    return pl.pallas_call(
        weights_kernel,
        out_shape=(
            jax.ShapeDtypeStruct(w_in.shape, w_in.dtype),
            jax.ShapeDtypeStruct(w_out.shape, w_out.dtype),
        ),
        in_specs=[pl.BlockSpec(memory_space=pl.ANY)] * 2,
        out_specs=[pl.BlockSpec(memory_space=pl.ANY)] * 2,
        scratch_shapes=[pltpu.SemaphoreType.DMA((8, W_CHUNKS))] * 2,
        compiler_params=pltpu.CompilerParams(collective_id=0, has_side_effects=True),
        name="gather_weights",
    )(w_in, w_out)


B_CHUNKS = 5


def band_kernel(docs, tags, queries, gd, gx, gq, send, recv, local):
    x, y, zl, c, r = coords()
    b = lax.axis_index("blk")
    cross = device(x, y, 1 - zl, c, 1 - r)
    near = device(x, y, 1 - zl, c, r)
    sibling = device(x, y, zl, 1 - c, r)
    step = NZ * NC * (1 - 2 * zl)
    onward = {"blk": wrap(b + step, NBLK), "rep": r}
    source = {"blk": wrap(b - step, NBLK), "rep": r}
    greet([cross, near, sibling, onward, source])

    rows = docs.shape[0]
    half = rows // 2
    tag_rows = tags.shape[0]

    def view(slot, chunk):
        if chunk == 2:
            return gx.at[pl.ds(pl.multiple_of(slot * tag_rows, tag_rows), tag_rows)]
        ref = gd if chunk < 2 else gq
        first = slot * rows + (chunk % 3) * half
        return ref.at[pl.ds(pl.multiple_of(first, half), half)]

    def own(chunk):
        if chunk == 2:
            return tags
        ref = docs if chunk < 2 else queries
        return ref.at[pl.ds((chunk % 3) * half, half)]

    z_slot = 8 - 8 * zl
    far_slot = 8 * zl
    started = []

    def make(flow, chunk, src, dst_slot, peer):
        return remote(
            src, view(dst_slot, chunk), send.at[flow, chunk], recv.at[flow, chunk], peer
        )

    def start(*args):
        op = make(*args)
        op.start()
        started.append(op)

    def arrived(flow, chunk, slot):
        make(flow, chunk, view(slot, chunk), slot, near).wait_recv()

    def band_to_sibling(chunk):
        return [
            make(7 + k, chunk, view(8 - 8 * c + k, chunk), 6 - 4 * c + k, sibling)
            for k in range(2)
        ]

    order = (0, 1, 2, 3, 4)
    theirs = 8 * zl
    keep = []
    for chunk in order:
        start(0, chunk, own(chunk), theirs, near)
        start(1, chunk, own(chunk), theirs + 1, cross)
        start(5, chunk, own(chunk), 2 + 4 * c, sibling)
        op = pltpu.make_async_copy(own(chunk), view(OWN, chunk), local.at[chunk])
        op.start()
        keep.append(op)
    for place, chunk in enumerate(order):
        arrived(0, chunk, z_slot)
        start(3, chunk, view(z_slot, chunk), far_slot, onward)
        if place % 2 == 0:
            start(2, chunk, view(z_slot, chunk), OWN + 1, cross)
        arrived(1, chunk, z_slot + 1)
        start(4, chunk, view(z_slot + 1, chunk), far_slot + 1, onward)
        if place % 2 == 1:
            start(2, chunk, view(z_slot + 1, chunk), OWN + 1, near)

        @pl.when(c == zl)
        def _():
            for op in band_to_sibling(chunk):
                op.start()

    for chunk in order:
        arrived(2, chunk, OWN + 1)
        start(6, chunk, view(OWN + 1, chunk), 3 + 4 * c, sibling)
        arrived(3, chunk, far_slot)
        arrived(4, chunk, far_slot + 1)

        @pl.when(c != zl)
        def _():
            for op in band_to_sibling(chunk):
                op.start()

    for chunk in order:
        arrived(5, chunk, 6 - 4 * c)
        arrived(6, chunk, 7 - 4 * c)
        for op in band_to_sibling(chunk):
            op.wait_send()
        arrived(7, chunk, 2 + 4 * c)
        arrived(8, chunk, 3 + 4 * c)
        keep[chunk].wait()
    for op in started:
        op.wait_send()


def gather_band(docs, tags, queries):
    return pl.pallas_call(
        band_kernel,
        out_shape=[
            jax.ShapeDtypeStruct((SLOTS * v.shape[0], v.shape[1]), v.dtype)
            for v in (docs, tags, queries)
        ],
        in_specs=[pl.BlockSpec(memory_space=pl.ANY)] * 3,
        out_specs=[pl.BlockSpec(memory_space=pl.ANY)] * 3,
        scratch_shapes=[
            pltpu.SemaphoreType.DMA((9, B_CHUNKS)),
            pltpu.SemaphoreType.DMA((9, B_CHUNKS)),
            pltpu.SemaphoreType.DMA((B_CHUNKS,)),
        ],
        compiler_params=pltpu.CompilerParams(collective_id=1, has_side_effects=True),
        name="gather_band",
    )(docs, tags, queries)


def totals_kernel(mine, out, send, recv):
    b = lax.axis_index("blk")
    r = lax.axis_index("rep")
    peers = []
    for offset in range(-2, 3):
        for other in range(2):
            if offset or other:
                rep = 1 - r if other else r
                peers.append((offset, other, {"blk": wrap(b + offset, NBLK), "rep": rep}))
    greet([peer for _, _, peer in peers])
    ops = []
    for i, (offset, other, peer) in enumerate(peers):
        slot = (2 - offset) * 2 + other
        op = remote(mine, out.at[slot], send.at[i], recv.at[slot], peer)
        op.start()
        ops.append(op)
    out[OWN] = mine[...]
    for slot in range(SLOTS):
        if slot != OWN:
            remote(mine, out.at[slot], send.at[0], recv.at[slot], peers[0][2]).wait_recv()
    for op in ops:
        op.wait_send()


def exchange_totals(log_total):
    rows = log_total.shape[0]
    tile = jnp.pad(log_total.reshape(rows // 128, 128), ((0, 8 - rows // 128), (0, 0)))
    out = pl.pallas_call(
        totals_kernel,
        out_shape=jax.ShapeDtypeStruct((SLOTS, 8, 128), jnp.float32),
        in_specs=[pl.BlockSpec(memory_space=pltpu.VMEM)],
        out_specs=pl.BlockSpec(memory_space=pltpu.VMEM),
        scratch_shapes=[
            pltpu.SemaphoreType.DMA((SLOTS,)),
            pltpu.SemaphoreType.DMA((SLOTS,)),
        ],
        compiler_params=pltpu.CompilerParams(collective_id=2, has_side_effects=True),
        name="exchange_totals",
    )(tile)
    return out[:, : rows // 128].reshape(SLOTS * rows)


GROUP = 16


def reduce_kernel(own, oth, small, out, total, r1, a1, r2, a2, r3, a3, r4, s_buf, sems):
    x, y, zl, c, r = coords()
    hid = own.shape[-1]
    mid = hid // 2
    sibling = device(x, y, zl, 1 - c, r)
    xs = [device(wrap(x + k, NX), y, zl, c, r) for k in range(1, RING)]
    ys = [device(x, wrap(y + k, NY), zl, c, r) for k in range(1, RING)]
    zs = [device(x, y, 1 - zl, c, r), device(x, y, zl, c, 1 - r), device(x, y, 1 - zl, c, 1 - r)]
    greet([sibling] + xs + ys + zs)
    state = {"n": 0}
    ops = []

    def send(src, dst, peer):
        n = state["n"]
        state["n"] = n + 1
        op = remote(src, dst, sems.at[0, n], sems.at[1, n], peer)
        op.start()
        ops.append(op)
        return op

    s_buf[12] = small[...]

    wait1 = [
        send(own.at[:, 1 - c], r1.at[0], sibling),
        send(oth.at[:, 1 - c], r1.at[1], sibling),
        send(s_buf.at[12], s_buf.at[13], sibling),
    ]
    for op in wait1:
        op.wait_recv()
    s_buf[x] = s_buf[12] + s_buf[13]
    for h, ref in enumerate((own, oth)):

        def add1(g, _):
            a1[h, g] = (
                ref[g, c].astype(jnp.float32) + r1[h, g].astype(jnp.float32)
            ).astype(jnp.bfloat16)
            return 0

        lax.fori_loop(0, NX * NY * NZ, add1, 0)

    wait2 = []
    for k in range(1, RING):
        slot = RING - 1 - k
        tx = wrap(x + k, NX)
        ty = wrap(y + k, NY)
        for h in range(2):
            wait2.append(
                send(
                    a1.at[h, pl.ds(tx * NY * NZ, NY * NZ), :, pl.ds(0, mid)],
                    r2.at[0, slot, h],
                    xs[k - 1],
                )
            )
            for xx in range(NX):
                wait2.append(
                    send(
                        a1.at[h, pl.ds((xx * NY + ty) * NZ, NZ), :, pl.ds(mid, mid)],
                        r2.at[1, slot, h, pl.ds(xx * NZ, NZ)],
                        ys[k - 1],
                    )
                )
        wait2.append(send(s_buf.at[x], s_buf.at[x], xs[k - 1]))
    for op in wait2:
        op.wait_recv()
    s_buf[4 + y] = ((s_buf[0] + s_buf[1]) + s_buf[2]) + s_buf[3]
    for h in range(2):

        def add2(g, _):
            first = a1[h, x * NY * NZ + g, :, pl.ds(0, mid)].astype(jnp.float32)
            second = a1[h, (g // NZ * NY + y) * NZ + g % NZ, :, pl.ds(mid, mid)].astype(
                jnp.float32
            )
            for k in range(RING - 1):
                first += r2[0, k, h, g].astype(jnp.float32)
                second += r2[1, k, h, g].astype(jnp.float32)
            a2[0, h, g] = first.astype(jnp.bfloat16)
            a2[1, h, g] = second.astype(jnp.bfloat16)
            return 0

        lax.fori_loop(0, NY * NZ, add2, 0)

    wait3 = []
    for k in range(1, RING):
        slot = RING - 1 - k
        tx = wrap(x + k, NX)
        ty = wrap(y + k, NY)
        wait3.append(send(a2.at[0, :, pl.ds(ty * NZ, NZ)], r3.at[0, slot], ys[k - 1]))
        wait3.append(send(a2.at[1, :, pl.ds(tx * NZ, NZ)], r3.at[1, slot], xs[k - 1]))
        wait3.append(send(s_buf.at[4 + y], s_buf.at[4 + y], ys[k - 1]))
    for op in wait3:
        op.wait_recv()
    s_buf[8 + 2 * r + zl] = ((s_buf[4] + s_buf[5]) + s_buf[6]) + s_buf[7]
    for part in range(2):
        at = (y, x)[part]
        for h in range(2):
            for z in range(NZ):
                tot = a2[part, h, at * NZ + z].astype(jnp.float32)
                for k in range(RING - 1):
                    tot += r3[part, k, h, z].astype(jnp.float32)
                a3[h, z, :, part * mid : (part + 1) * mid] = tot.astype(jnp.bfloat16)

    mine = s_buf.at[8 + 2 * r + zl]
    wait4 = [
        send(a3.at[0, 1 - zl], r4.at[0], zs[0]),
        send(a3.at[1, zl], r4.at[1], zs[1]),
        send(a3.at[1, 1 - zl], r4.at[2], zs[2]),
    ] + [send(mine, mine, peer) for peer in zs]
    for op in wait4:
        op.wait_recv()
    out[...] = (
        (a3[0, zl].astype(jnp.float32) + r4[0].astype(jnp.float32))
        + (r4[1].astype(jnp.float32) + r4[2].astype(jnp.float32))
    )
    total[...] = (s_buf[8] + s_buf[9]) + (s_buf[10] + s_buf[11])
    for op in ops:
        op.wait_send()


def reduce_all(own, oth, small):
    hid = own.shape[1]
    groups = NX * NY * NZ
    shape = (groups, NC, GROUP, hid)
    n_copies = 3 + 3 * (2 + 2 * NX + 1) + 9 + 6
    bf = jnp.bfloat16
    return pl.pallas_call(
        reduce_kernel,
        out_shape=(
            jax.ShapeDtypeStruct((GROUP, hid), jnp.float32),
            jax.ShapeDtypeStruct(small.shape, jnp.float32),
        ),
        in_specs=[pl.BlockSpec(memory_space=pltpu.VMEM)] * 3,
        out_specs=[pl.BlockSpec(memory_space=pltpu.VMEM)] * 2,
        scratch_shapes=[
            pltpu.VMEM((2, groups, GROUP, hid), bf),
            pltpu.VMEM((2, groups, GROUP, hid), bf),
            pltpu.VMEM((2, RING - 1, 2, NY * NZ, GROUP, hid // 2), bf),
            pltpu.VMEM((2, 2, NY * NZ, GROUP, hid // 2), bf),
            pltpu.VMEM((2, RING - 1, 2, NZ, GROUP, hid // 2), bf),
            pltpu.VMEM((2, NZ, GROUP, hid), bf),
            pltpu.VMEM((3, GROUP, hid), bf),
            pltpu.VMEM((14,) + small.shape, jnp.float32),
            pltpu.SemaphoreType.DMA((2, n_copies)),
        ],
        compiler_params=pltpu.CompilerParams(
            collective_id=3, has_side_effects=True, vmem_limit_bytes=56 * MIB
        ),
        name="reduce_all",
    )(own.reshape(shape), oth.reshape(shape), small)


def dot(a, b, dims):
    return lax.dot_general(a, b, (dims, ((), ())), preferred_element_type=jnp.float32)


def gelu_and_slope(p):
    hidden, back = jax.vjp(lambda v: jax.nn.gelu(v, approximate=True), p)
    return hidden, back


def on_device(query_in, doc_in, cluster, gain, w_in, w_out):
    rows, width = query_in.shape
    inv_root = 1.0 / math.sqrt(width)
    o_in, o_out = gather_weights(w_in, w_out)

    rows_in = jnp.concatenate([query_in, doc_in], axis=0)
    values = rows_in.astype(jnp.float32)
    inv_rms = lax.rsqrt(jnp.mean(values * values, axis=-1, keepdims=True) + EPSILON)
    unit_rows = values * inv_rms
    normed = (unit_rows * gain).astype(jnp.bfloat16)
    pre = [jnp.dot(normed, w, preferred_element_type=jnp.float32) for w in (w_in, o_in)]
    hidden = [jax.nn.gelu(p, approximate=True).astype(jnp.bfloat16) for p in pre]
    mixed = jnp.dot(hidden[0], w_out, preferred_element_type=jnp.float32) + jnp.dot(
        hidden[1], o_out, preferred_element_type=jnp.float32
    )
    embedded = (values + mixed).astype(jnp.bfloat16)
    queries, docs = embedded[:rows], embedded[rows:]

    tags = jnp.broadcast_to(cluster.astype(jnp.bfloat16)[None, :], (16, rows))
    band_docs, band_tags, band_queries = gather_band(docs, tags, queries)
    band_cluster = band_tags.reshape(SLOTS, 16, rows)[:, 0].astype(jnp.int32).reshape(-1)

    columns = jnp.arange(SLOTS * rows, dtype=jnp.int32)[None, :]
    is_positive = columns == (OWN * rows + jnp.arange(rows, dtype=jnp.int32))[:, None]
    allowed = (band_cluster[None, :] != cluster[:, None]) | is_positive
    positive_value = is_positive.astype(jnp.float32)

    scores = dot(queries, band_docs, ((1,), (1,))) * inv_root
    masked = jnp.where(allowed, scores, -jnp.inf)
    row_max = jnp.max(masked, axis=1, keepdims=True)
    log_total = row_max + jnp.log(jnp.sum(jnp.exp(masked - row_max), axis=1, keepdims=True))
    positive_score = jnp.sum(jnp.where(is_positive, scores, 0.0), axis=1)
    loss_part = jnp.sum(log_total[:, 0] - positive_score)
    weights = (jnp.exp(masked - log_total) - positive_value).astype(jnp.bfloat16)

    band_totals = exchange_totals(log_total[:, 0])
    back_scores = dot(docs, band_queries, ((1,), (1,))) * inv_root
    back_masked = jnp.where(allowed, back_scores, -jnp.inf)
    back_weights = (jnp.exp(back_masked - band_totals[None, :]) - positive_value).astype(
        jnp.bfloat16
    )
    query_grad = (dot(weights, band_docs, ((1,), (0,))) * inv_root).astype(jnp.bfloat16)
    doc_grad = (dot(back_weights, band_queries, ((1,), (0,))) * inv_root).astype(jnp.bfloat16)
    upstream = jnp.concatenate([query_grad, doc_grad], axis=0)

    g_norm = jnp.zeros((2 * rows, width), jnp.float32)
    downs = []
    for p, h, up, down in zip(pre, hidden, (w_in, o_in), (w_out, o_out)):
        g_act = dot(upstream, down, ((1,), (1,)))
        g_pre = jax.vjp(lambda v: jax.nn.gelu(v, approximate=True), p)[1](g_act)[0]
        g_norm = g_norm + dot(g_pre.astype(jnp.bfloat16), up, ((1,), (1,)))
        downs.append(dot(upstream, h, ((0,), (0,))).astype(jnp.bfloat16))
    gain_term = jnp.sum(g_norm * unit_rows, axis=0)
    d_unit = g_norm * gain
    d_values = inv_rms * (d_unit - unit_rows * jnp.mean(d_unit * unit_rows, axis=-1, keepdims=True))
    grad_rows = (upstream.astype(jnp.float32) + d_values).astype(jnp.bfloat16)

    small = jnp.concatenate(
        [gain_term.reshape(width // 128, 128), jnp.broadcast_to(loss_part, (8, 128))], axis=0
    )
    down_t, total = reduce_all(downs[0], downs[1], small)
    loss = total[width // 128, 0] / (rows * 2 * NBLK)
    gain_total = total[: width // 128].reshape(width)
    return (loss, down_t.T, gain_total, grad_rows[:rows], grad_rows[rows:])


def solution(mesh):
    in_specs = (
        P(("blk", "rep"), None),
        P(("blk", "rep"), None),
        P(("blk", "rep")),
        P(),
        P(None, "rep"),
        P("rep", None),
    )
    out_specs = (P(), P("rep", "blk"), P(), P(("blk", "rep"), None), P(("blk", "rep"), None))
    return jax.shard_map(
        on_device, mesh=mesh, in_specs=in_specs, out_specs=out_specs, check_vma=False
    )
```

time: 882 us -> 256 us (0.29)
  waiting for transfers between devices: 664 us -> 0 us
  Pallas kernels: 0 us -> 168 us
  blocking collectives: 91.4 us -> 0 us
  starting transfers between devices: 30.8 us -> 0 us
  between operations: 16.1 us -> 2.65 us
  matrix products: 57.8 us -> 67.5 us
    all_gather x3 -> x0, waiting for transfers between devices: 234 us -> none  [the longest x1 111 us: on_device(): inner_full = lax.all_gather(w_in, 'rep', axis=1, tiled=True)]
    unnamed x7 -> x0, waiting for transfers between devices: 213 us -> none
    pallas_call x0 -> x4, Pallas kernels: none -> 168 us  [the longest x1 60.8 us: gather_band(): pl.pallas_call(band_kernel, out_shape=[jax.ShapeDtypeStruct((SLOTS * v.sh...]
    reduce_scatter x2 -> x0, waiting for transfers between devices: 134 us -> none  [the longest x1 103 us: on_device(): lax.psum_scatter(down_term.astype(jnp.bfloat16), 'rep', scatter_dimension...]
    ppermute x12 -> x0, waiting for transfers between devices: 82 us -> none  [from_behind(): lax.ppermute(x, axis, [(i, (i + by) % devices) for i in range(devices)])]
    psum x1 -> x0, blocking collectives: 65.3 us -> none  [on_device(): loss_total, gain_total = lax.psum((loss_part, gain_term), ('blk', 'rep'))]
    ppermute x12 -> x0, starting transfers between devices: 30.3 us -> none  [from_behind(): lax.ppermute(x, axis, [(i, (i + by) % devices) for i in range(devices)])]
    all_gather x1 -> x0, blocking collectives: 26.1 us -> none  [on_device(): lax.all_gather(cluster, 'rep', axis=0, tiled=True)]
  transfers between devices with their start and end apart: 18 -> 0, of which waited for: 10 -> 0; matrix products, arithmetic and copies ran while one was open for 4% -> 0% of each run, Pallas kernels for 0% -> 0%
where the time goes in v1:
time: 256 us
  Pallas kernels  168 us (66%)
  matrix products  67.5 us (26%)
  local copies, waits for them, and re-layouts  11.5 us (4%)
  other arithmetic  5.65 us (2%)
  between operations  2.65 us (1%)
    pallas_call x1, Pallas kernels, gather_band(): pl.pallas_call(band_kernel, out_shape=[jax.ShapeDtypeStruct((SLOTS * v.sh...  60.8 us
    pallas_call x1, Pallas kernels, reduce_all(): pl.pallas_call(reduce_kernel, out_shape=(jax.ShapeDtypeStruct((GROUP, hid...  56 us
    dot_general x7, matrix products, dot(): lax.dot_general(a, b, (dims, ((), ())), preferred_element_type=jnp.float32)  50.9 us
    pallas_call x1, Pallas kernels, gather_weights(): pl.pallas_call(weights_kernel, out_shape=(jax.ShapeDtypeStruct(w_in.shape...  39.6 us
    pallas_call x1, Pallas kernels, exchange_totals(): pl.pallas_call(totals_kernel, out_shape=jax.ShapeDtypeStruct((SLOTS, 8, 1...  12.1 us
    dot_general x2, matrix products, on_device(): jnp.dot(normed, w, preferred_element_type=jnp.float32)  9.84 us

profile of v1, /device:TPU:0, one launch (start us, length us, event | category | flops | bytes accessed | tf_op | source)
XLA Modules:
  0.0 255.7 jit_solution(4230594096517538262)
XLA Ops:
  1.3 1.5 fusion.32
  3.4 5.1 %fusion.55 = f32[512,2048]{1,0:T(8,128)S(1)} fusion(bf16[1024,2048]{1,0:T(8,128)(2,1)} %win.1, f32[1024]{0:T(1024)} %param.9, f32[512]{0:T(512)S(1)} %add_rsqrt_fusion, bf16[256,1024]{1,0:T(8,128)(2,1)} %param.7, bf16[256,1024]{1,0:T(8,128)(2,1)} %param.6), kind=kOutput, calls=%fused_computation.68 | convolution fusion | flops 2151153664 | bytes 9443328 | tf_op jit(solution)/shard_map/dot_general | solution.py:469
  8.5 2.1 copy-done.11
  10.6 4.0 %fusion.78 = f32[512,1024]{1,0:T(8,128)} fusion(bf16[2048,1024]{1,0:T(8,128)(2,1)S(1)} %copy-done, f32[512,2048]{1,0:T(8,128)S(1)} %fusion.55), kind=kOutput, calls=%fused_computation.96 | convolution fusion | flops 2156920832 | bytes 10485760 | tf_op jit(solution)/shard_map/dot_general | solution.py:471
  14.6 39.6 %gather_weights.1 = (bf16[1024,2048]{1,0:T(8,128)(2,1)}, bf16[2048,1024]{1,0:T(8,128)(2,1)}) custom-call(bf16[1024,2048]{1,0:T(8,128)(2,1)} %win.1, bf16[2048,1024]{1,0:T(8,128)(2,1)} %wout.1), custom_call_target="tpu_custom_call" | custom-call | tf_op jit(solution)/shard_map/gather_weights/pallas_call | solution.py:120
  54.3 4.8 %fusion.53 = f32[512,2048]{1,0:T(8,128)S(1)} fusion(bf16[1024,2048]{1,0:T(8,128)(2,1)} %get-tuple-element.12, f32[1024]{0:T(1024)S(1)} %copy-done.7, f32[512]{0:T(512)S(1)} %add_rsqrt_fusion, bf16[256,1024]{1,0:T(8,128)(2,1)S(1)} %copy-done.1, bf16[256,1024]{1,0:T(8,128)(2,1)S(1)} %copy-done.2), kind=kOutput, calls=%fused_computation.67 | convolution fusion | flops 2151153664 | bytes 9443328 | tf_op jit(solution)/shard_map/dot_general | solution.py:469
  59.1 2.7 %fusion.33 = bf16[512,1024]{1,0:T(8,128)(2,1)S(1)} fusion(f32[512,1024]{1,0:T(8,128)S(1)} %copy-done.13, bf16[2048,1024]{1,0:T(8,128)(2,1)S(1)} %copy-done.10, bf16[256,1024]{1,0:T(8,128)(2,1)S(1)} %copy-done.1, bf16[256,1024]{1,0:T(8,128)(2,1)S(1)} %copy-done.2, f32[512,2048]{1,0:T(8,128)S(1)} %fusion.53), kind=kOutput, calls=%fused_computation.50 | convolution fusion | flops 2160590848 | bytes 12582912 | tf_op jit(solution)/shard_map/dot_general | solution.py:471
  61.8 1.0 fusion.80
  62.8 60.8 %gather_band.1 = (bf16[2560,1024]{1,0:T(8,128)(2,1)}, bf16[160,256]{1,0:T(8,128)(2,1)}, bf16[2560,1024]{1,0:T(8,128)(2,1)}) custom-call(bf16[256,1024]{1,0:T(8,128)(2,1)} %get-tuple-element.28.docs, bf16[16,256]{1,0:T(8,128)(2,1)} %broadcast_in_dim.9.tags, bf16[256,1024]{1,0:T(8,128)(2,1)} %get-tuple-element.27.queries), custom_call_target="tpu_custom_call" | custom-call | tf_op jit(solution)/shard_map/gather_band/pallas_call | solution.py:237
  124.5 4.5 %fusion.42 = (f32[256]{0:T(256)S(1)}, f32[256,2560]{1,0:T(8,128)S(1)}) fusion(s32[256]{0:T(256)S(1)} %iota_add_fusion, s32[2560]{0:T(1024)S(1)} %reshape.72, s32[256]{0:T(256)S(1)} %copy-done.8, bf16[2560,1024]{1,0:T(8,128)(2,1)} %get-tuple-element.15, bf16[512,1024]{1,0:T(8,128)(2,1)S(1)} %fusion.33), kind=kOutput, calls=%fused_computation.55 | convolution fusion | flops 1346109184 | bytes 8403968 | tf_op jit(solution)/shard_map/dot_general | solution.py:451
  129.0 1.4 select_reduce_fusion
  131.0 1.9 fusion.49
  133.6 12.1 %exchange_totals.1 = f32[10,8,128]{2,1,0:T(8,128)} custom-call(f32[8,128]{1,0:T(8,128)} %pad.5.mine), custom_call_target="tpu_custom_call" | custom-call | tf_op jit(solution)/shard_map/exchange_totals/pallas_call | solution.py:282
  146.5 7.2 %fusion.52 = bf16[256,1024]{1,0:T(8,128)(2,1)S(1)} fusion(bf16[2560,1024]{1,0:T(8,128)(2,1)} %get-tuple-element.16, f32[2560]{0:T(1024)S(1)} %sub.49, s32[256]{0:T(256)S(1)} %iota_add_fusion, s32[2560]{0:T(1024)S(1)} %reshape.72, s32[256]{0:T(256)S(1)} %copy-done.8, bf16[512,1024]{1,0:T(8,128)(2,1)S(1)} %fusion.33), kind=kOutput, calls=%fused_computation.64 | convolution fusion | flops 2690777088 | bytes 11560960 | tf_op jit(solution)/shard_map/dot_general | solution.py:451
  153.7 11.8 %fusion.34 = f32[512,1024]{1,0:T(8,128)} fusion(bf16[1024,2048]{1,0:T(8,128)(2,1)} %get-tuple-element.12, f32[512,2048]{1,0:T(8,128)} %copy-done.12, bf16[2048,1024]{1,0:T(8,128)(2,1)} %get-tuple-element.13, bf16[256,1024]{1,0:T(8,128)(2,1)S(1)} %fusion.52, bf16[256,1024]{1,0:T(8,128)(2,1)S(1)} %fusion.49), kind=kOutput, calls=%fused_computation.51 | convolution fusion | flops 4318035968 | bytes 15728640 | tf_op jit(solution)/shard_map/dot_general | solution.py:451
  165.5 6.9 %convolution_convert_fusion = bf16[1024,2048]{1,0:T(8,128)(2,1)} fusion(bf16[256,1024]{1,0:T(8,128)(2,1)S(1)} %fusion.52, bf16[256,1024]{1,0:T(8,128)(2,1)S(1)} %fusion.49, f32[512,2048]{1,0:T(8,128)} %copy-done.12), kind=kOutput, calls=%fused_computation.27 | convolution fusion | flops 2161115136 | bytes 9437184 | tf_op jit(solution)/shard_map/dot_general | solution.py:451
  172.4 11.5 %fusion.27 = (f32[512]{0:T(512)S(1)}, f32[1024]{0:T(1024)S(1)}, f32[512,1024]{1,0:T(8,128)S(1)}) fusion(f32[1024]{0:T(1024)S(1)} %copy-done.7, f32[512]{0:T(512)S(1)} %add_rsqrt_fusion, bf16[256,1024]{1,0:T(8,128)(2,1)S(1)} %copy-done.1, bf16[256,1024]{1,0:T(8,128)(2,1)S(1)} %copy-done.2, f32[512,1024]{1,0:T(8,128)} %fusion.34, bf16[1024,2048]{1,0:T(8,128)(2,1)} %win.1, ...), kind=kOutput, calls=%fused_computation.44 | convolution fusion | flops 4323801600 | bytes 18886656 | tf_op jit(solution)/shard_map/dot_general | solution.py:451
  184.0 7.0 %convolution_convert_fusion.1 = bf16[1024,2048]{1,0:T(8,128)(2,1)} fusion(bf16[256,1024]{1,0:T(8,128)(2,1)} %copy-done.5, bf16[256,1024]{1,0:T(8,128)(2,1)} %copy-done.3, f32[512,2048]{1,0:T(8,128)} %copy-done.11), kind=kOutput, calls=%fused_computation.28 | convolution fusion | flops 2161115136 | bytes 9437184 | tf_op jit(solution)/shard_map/dot_general | solution.py:451
  191.7 1.0 fusion.79
  192.7 1.2 concatenate.11.small
  194.0 56.0 %reduce_all.1 = (f32[16,2048]{1,0:T(8,128)}, f32[16,128]{1,0:T(8,128)}) custom-call(bf16[32,2,16,2048]{3,2,1,0:T(8,128)(2,1)} %bitcast.24, bf16[32,2,16,2048]{3,2,1,0:T(8,128)(2,1)} %bitcast.23, f32[16,128]{1,0:T(8,128)} %concatenate.11.small), custom_call_target="tpu_custom_call" | custom-call | tf_op jit(solution)/shard_map/reduce_all/pallas_call | solution.py:424
  249.9 1.2 slice.28
  251.8 1.3 slice_bitcast_fusion
  253.0 1.6 copy.14
  (39 shorter events, 4.9 us)
Async XLA Ops:
  3.4 7.2 %copy-start = (bf16[2048,1024]{1,0:T(8,128)(2,1)S(1)}, bf16[2048,1024]{1,0:T(8,128)(2,1)}, u32[]{:S(2)}) copy-start(bf16[2048,1024]{1,0:T(8,128)(2,1)} %wout.1) | copy-start | bytes 12582916
  8.5 2.1 copy-start.11
  14.6 39.6 %copy-start.1 = (bf16[256,1024]{1,0:T(8,128)(2,1)S(1)}, bf16[256,1024]{1,0:T(8,128)(2,1)}, u32[]{:S(2)}) copy-start(bf16[256,1024]{1,0:T(8,128)(2,1)} %param.7) | copy-start | bytes 1572868
  14.6 39.6 %copy-start.2 = (bf16[256,1024]{1,0:T(8,128)(2,1)S(1)}, bf16[256,1024]{1,0:T(8,128)(2,1)}, u32[]{:S(2)}) copy-start(bf16[256,1024]{1,0:T(8,128)(2,1)} %param.6) | copy-start | bytes 1572868
  14.6 39.6 %copy-start.7 = (f32[1024]{0:T(1024)S(1)}, f32[1024]{0:T(1024)}, u32[]{:S(2)}) copy-start(f32[1024]{0:T(1024)} %param.9) | copy-start | bytes 12292
  54.2 4.8 %copy-start.10 = (bf16[2048,1024]{1,0:T(8,128)(2,1)S(1)}, bf16[2048,1024]{1,0:T(8,128)(2,1)}, u32[]{:S(2)}) copy-start(bf16[2048,1024]{1,0:T(8,128)(2,1)} %get-tuple-element.13) | copy-start | bytes 12582916
  54.2 4.8 %copy-start.13 = (f32[512,1024]{1,0:T(8,128)S(1)}, f32[512,1024]{1,0:T(8,128)}, u32[]{:S(2)}) copy-start(f32[512,1024]{1,0:T(8,128)} %fusion.78) | copy-start | bytes 6291460
  59.0 2.7 %copy-start.12 = (f32[512,2048]{1,0:T(8,128)}, f32[512,2048]{1,0:T(8,128)S(1)}, u32[]{:S(2)}) copy-start(f32[512,2048]{1,0:T(8,128)S(1)} %fusion.53) | copy-start | bytes 12582916
  59.0 65.4 %copy-start.8 = (s32[256]{0:T(256)S(1)}, s32[256]{0:T(256)}, u32[]{:S(2)}) copy-start(s32[256]{0:T(256)} %param.8) | copy-start | bytes 3076
  124.5 6.5 %copy-start.9 = (bf16[2560,1024]{1,0:T(8,128)(2,1)S(1)}, bf16[2560,1024]{1,0:T(8,128)(2,1)}, u32[]{:S(2)}) copy-start(bf16[2560,1024]{1,0:T(8,128)(2,1)} %get-tuple-element.15) | copy-start | bytes 15728644
  133.0 32.5 %copy-start.3 = (bf16[256,1024]{1,0:T(8,128)(2,1)}, bf16[256,1024]{1,0:T(8,128)(2,1)S(1)}, u32[]{:S(2)}) copy-start(bf16[256,1024]{1,0:T(8,128)(2,1)S(1)} %fusion.49) | copy-start | bytes 1572868
  153.7 11.8 %copy-start.5 = (bf16[256,1024]{1,0:T(8,128)(2,1)}, bf16[256,1024]{1,0:T(8,128)(2,1)S(1)}, u32[]{:S(2)}) copy-start(bf16[256,1024]{1,0:T(8,128)(2,1)S(1)} %fusion.52) | copy-start | bytes 1572868
  183.9 7.1 %copy-start.4 = (bf16[256,1024]{1,0:T(8,128)(2,1)S(1)}, bf16[256,1024]{1,0:T(8,128)(2,1)}, u32[]{:S(2)}) copy-start(bf16[256,1024]{1,0:T(8,128)(2,1)} %copy-done.3) | copy-start | bytes 1572868
  184.0 7.1 %copy-start.6 = (bf16[256,1024]{1,0:T(8,128)(2,1)S(1)}, bf16[256,1024]{1,0:T(8,128)(2,1)}, u32[]{:S(2)}) copy-start(bf16[256,1024]{1,0:T(8,128)(2,1)} %copy-done.5) | copy-start | bytes 1572868

commit v2 on v1

--- a/solution.py
+++ b/solution.py
@@ -295,16 +295,75 @@
 
 
 GROUP = 16
-
-
-def reduce_kernel(own, oth, small, out, total, r1, a1, r2, a2, r3, a3, r4, s_buf, sems):
+CHUNKS = 4
+
+
+def nt(a, b):
+    return lax.dot_general(a, b, (((1,), (1,)), ((), ())), preferred_element_type=jnp.float32)
+
+
+def nn(a, b):
+    return lax.dot_general(a, b, (((1,), (0,)), ((), ())), preferred_element_type=jnp.float32)
+
+
+def backward_kernel(
+    rows_ref,
+    up_ref,
+    upt_ref,
+    gain_ref,
+    loss_ref,
+    hid_hbm,
+    slope_hbm,
+    win_hbm,
+    oin_hbm,
+    wout_hbm,
+    oout_hbm,
+    out,
+    total,
+    grads,
+    hid,
+    slope,
+    win,
+    wout,
+    s1,
+    r1,
+    a1,
+    r2,
+    a2,
+    r3,
+    a3,
+    r4,
+    acc,
+    s_buf,
+    local,
+    sems,
+):
     x, y, zl, c, r = coords()
-    hid = own.shape[-1]
-    mid = hid // 2
+    width = up_ref.shape[1]
+    half = win_hbm.shape[1]
+    cols = 2 * half // CHUNKS
     sibling = device(x, y, zl, 1 - c, r)
     xs = [device(wrap(x + k, NX), y, zl, c, r) for k in range(1, RING)]
     ys = [device(x, wrap(y + k, NY), zl, c, r) for k in range(1, RING)]
     zs = [device(x, y, 1 - zl, c, r), device(x, y, zl, c, 1 - r), device(x, y, 1 - zl, c, 1 - r)]
+
+    loads = []
+
+    def load(src, dst):
+        op = pltpu.make_async_copy(src, dst, local.at[len(loads)])
+        op.start()
+        loads.append(op)
+
+    for j in range(CHUNKS):
+        part = pl.ds(j * cols, cols)
+        load(hid_hbm.at[:, part], hid.at[j])
+    for j in range(CHUNKS):
+        part = pl.ds(j * cols, cols)
+        load(slope_hbm.at[:, part], slope.at[j])
+    for k, (inner, outer) in enumerate(((win_hbm, wout_hbm), (oin_hbm, oout_hbm))):
+        load(inner, win.at[k])
+        load(outer, wout.at[k])
+
     greet([sibling] + xs + ys + zs)
     state = {"n": 0}
     ops = []
@@ -317,143 +376,197 @@
         ops.append(op)
         return op
 
-    s_buf[12] = small[...]
-
-    wait1 = [
-        send(own.at[:, 1 - c], r1.at[0], sibling),
-        send(oth.at[:, 1 - c], r1.at[1], sibling),
-        send(s_buf.at[12], s_buf.at[13], sibling),
-    ]
-    for op in wait1:
+    wait1 = []
+    for j in range(CHUNKS):
+        loads[j].wait()
+        s1[j] = nn(upt_ref[1 - c], hid[j]).astype(jnp.bfloat16)
+        wait1.append(send(s1.at[j], r1.at[j], sibling))
+
+    wait2 = []
+    for j in range(CHUNKS):
+        mine = nn(upt_ref[c], hid[j])
+        wait1[j].wait_recv()
+        mine = mine + r1[j].astype(jnp.float32)
+        a1[j] = mine.astype(jnp.bfloat16).reshape(NX, NY, NZ, GROUP, cols)
+        waits = []
+        for k in range(1, RING):
+            slot = RING - 1 - k
+            if j % 2 == 0:
+                waits.append(send(a1.at[j, wrap(x + k, NX)], r2.at[j, slot], xs[k - 1]))
+            else:
+                waits.append(send(a1.at[j, :, wrap(y + k, NY)], r2.at[j, slot], ys[k - 1]))
+        wait2.append(waits)
+
+    per_half = CHUNKS // 2
+    for j in range(CHUNKS):
+        loads[CHUNKS + j].wait()
+    for k in range(2):
+        loads[2 * CHUNKS + 2 * k].wait()
+        loads[2 * CHUNKS + 2 * k + 1].wait()
+    tile = 512
+    for j in range(CHUNKS):
+        k = j // per_half
+
+        def tile_step(t, _, j=j, k=k):
+            first = pl.multiple_of(t * tile, tile)
+            there = pl.multiple_of((j % per_half) * cols + t * tile, tile)
+            g_act = nt(up_ref[...], wout[k, pl.ds(there, tile), :])
+            g_pre = (g_act * slope[j, :, pl.ds(first, tile)].astype(jnp.float32)).astype(
+                jnp.bfloat16
+            )
+            step = nt(g_pre, win[k, :, pl.ds(there, tile)])
+            if j == 0:
+                before = jnp.where(t == 0, 0.0, acc[...])
+            else:
+                before = acc[...]
+            acc[...] = before + step
+            return 0
+
+        if j == 0:
+            acc[...] = jnp.zeros_like(acc)
+        lax.fori_loop(0, cols // tile, tile_step, 0)
+
+    values = rows_ref[...].astype(jnp.float32)
+    inv_rms = lax.rsqrt(jnp.mean(values * values, axis=1, keepdims=True) + EPSILON)
+    unit_rows = values * inv_rms
+    g_norm = acc[...]
+    weighted = g_norm * unit_rows
+    gain_term = jnp.sum(weighted, axis=0, keepdims=True)
+    gain = gain_ref[...]
+    mean = jnp.mean(weighted * gain, axis=1, keepdims=True)
+    d_values = inv_rms * (g_norm * gain - unit_rows * mean)
+    grads[...] = (up_ref[...].astype(jnp.float32) + d_values).astype(jnp.bfloat16)
+
+    row = lax.broadcasted_iota(jnp.int32, (8, width), 0)
+    s_buf[12] = jnp.where(
+        row == 0,
+        jnp.broadcast_to(gain_term, (8, width)),
+        jnp.broadcast_to(loss_ref[0:1, 0:1], (8, width)),
+    )
+    small = send(s_buf.at[12], s_buf.at[13], sibling)
+    small.wait_recv()
+    s_buf[x] = s_buf[12] + s_buf[13]
+    small = [send(s_buf.at[x], s_buf.at[x], peer) for peer in xs]
+
+    wait3 = []
+    for j in range(CHUNKS):
+        for op in wait2[j]:
+            op.wait_recv()
+        tot = (a1[j, x] if j % 2 == 0 else a1[j, :, y]).astype(jnp.float32)
+        for k in range(RING - 1):
+            tot = tot + r2[j, k].astype(jnp.float32)
+        a2[j] = tot.astype(jnp.bfloat16)
+        waits = []
+        for k in range(1, RING):
+            slot = RING - 1 - k
+            if j % 2 == 0:
+                waits.append(send(a2.at[j, wrap(y + k, NY)], r3.at[j, slot], ys[k - 1]))
+            else:
+                waits.append(send(a2.at[j, wrap(x + k, NX)], r3.at[j, slot], xs[k - 1]))
+        wait3.append(waits)
+        if j == 1:
+            for op in small:
+                op.wait_recv()
+            s_buf[4 + y] = ((s_buf[0] + s_buf[1]) + s_buf[2]) + s_buf[3]
+            small = [send(s_buf.at[4 + y], s_buf.at[4 + y], peer) for peer in ys]
+
+    for op in small:
         op.wait_recv()
-    s_buf[x] = s_buf[12] + s_buf[13]
-    for h, ref in enumerate((own, oth)):
-
-        def add1(g, _):
-            a1[h, g] = (
-                ref[g, c].astype(jnp.float32) + r1[h, g].astype(jnp.float32)
-            ).astype(jnp.bfloat16)
-            return 0
-
-        lax.fori_loop(0, NX * NY * NZ, add1, 0)
-
-    wait2 = []
-    for k in range(1, RING):
-        slot = RING - 1 - k
-        tx = wrap(x + k, NX)
-        ty = wrap(y + k, NY)
-        for h in range(2):
-            wait2.append(
-                send(
-                    a1.at[h, pl.ds(tx * NY * NZ, NY * NZ), :, pl.ds(0, mid)],
-                    r2.at[0, slot, h],
-                    xs[k - 1],
-                )
-            )
-            for xx in range(NX):
-                wait2.append(
-                    send(
-                        a1.at[h, pl.ds((xx * NY + ty) * NZ, NZ), :, pl.ds(mid, mid)],
-                        r2.at[1, slot, h, pl.ds(xx * NZ, NZ)],
-                        ys[k - 1],
-                    )
-                )
-        wait2.append(send(s_buf.at[x], s_buf.at[x], xs[k - 1]))
-    for op in wait2:
+    here = s_buf.at[8 + 2 * r + zl]
+    here[...] = ((s_buf[4] + s_buf[5]) + s_buf[6]) + s_buf[7]
+    small = [send(here, here, peer) for peer in zs]
+
+    wait4 = []
+    for j in range(CHUNKS):
+        for op in wait3[j]:
+            op.wait_recv()
+        tot = (a2[j, y] if j % 2 == 0 else a2[j, x]).astype(jnp.float32)
+        for k in range(RING - 1):
+            tot = tot + r3[j, k].astype(jnp.float32)
+        a3[j] = tot.astype(jnp.bfloat16)
+        if j < per_half:
+            wait4.append([send(a3.at[j, 1 - zl], r4.at[0, j], zs[0])])
+        else:
+            i = j - per_half
+            wait4[i].append(send(a3.at[j, zl], r4.at[1, i], zs[1]))
+            wait4[i].append(send(a3.at[j, 1 - zl], r4.at[2, i], zs[2]))
+    for i in range(per_half):
+        for op in wait4[i]:
+            op.wait_recv()
+        out[:, i * cols : (i + 1) * cols] = (
+            a3[i, zl].astype(jnp.float32) + r4[0, i].astype(jnp.float32)
+        ) + (r4[1, i].astype(jnp.float32) + r4[2, i].astype(jnp.float32))
+    for op in small:
         op.wait_recv()
-    s_buf[4 + y] = ((s_buf[0] + s_buf[1]) + s_buf[2]) + s_buf[3]
-    for h in range(2):
-
-        def add2(g, _):
-            first = a1[h, x * NY * NZ + g, :, pl.ds(0, mid)].astype(jnp.float32)
-            second = a1[h, (g // NZ * NY + y) * NZ + g % NZ, :, pl.ds(mid, mid)].astype(
-                jnp.float32
-            )
-            for k in range(RING - 1):
-                first += r2[0, k, h, g].astype(jnp.float32)
-                second += r2[1, k, h, g].astype(jnp.float32)
-            a2[0, h, g] = first.astype(jnp.bfloat16)
-            a2[1, h, g] = second.astype(jnp.bfloat16)
-            return 0
-
-        lax.fori_loop(0, NY * NZ, add2, 0)
-
-    wait3 = []
-    for k in range(1, RING):
-        slot = RING - 1 - k
-        tx = wrap(x + k, NX)
-        ty = wrap(y + k, NY)
-        wait3.append(send(a2.at[0, :, pl.ds(ty * NZ, NZ)], r3.at[0, slot], ys[k - 1]))
-        wait3.append(send(a2.at[1, :, pl.ds(tx * NZ, NZ)], r3.at[1, slot], xs[k - 1]))
-        wait3.append(send(s_buf.at[4 + y], s_buf.at[4 + y], ys[k - 1]))
-    for op in wait3:
-        op.wait_recv()
-    s_buf[8 + 2 * r + zl] = ((s_buf[4] + s_buf[5]) + s_buf[6]) + s_buf[7]
-    for part in range(2):
-        at = (y, x)[part]
-        for h in range(2):
-            for z in range(NZ):
-                tot = a2[part, h, at * NZ + z].astype(jnp.float32)
-                for k in range(RING - 1):
-                    tot += r3[part, k, h, z].astype(jnp.float32)
-                a3[h, z, :, part * mid : (part + 1) * mid] = tot.astype(jnp.bfloat16)
-
-    mine = s_buf.at[8 + 2 * r + zl]
-    wait4 = [
-        send(a3.at[0, 1 - zl], r4.at[0], zs[0]),
-        send(a3.at[1, zl], r4.at[1], zs[1]),
-        send(a3.at[1, 1 - zl], r4.at[2], zs[2]),
-    ] + [send(mine, mine, peer) for peer in zs]
-    for op in wait4:
-        op.wait_recv()
-    out[...] = (
-        (a3[0, zl].astype(jnp.float32) + r4[0].astype(jnp.float32))
-        + (r4[1].astype(jnp.float32) + r4[2].astype(jnp.float32))
-    )
     total[...] = (s_buf[8] + s_buf[9]) + (s_buf[10] + s_buf[11])
     for op in ops:
         op.wait_send()
 
 
-def reduce_all(own, oth, small):
-    hid = own.shape[1]
+def backward(rows_in, upstream, gain, loss_part, hidden, slope, w_in, o_in, w_out, o_out):
+    rows, width = rows_in.shape
+    half = w_in.shape[1]
+    cols = 2 * half // CHUNKS
     groups = NX * NY * NZ
-    shape = (groups, NC, GROUP, hid)
-    n_copies = 3 + 3 * (2 + 2 * NX + 1) + 9 + 6
-    bf = jnp.bfloat16
+    bf, f32 = jnp.bfloat16, jnp.float32
+    upt = upstream.T.reshape(groups, NC, GROUP, rows).transpose(1, 0, 2, 3)
+    upt = upt.reshape(NC, groups * GROUP, rows)
+    vmem = pl.BlockSpec(memory_space=pltpu.VMEM)
+    hbm = pl.BlockSpec(memory_space=pl.ANY)
     return pl.pallas_call(
-        reduce_kernel,
+        backward_kernel,
         out_shape=(
-            jax.ShapeDtypeStruct((GROUP, hid), jnp.float32),
-            jax.ShapeDtypeStruct(small.shape, jnp.float32),
+            jax.ShapeDtypeStruct((GROUP, half), f32),
+            jax.ShapeDtypeStruct((8, width), f32),
+            jax.ShapeDtypeStruct((rows, width), bf),
         ),
-        in_specs=[pl.BlockSpec(memory_space=pltpu.VMEM)] * 3,
-        out_specs=[pl.BlockSpec(memory_space=pltpu.VMEM)] * 2,
+        in_specs=[vmem] * 5 + [hbm] * 6,
+        out_specs=[vmem] * 3,
         scratch_shapes=[
-            pltpu.VMEM((2, groups, GROUP, hid), bf),
-            pltpu.VMEM((2, groups, GROUP, hid), bf),
-            pltpu.VMEM((2, RING - 1, 2, NY * NZ, GROUP, hid // 2), bf),
-            pltpu.VMEM((2, 2, NY * NZ, GROUP, hid // 2), bf),
-            pltpu.VMEM((2, RING - 1, 2, NZ, GROUP, hid // 2), bf),
-            pltpu.VMEM((2, NZ, GROUP, hid), bf),
-            pltpu.VMEM((3, GROUP, hid), bf),
-            pltpu.VMEM((14,) + small.shape, jnp.float32),
-            pltpu.SemaphoreType.DMA((2, n_copies)),
+            pltpu.VMEM((CHUNKS, rows, cols), bf),
+            pltpu.VMEM((CHUNKS, rows, cols), bf),
+            pltpu.VMEM((2,) + w_in.shape, bf),
+            pltpu.VMEM((2,) + w_out.shape, bf),
+            pltpu.VMEM((CHUNKS, groups * GROUP, cols), bf),
+            pltpu.VMEM((CHUNKS, groups * GROUP, cols), bf),
+            pltpu.VMEM((CHUNKS, NX, NY, NZ, GROUP, cols), bf),
+            pltpu.VMEM((CHUNKS, RING - 1, RING, NZ, GROUP, cols), bf),
+            pltpu.VMEM((CHUNKS, RING, NZ, GROUP, cols), bf),
+            pltpu.VMEM((CHUNKS, RING - 1, NZ, GROUP, cols), bf),
+            pltpu.VMEM((CHUNKS, NZ, GROUP, cols), bf),
+            pltpu.VMEM((3, CHUNKS // 2, GROUP, cols), bf),
+            pltpu.VMEM((rows, width), f32),
+            pltpu.VMEM((14, 8, width), f32),
+            pltpu.SemaphoreType.DMA((2 * CHUNKS + 4,)),
+            pltpu.SemaphoreType.DMA((2, 7 * CHUNKS + 16)),
         ],
         compiler_params=pltpu.CompilerParams(
-            collective_id=3, has_side_effects=True, vmem_limit_bytes=56 * MIB
+            collective_id=3, has_side_effects=True, vmem_limit_bytes=60 * MIB
         ),
-        name="reduce_all",
-    )(own.reshape(shape), oth.reshape(shape), small)
+        name="backward",
+    )(
+        rows_in,
+        upstream,
+        upt,
+        gain.reshape(1, width),
+        jnp.broadcast_to(loss_part, (8, 128)),
+        hidden,
+        slope,
+        w_in,
+        o_in,
+        w_out,
+        o_out,
+    )
 
 
 def dot(a, b, dims):
     return lax.dot_general(a, b, (dims, ((), ())), preferred_element_type=jnp.float32)
 
 
-def gelu_and_slope(p):
-    hidden, back = jax.vjp(lambda v: jax.nn.gelu(v, approximate=True), p)
-    return hidden, back
+def gelu_slope(p):
+    k = math.sqrt(2.0 / math.pi)
+    t = jnp.tanh(k * (p + 0.044715 * (p * p * p)))
+    return 0.5 * (1.0 + t) + 0.5 * p * (1.0 - t * t) * (k * (1.0 + 3 * 0.044715 * (p * p)))
 
 
 def on_device(query_in, doc_in, cluster, gain, w_in, w_out):
@@ -501,25 +614,13 @@
     doc_grad = (dot(back_weights, band_queries, ((1,), (0,))) * inv_root).astype(jnp.bfloat16)
     upstream = jnp.concatenate([query_grad, doc_grad], axis=0)
 
-    g_norm = jnp.zeros((2 * rows, width), jnp.float32)
-    downs = []
-    for p, h, up, down in zip(pre, hidden, (w_in, o_in), (w_out, o_out)):
-        g_act = dot(upstream, down, ((1,), (1,)))
-        g_pre = jax.vjp(lambda v: jax.nn.gelu(v, approximate=True), p)[1](g_act)[0]
-        g_norm = g_norm + dot(g_pre.astype(jnp.bfloat16), up, ((1,), (1,)))
-        downs.append(dot(upstream, h, ((0,), (0,))).astype(jnp.bfloat16))
-    gain_term = jnp.sum(g_norm * unit_rows, axis=0)
-    d_unit = g_norm * gain
-    d_values = inv_rms * (d_unit - unit_rows * jnp.mean(d_unit * unit_rows, axis=-1, keepdims=True))
-    grad_rows = (upstream.astype(jnp.float32) + d_values).astype(jnp.bfloat16)
-
-    small = jnp.concatenate(
-        [gain_term.reshape(width // 128, 128), jnp.broadcast_to(loss_part, (8, 128))], axis=0
-    )
-    down_t, total = reduce_all(downs[0], downs[1], small)
-    loss = total[width // 128, 0] / (rows * 2 * NBLK)
-    gain_total = total[: width // 128].reshape(width)
-    return (loss, down_t.T, gain_total, grad_rows[:rows], grad_rows[rows:])
+    hidden_all = jnp.concatenate(hidden, axis=1)
+    slope_all = jnp.concatenate([gelu_slope(p).astype(jnp.bfloat16) for p in pre], axis=1)
+    down_t, total, grad_rows = backward(
+        rows_in, upstream, gain, loss_part, hidden_all, slope_all, w_in, o_in, w_out, o_out
+    )
+    loss = total[1, 0] / (rows * 2 * NBLK)
+    return (loss, down_t.T, total[0], grad_rows[:rows], grad_rows[rows:])
 
 
 def solution(mesh):

time: 256 us -> 225 us (0.88)
  matrix products: 67.5 us -> 34.7 us
  Pallas kernels: 168 us -> 162 us
  local copies, waits for them, and re-layouts: 11.5 us -> 16 us
  other arithmetic: 5.65 us -> 8.61 us
    dot_general x7 -> x3, matrix products: 50.9 us -> 13.9 us  [dot(): lax.dot_general(a, b, (dims, ((), ())), preferred_element_type=jnp.float32)]
    pallas_call x1, Pallas kernels: 56 us -> 49.4 us  [backward(): pl.pallas_call(backward_kernel, out_shape=(jax.ShapeDtypeStruct((GROUP, h...]
    dot_general x2, matrix products: 9.84 us -> 14.7 us  [on_device(): jnp.dot(normed, w, preferred_element_type=jnp.float32)]
    concatenate x0 -> x1, other arithmetic: none -> 3.74 us  [on_device(): hidden_all = jnp.concatenate(hidden, axis=1)]
where the time goes in v2:
time: 225 us; the launch traced here: 224 us
  Pallas kernels  162 us (72%)
  matrix products  34.7 us (15%)
  local copies, waits for them, and re-layouts  16 us (7%)
  other arithmetic  8.61 us (4%)
  between operations  2.65 us (1%)
    pallas_call x1, Pallas kernels, gather_band(): pl.pallas_call(band_kernel, out_shape=[jax.ShapeDtypeStruct((SLOTS * v.sh...  61 us
    pallas_call x1, Pallas kernels, backward(): pl.pallas_call(backward_kernel, out_shape=(jax.ShapeDtypeStruct((GROUP, h...  49.4 us
    pallas_call x1, Pallas kernels, gather_weights(): pl.pallas_call(weights_kernel, out_shape=(jax.ShapeDtypeStruct(w_in.shape...  39.6 us
    dot_general x2, matrix products, on_device(): jnp.dot(normed, w, preferred_element_type=jnp.float32)  14.7 us
    dot_general x3, matrix products, dot(): lax.dot_general(a, b, (dims, ((), ())), preferred_element_type=jnp.float32)  13.9 us
    pallas_call x1, Pallas kernels, exchange_totals(): pl.pallas_call(totals_kernel, out_shape=jax.ShapeDtypeStruct((SLOTS, 8, 1...  12.1 us

profile of v2, /device:TPU:0, one launch (start us, length us, event | category | flops | bytes accessed | tf_op | source)
XLA Modules:
  0.0 224.0 jit_solution(7859015962127259729)
XLA Ops:
  1.9 1.1 constant_dynamic-update-slice_fusion.1
  3.0 1.1 constant_dynamic-update-slice_fusion.rows_ref
  4.4 7.4 %fusion.8 = (bf16[512,2048]{1,0:T(8,128)(2,1)S(1)}, bf16[512,2048]{1,0:T(8,128)(2,1)S(1)}) fusion(bf16[1024,2048]{1,0:T(8,128)(2,1)} %win_hbm.1, bf16[512,1024]{1,0:T(8,128)(2,1)S(1)} %constant_dynamic-update-slice_fusion.rows_ref, f32[1024]{0:T(1024)S(1)} %copy-done.7, f32[512]{0:T(512)S(1)} %add_rsqrt_fusion), kind=kOutput, calls=%fused_computation.12 | convolution fusion | flops 2169503744 | bytes 9443328 | tf_op jit(solution)/shard_map/dot_general | solution.py:582
  11.8 1.3 copy-done.3
  13.1 3.7 %fusion.55 = f32[512,1024]{1,0:T(8,128)} fusion(bf16[512,2048]{1,0:T(8,128)(2,1)S(1)} %get-tuple-element.26, bf16[2048,1024]{1,0:T(8,128)(2,1)S(1)} %copy-done), kind=kOutput, calls=%fused_computation.78 | convolution fusion | flops 2147483648 | bytes 8388608 | tf_op jit(solution)/shard_map/dot_general | solution.py:584
  16.8 39.6 %gather_weights.1 = (bf16[1024,2048]{1,0:T(8,128)(2,1)}, bf16[2048,1024]{1,0:T(8,128)(2,1)}) custom-call(bf16[1024,2048]{1,0:T(8,128)(2,1)} %win_hbm.1, bf16[2048,1024]{1,0:T(8,128)(2,1)} %wout_hbm.1), custom_call_target="tpu_custom_call" | custom-call | tf_op jit(solution)/shard_map/gather_weights/pallas_call | solution.py:120
  56.4 7.4 %fusion.17 = (bf16[512,2048]{1,0:T(8,128)(2,1)S(1)}, bf16[512,2048]{1,0:T(8,128)(2,1)S(1)}) fusion(bf16[1024,2048]{1,0:T(8,128)(2,1)} %get-tuple-element.13.oin_hbm, bf16[512,1024]{1,0:T(8,128)(2,1)S(1)} %constant_dynamic-update-slice_fusion.rows_ref, f32[1024]{0:T(1024)S(1)} %copy-done.7, f32[512]{0:T(512)S(1)} %add_rsqrt_fusion), kind=kOutput, calls=%fused_computation.21 | convolution fusion | flops 2169503744 | bytes 9443328 | tf_op jit(solution)/shard_map/dot_general | solution.py:582
  63.8 2.4 %fusion.28 = bf16[512,1024]{1,0:T(8,128)(2,1)S(1)} fusion(bf16[512,1024]{1,0:T(8,128)(2,1)S(1)} %constant_dynamic-update-slice_fusion.rows_ref, f32[512,1024]{1,0:T(8,128)S(1)} %copy-done.10, bf16[512,2048]{1,0:T(8,128)(2,1)S(1)} %get-tuple-element.28, bf16[2048,1024]{1,0:T(8,128)(2,1)S(1)} %copy-done.2), kind=kOutput, calls=%fused_computation.47 | convolution fusion | flops 2149580800 | bytes 10485760 | tf_op jit(solution)/shard_map/dot_general | solution.py:584
  66.3 3.7 %pad_maximum_fusion = (bf16[512,4096]{1,0:T(8,128)(2,1)}, bf16[512,4096]{1,0:T(8,128)(2,1)}) fusion(bf16[512,2048]{1,0:T(8,128)(2,1)S(1)} %get-tuple-element.28, bf16[512,2048]{1,0:T(8,128)(2,1)S(1)} %copy-done.4, bf16[512,2048]{1,0:T(8,128)(2,1)S(1)} %get-tuple-element.27, bf16[512,2048]{1,0:T(8,128)(2,1)S(1)} %get-tuple-element.25), kind=kLoop, calls=%fused_computation.22 | loop fusion | flops 16777216 | bytes 16777216 | tf_op jit(solution)/shard_map/concatenate | solution.py:617
  70.0 1.0 fusion.54
  71.0 61.0 %gather_band.1 = (bf16[2560,1024]{1,0:T(8,128)(2,1)}, bf16[160,256]{1,0:T(8,128)(2,1)}, bf16[2560,1024]{1,0:T(8,128)(2,1)}) custom-call(bf16[256,1024]{1,0:T(8,128)(2,1)} %get-tuple-element.34.docs, bf16[16,256]{1,0:T(8,128)(2,1)} %broadcast_in_dim.26.tags, bf16[256,1024]{1,0:T(8,128)(2,1)} %get-tuple-element.33.queries), custom_call_target="tpu_custom_call" | custom-call | tf_op jit(solution)/shard_map/gather_band/pallas_call | solution.py:237
  132.9 4.7 %fusion.30 = (f32[256]{0:T(256)S(1)}, f32[256,2560]{1,0:T(8,128)S(1)}) fusion(s32[256]{0:T(256)S(1)} %iota_add_fusion, s32[2560]{0:T(1024)S(1)} %reshape.61, s32[256]{0:T(256)S(1)} %copy-done.8, bf16[2560,1024]{1,0:T(8,128)(2,1)} %get-tuple-element.16, bf16[512,1024]{1,0:T(8,128)(2,1)} %copy-done.5), kind=kOutput, calls=%fused_computation.49 | convolution fusion | flops 1346109184 | bytes 8401920 | tf_op jit(solution)/shard_map/dot_general | solution.py:563
  137.6 1.2 select_reduce_fusion
  139.4 1.9 fusion.37
  141.9 1.2 broadcast_in_dim.30.loss_ref
  143.2 12.1 %exchange_totals.1 = f32[10,8,128]{2,1,0:T(8,128)} custom-call(f32[8,128]{1,0:T(8,128)} %pad.4.mine), custom_call_target="tpu_custom_call" | custom-call | tf_op jit(solution)/shard_map/exchange_totals/pallas_call | solution.py:282
  156.1 7.2 %fusion.40 = bf16[256,1024]{1,0:T(8,128)(2,1)S(1)} fusion(bf16[2560,1024]{1,0:T(8,128)(2,1)} %get-tuple-element.17, f32[2560]{0:T(1024)S(1)} %sub.46, s32[256]{0:T(256)S(1)} %iota_add_fusion, s32[2560]{0:T(1024)S(1)} %reshape.61, s32[256]{0:T(256)S(1)} %copy-done.8, bf16[512,1024]{1,0:T(8,128)(2,1)S(1)} %copy-done.6), kind=kOutput, calls=%fused_computation.58 | convolution fusion | flops 2690777088 | bytes 11560960 | tf_op jit(solution)/shard_map/dot_general | solution.py:563
  163.3 1.3 fusion.52
  165.3 1.1 copy.13
  166.4 49.4 %backward.1 = (f32[16,2048]{1,0:T(8,128)}, f32[8,1024]{1,0:T(8,128)}, bf16[512,1024]{1,0:T(8,128)(2,1)}) custom-call(bf16[512,1024]{1,0:T(8,128)(2,1)} %copy-done.1, bf16[512,1024]{1,0:T(8,128)(2,1)} %get-tuple-element.32.up_ref, bf16[2,512,512]{2,1,0:T(8,128)(2,1)} %bitcast.25, f32[1,1024]{1,0:T(1,128)} %bitcast.27, f32[8,128]{1,0:T(8,128)} %broadcast_in_dim.30.loss_ref, ...), custom_call_target="tpu_custom_call" | custom-call | tf_op jit(solution)/shard_map/backward/pallas_call | solution.py:516
  215.9 1.2 slice.28
  217.7 1.4 slice.29
  219.0 2.2 fusion.53
  221.3 1.6 copy.18
  (33 shorter events, 5.2 us)
Async XLA Ops:
  0.6 3.8 %copy-start.7 = (f32[1024]{0:T(1024)S(1)}, f32[1024]{0:T(1024)}, u32[]{:S(2)}) copy-start(f32[1024]{0:T(1024)} %param.9) | copy-start | bytes 12292
  4.1 59.7 %copy-start.1 = (bf16[512,1024]{1,0:T(8,128)(2,1)}, bf16[512,1024]{1,0:T(8,128)(2,1)S(1)}, u32[]{:S(2)}) copy-start(bf16[512,1024]{1,0:T(8,128)(2,1)S(1)} %constant_dynamic-update-slice_fusion.rows_ref) | copy-start | bytes 3145732
  4.4 8.7 %copy-start = (bf16[2048,1024]{1,0:T(8,128)(2,1)S(1)}, bf16[2048,1024]{1,0:T(8,128)(2,1)}, u32[]{:S(2)}) copy-start(bf16[2048,1024]{1,0:T(8,128)(2,1)} %wout_hbm.1) | copy-start | bytes 12582916
  11.8 1.3 copy-start.3
  56.4 7.4 %copy-start.2 = (bf16[2048,1024]{1,0:T(8,128)(2,1)S(1)}, bf16[2048,1024]{1,0:T(8,128)(2,1)}, u32[]{:S(2)}) copy-start(bf16[2048,1024]{1,0:T(8,128)(2,1)} %get-tuple-element.14.oout_hbm) | copy-start | bytes 12582916
  56.4 7.4 %copy-start.10 = (f32[512,1024]{1,0:T(8,128)S(1)}, f32[512,1024]{1,0:T(8,128)}, u32[]{:S(2)}) copy-start(f32[512,1024]{1,0:T(8,128)} %fusion.55) | copy-start | bytes 6291460
  63.8 2.4 %copy-start.4 = (bf16[512,2048]{1,0:T(8,128)(2,1)S(1)}, bf16[512,2048]{1,0:T(8,128)(2,1)}, u32[]{:S(2)}) copy-start(bf16[512,2048]{1,0:T(8,128)(2,1)} %copy-done.3) | copy-start | bytes 6291460
  66.2 3.8 %copy-start.5 = (bf16[512,1024]{1,0:T(8,128)(2,1)}, bf16[512,1024]{1,0:T(8,128)(2,1)S(1)}, u32[]{:S(2)}) copy-start(bf16[512,1024]{1,0:T(8,128)(2,1)S(1)} %fusion.28) | copy-start | bytes 3145732
  70.0 62.9 %copy-start.8 = (s32[256]{0:T(256)S(1)}, s32[256]{0:T(256)}, u32[]{:S(2)}) copy-start(s32[256]{0:T(256)} %param.8) | copy-start | bytes 3076
  132.9 6.5 %copy-start.9 = (bf16[2560,1024]{1,0:T(8,128)(2,1)S(1)}, bf16[2560,1024]{1,0:T(8,128)(2,1)}, u32[]{:S(2)}) copy-start(bf16[2560,1024]{1,0:T(8,128)(2,1)} %get-tuple-element.16) | copy-start | bytes 15728644
  139.4 16.7 %copy-start.6 = (bf16[512,1024]{1,0:T(8,128)(2,1)S(1)}, bf16[512,1024]{1,0:T(8,128)(2,1)}, u32[]{:S(2)}) copy-start(bf16[512,1024]{1,0:T(8,128)(2,1)} %copy-done.5) | copy-start | bytes 3145732

commit v3 on v2

v3 whole, which is shorter than its diff:
```python
import math

import jax
import jax.numpy as jnp
from jax import lax
from jax.experimental import pallas as pl
from jax.experimental.pallas import tpu as pltpu
from jax.sharding import PartitionSpec as P

MESH = pl.DeviceIdType.MESH
MIB = 2**20
NX, NY, NZ, NC = 4, 4, 2, 2
NBLK = NX * NY * NZ * NC
RING = NX
EPSILON = 1e-06
SLOTS = 10
OWN = 4


def coords():
    b = lax.axis_index("blk")
    r = lax.axis_index("rep")
    return b // (NY * NZ * NC), (b // (NZ * NC)) % NY, (b // NC) % NZ, b % NC, r


def device(x, y, zl, c, r):
    return {"blk": ((x * NY + y) * NZ + zl) * NC + c, "rep": r}


def wrap(v, n):
    return lax.rem(v + n, n)


def greet(peers):
    barrier = pltpu.get_barrier_semaphore()
    for peer in peers:
        pl.semaphore_signal(barrier, inc=1, device_id=peer, device_id_type=MESH)
    pl.semaphore_wait(barrier, len(peers))


def remote(src, dst, send, recv, peer):
    return pltpu.make_async_remote_copy(
        src_ref=src,
        dst_ref=dst,
        send_sem=send,
        recv_sem=recv,
        device_id=peer,
        device_id_type=MESH,
    )


WBLK = 256
W_CHUNKS = 8
STRIP = 64


def nt(a, b):
    return lax.dot_general(a, b, (((1,), (1,)), ((), ())), preferred_element_type=jnp.float32)


def nn(a, b):
    return lax.dot_general(a, b, (((1,), (0,)), ((), ())), preferred_element_type=jnp.float32)


def gelu_both(p):
    k = math.sqrt(2.0 / math.pi)
    square = p * p
    t = jnp.tanh(p * (k + (k * 0.044715) * square))
    up = 0.5 + 0.5 * t
    slope = up + (0.5 * p) * ((1.0 - t * t) * (k + (3 * k * 0.044715) * square))
    return p * up, slope


def weight_view(in_ref, out_ref, block, chunk):
    if chunk < W_CHUNKS // 2:
        rows = in_ref.shape[0] // (W_CHUNKS // 2)
        return in_ref.at[
            pl.ds(chunk * rows, rows), pl.ds(pl.multiple_of(block * WBLK, WBLK), WBLK)
        ]
    rows = WBLK // (W_CHUNKS // 2)
    first = block * WBLK + (chunk - W_CHUNKS // 2) * rows
    return out_ref.at[pl.ds(pl.multiple_of(first, rows), rows)]


def forward_kernel(
    q_in,
    d_in,
    gain_ref,
    win_hbm,
    wout_hbm,
    q_emb,
    d_emb,
    hid_hbm,
    slope_hbm,
    oin_hbm,
    oout_hbm,
    win,
    wout,
    oin,
    oout,
    normed,
    hid,
    slope,
    pre,
    acc,
    local,
    stores,
    send,
    recv,
):
    x, y, zl, c, r = coords()
    cross = device(x, y, 1 - zl, c, 1 - r)
    near = device(x, y, 1 - zl, c, r)
    ahead = device(wrap(x + 1, NX), y, zl, c, r)
    behind = device(wrap(x - 1, NX), y, zl, c, r)
    sibling = device(x, y, zl, 1 - c, r)
    half = win_hbm.shape[1]
    rows = q_in.shape[0]
    load_in = pltpu.make_async_copy(win_hbm, win, local.at[0])
    load_out = pltpu.make_async_copy(wout_hbm, wout, local.at[1])
    load_in.start()
    load_out.start()
    greet([cross, near, ahead, behind, sibling])
    color = lax.rem(x + 2 * zl, 4)
    started = []

    def color_at(shift):
        return lax.rem(color + shift, 4)

    def block_of(shift):
        return 2 * color_at(shift) + c

    def copy(flow, block, chunk, peer, source=None):
        src = weight_view(*(source or (oin, oout)), block, chunk)
        dst = weight_view(oin, oout, block, chunk)
        return remote(src, dst, send.at[flow, chunk], recv.at[flow, chunk], peer)

    def start(*args):
        op = copy(*args)
        op.start()
        started.append(op)

    def first_hop(chunk):
        mine = block_of(0)
        copy(0, mine, chunk, cross).wait_recv()
        start(1, mine, chunk, ahead)
        start(2, mine, chunk, behind)
        start(3, mine, chunk, near)
        start(4, mine, chunk, sibling)

    def second_hop(chunk):
        for flow, shift in ((1, 3), (2, 1), (3, 2)):
            block = block_of(shift)
            copy(flow, block, chunk, near).wait_recv()
            start(4 + shift, block, chunk, sibling)

    def from_sibling(shift, chunks):
        block = 2 * color_at(shift) + (1 - c)
        for chunk in chunks:
            copy(4 + shift, block, chunk, sibling).wait_recv()

    stored = []

    def store(src, dst):
        op = pltpu.make_async_copy(src, dst, stores.at[len(stored)])
        op.start()
        stored.append(op)

    tile = 2 * WBLK

    def activate(block):
        def strip(i, _):
            at = pl.ds(pl.multiple_of(i * STRIP, STRIP), STRIP)
            h, s = gelu_both(pre[at, :])
            hid[block, at, :] = h.astype(jnp.bfloat16)
            slope[block, at, :] = s.astype(jnp.bfloat16)
            return 0

        lax.fori_loop(0, 2 * rows // STRIP, strip, 0)
        there = (block // 2, slice(None), pl.ds(pl.multiple_of((block % 2) * tile, tile), tile))
        store(hid.at[block], hid_hbm.at[there])
        store(slope.at[block], slope_hbm.at[there])

    def up_own(t):
        pre[...] = nn(normed[...], win[:, t * tile : (t + 1) * tile])
        activate(t)

    def down_own(t):
        step = nn(hid[t], wout[t * tile : (t + 1) * tile, :])
        acc[...] = step if t == 0 else acc[...] + step

    def up_other(shift):
        from_sibling(shift, range(W_CHUNKS // 2))
        at = pl.ds(pl.multiple_of(color_at(shift) * tile, tile), tile)
        pre[...] = nn(normed[...], oin[:, at])
        activate(half // tile + color_at(shift))
        store(oin.at[:, at], oin_hbm.at[:, at])

    def down_other(shift):
        from_sibling(shift, range(W_CHUNKS // 2, W_CHUNKS))
        at = pl.ds(pl.multiple_of(color_at(shift) * tile, tile), tile)
        acc[...] += nn(hid[half // tile + color_at(shift)], oout[at, :])
        store(oout.at[at, :], oout_hbm.at[at, :])

    for chunk in range(W_CHUNKS):
        start(0, block_of(2), chunk, cross, (win_hbm, wout_hbm))
    for k, ref in enumerate((q_in, d_in)):
        values = ref[...].astype(jnp.float32)
        inv_rms = lax.rsqrt(jnp.mean(values * values, axis=1, keepdims=True) + EPSILON)
        normed[k * rows : (k + 1) * rows, :] = ((values * inv_rms) * gain_ref[...]).astype(
            jnp.bfloat16
        )
    load_in.wait()
    up_own(0)
    first_hop(0)
    up_own(1)
    first_hop(1)
    second_hop(0)
    up_own(2)
    first_hop(2)
    second_hop(1)
    up_own(3)
    first_hop(3)
    second_hop(2)
    load_out.wait()
    down_own(0)
    down_own(1)
    first_hop(4)
    second_hop(3)
    up_other(0)
    first_hop(5)
    second_hop(4)
    up_other(1)
    first_hop(6)
    second_hop(5)
    up_other(2)
    first_hop(7)
    second_hop(6)
    up_other(3)
    second_hop(7)
    down_own(2)
    down_own(3)
    for shift in (0, 3, 1, 2):
        down_other(shift)
    for k, (ref, emb) in enumerate(((q_in, q_emb), (d_in, d_emb))):
        emb[...] = (ref[...].astype(jnp.float32) + acc[k * rows : (k + 1) * rows, :]).astype(
            jnp.bfloat16
        )
    for op in started:
        op.wait_send()
    for op in stored:
        op.wait()


def forward(q_in, d_in, gain, w_in, w_out):
    rows, width = q_in.shape
    half = w_in.shape[1]
    bf, f32 = jnp.bfloat16, jnp.float32
    tile = 2 * WBLK
    vmem = pl.BlockSpec(memory_space=pltpu.VMEM)
    hbm = pl.BlockSpec(memory_space=pl.ANY)
    per_chunk = jax.ShapeDtypeStruct((CHUNKS, 2 * rows, 2 * half // CHUNKS), bf)
    return pl.pallas_call(
        forward_kernel,
        out_shape=(
            jax.ShapeDtypeStruct(q_in.shape, bf),
            jax.ShapeDtypeStruct(d_in.shape, bf),
            per_chunk,
            per_chunk,
            jax.ShapeDtypeStruct(w_in.shape, bf),
            jax.ShapeDtypeStruct(w_out.shape, bf),
        ),
        in_specs=[vmem] * 3 + [hbm] * 2,
        out_specs=[vmem] * 2 + [hbm] * 4,
        scratch_shapes=[
            pltpu.VMEM(w_in.shape, bf),
            pltpu.VMEM(w_out.shape, bf),
            pltpu.VMEM(w_in.shape, bf),
            pltpu.VMEM(w_out.shape, bf),
            pltpu.VMEM((2 * rows, width), bf),
            pltpu.VMEM((2 * half // tile, 2 * rows, tile), bf),
            pltpu.VMEM((2 * half // tile, 2 * rows, tile), bf),
            pltpu.VMEM((2 * rows, tile), f32),
            pltpu.VMEM((2 * rows, width), f32),
            pltpu.SemaphoreType.DMA((2,)),
            pltpu.SemaphoreType.DMA((2 * 2 * half // tile + 8,)),
            pltpu.SemaphoreType.DMA((8, W_CHUNKS)),
            pltpu.SemaphoreType.DMA((8, W_CHUNKS)),
        ],
        compiler_params=pltpu.CompilerParams(
            collective_id=0, has_side_effects=True, vmem_limit_bytes=56 * MIB
        ),
        name="forward",
    )(q_in, d_in, gain.reshape(1, width), w_in, w_out)


PIECES = (
    (0, 0, 64, 0, 0),
    (1, 0, 16, 0, 0),
    (0, 64, 64, 1, 0),
    (0, 128, 80, 0, 0),
    (0, 208, 48, 1, 1),
    (2, 0, 64, 0, 0),
    (2, 64, 64, 1, 0),
    (2, 128, 80, 0, 0),
    (2, 208, 48, 1, 1),
)
DOC_PIECES = (0, 1, 2, 3, 4)
QUERY_PIECES = (5, 6, 7, 8)
DETOUR_ROWS = 48


def band_kernel(
    docs, tags, queries, column_tag, up, loss, gd, gx, gq, transit, s, w, lt, mine, acc, send, recv, tsem
):
    x, y, zl, c, r = coords()
    b = lax.axis_index("blk")
    rows, width = docs.shape
    inv_root = 1.0 / math.sqrt(width)
    cross = device(x, y, 1 - zl, c, 1 - r)
    near = device(x, y, 1 - zl, c, r)
    sibling = device(x, y, zl, 1 - c, r)
    step = NZ * NC * (1 - 2 * zl)
    onward = {"blk": wrap(b + step, NBLK), "rep": r}
    source = {"blk": wrap(b - step, NBLK), "rep": r}
    peers = []
    for offset in range(-2, 3):
        for other in range(2):
            if offset or other:
                rep = 1 - r if other else r
                peers.append((offset, other, {"blk": wrap(b + offset, NBLK), "rep": rep}))
    greet([peer for _, _, peer in peers] + [onward, source])

    def view(slot, p):
        kind, first, count = PIECES[p][:3]
        return (gd, gx, gq)[kind].at[slot, pl.ds(first, count)]

    def own(p):
        kind, first, count = PIECES[p][:3]
        return (docs, tags, queries)[kind].at[pl.ds(first, count)]

    z_slot = 8 - 8 * zl
    far_slot = 8 * zl
    theirs = 8 * zl
    started = []

    def make(flow, p, src, dst, peer):
        return remote(src, dst, send.at[flow, p], recv.at[flow, p], peer)

    def start(*args):
        op = make(*args)
        op.start()
        started.append(op)

    def arrived(flow, p, slot):
        make(flow, p, view(slot, p), view(slot, p), near).wait_recv()

    def band_to_sibling(p):
        return [
            make(7 + k, p, view(8 - 8 * c + k, p), view(6 - 4 * c + k, p), sibling)
            for k in range(2)
        ]

    def through(p):
        return transit.at[p // 5]

    def send_own(p):
        start(0, p, own(p), view(theirs, p), near)
        start(1, p, own(p), view(theirs + 1, p), cross)
        if PIECES[p][4]:
            start(9, p, own(p), through(p), source)
        start(5, p, own(p), view(2 + 4 * c, p), sibling)

    def from_z(p):
        by_near, detour = PIECES[p][3:]
        arrived(0, p, z_slot)
        if not detour:
            start(3, p, view(z_slot, p), view(far_slot, p), onward)
        if not by_near:
            start(2, p, view(z_slot, p), view(OWN + 1, p), cross)
        arrived(1, p, z_slot + 1)
        if not detour:
            start(4, p, view(z_slot + 1, p), view(far_slot + 1, p), onward)
        if by_near:
            start(2, p, view(z_slot + 1, p), view(OWN + 1, p), near)

        @pl.when(c == zl)
        def _():
            for op in band_to_sibling(p):
                op.start()

    def from_transit(p):
        if PIECES[p][4]:
            make(9, p, own(p), through(p), source).wait_recv()
            start(10, p, through(p), view(8 - 8 * zl, p), near)
            start(11, p, through(p), view(8 - 8 * zl + 1, p), cross)

    def from_rep(p):
        arrived(2, p, OWN + 1)
        start(6, p, view(OWN + 1, p), view(3 + 4 * c, p), sibling)

    def from_far(p):
        detour = PIECES[p][4]
        arrived(10 if detour else 3, p, far_slot)
        arrived(11 if detour else 4, p, far_slot + 1)

        @pl.when(c != zl)
        def _():
            for op in band_to_sibling(p):
                op.start()

    def from_sibling(p):
        arrived(5, p, 6 - 4 * c)
        arrived(6, p, 7 - 4 * c)

    def band_from_sibling(p):
        arrived(7, p, 2 + 4 * c)
        arrived(8, p, 3 + 4 * c)

    row = lax.broadcasted_iota(jnp.int32, (rows, rows), 0)
    col = lax.broadcasted_iota(jnp.int32, (rows, rows), 1)
    diagonal = row == col

    def masked(a, g, slot):
        scores = nt(a[...], g[slot]) * inv_root
        tag_row = gx[slot].astype(jnp.float32)[0:1, :]
        allowed = tag_row != column_tag[...]
        if isinstance(slot, int) and slot == OWN:
            allowed = allowed | diagonal
        return scores, jnp.where(allowed, scores, -jnp.inf)

    def score(slot):
        s[slot] = masked(queries, gd, slot)[1]

    def backward_of(slot):
        m = masked(docs, gq, slot)[1]
        wt = jnp.exp(m - lt[slot, 0:1, :])
        if isinstance(slot, int) and slot == OWN:
            wt = wt - diagonal.astype(jnp.float32)
        acc[...] += nn(wt.astype(jnp.bfloat16), gq[slot])

    for p in DOC_PIECES:
        send_own(p)
    gd[OWN] = docs[...]
    gq[OWN] = queries[...]
    gx[OWN] = tags[...]
    for p in DOC_PIECES:
        from_z(p)
    for p in QUERY_PIECES:
        send_own(p)
    for p in DOC_PIECES:
        from_transit(p)
    score(OWN)
    positive = jnp.sum(jnp.where(diagonal, s[OWN], 0.0), axis=1, keepdims=True)
    score(z_slot)
    score(z_slot + 1)
    for p in DOC_PIECES:
        from_rep(p)
    for p in DOC_PIECES[:3]:
        from_far(p)
    from_z(QUERY_PIECES[0])
    for p in DOC_PIECES[3:]:
        from_far(p)
    for p in DOC_PIECES:
        from_sibling(p)
    from_z(QUERY_PIECES[1])
    score(OWN + 1)
    score(6 - 4 * c)
    score(7 - 4 * c)
    score(far_slot)
    score(far_slot + 1)
    from_z(QUERY_PIECES[2])
    for p in DOC_PIECES:
        band_from_sibling(p)
    score(2 + 4 * c)
    score(3 + 4 * c)
    top = s[0]
    for slot in range(1, SLOTS):
        top = jnp.maximum(top, s[slot])
    row_max = jnp.max(top, axis=1, keepdims=True)
    total = jnp.exp(s[0] - row_max)
    for slot in range(1, SLOTS):
        total = total + jnp.exp(s[slot] - row_max)
    log_total = row_max + jnp.log(jnp.sum(total, axis=1, keepdims=True))
    loss[...] = jnp.broadcast_to(
        jnp.sum(log_total - positive, axis=0, keepdims=True), loss.shape
    )
    mine[...] = jnp.transpose(jnp.broadcast_to(log_total, (rows, 128)))[0:8, :]
    lt[OWN] = mine[...]
    tops = []
    for i, (offset, other, peer) in enumerate(peers):
        slot = (2 - offset) * 2 + other
        op = remote(mine, lt.at[slot], tsem.at[0, i], tsem.at[1, slot], peer)
        op.start()
        tops.append(op)
    from_z(QUERY_PIECES[3])
    for p in QUERY_PIECES:
        from_transit(p)
    for slot in range(SLOTS):
        wt = jnp.exp(s[slot] - log_total)
        if slot == OWN:
            wt = wt - diagonal.astype(jnp.float32)
        w[:, slot * rows : (slot + 1) * rows] = wt.astype(jnp.bfloat16)
    query_grad = nn(w[...], gd[...].reshape(SLOTS * rows, width))
    up[0:rows, :] = (query_grad * inv_root).astype(jnp.bfloat16)

    for slot in range(SLOTS):
        if slot != OWN:
            remote(mine, lt.at[slot], tsem.at[0, 0], tsem.at[1, slot], near).wait_recv()
    for p in QUERY_PIECES:
        from_rep(p)
    acc[...] = jnp.zeros_like(acc)
    backward_of(OWN)
    backward_of(z_slot)
    backward_of(z_slot + 1)
    backward_of(OWN + 1)
    for p in QUERY_PIECES:
        from_sibling(p)
    backward_of(6 - 4 * c)
    backward_of(7 - 4 * c)
    for p in QUERY_PIECES:
        from_far(p)
    backward_of(far_slot)
    backward_of(far_slot + 1)
    for p in QUERY_PIECES:
        band_from_sibling(p)
    backward_of(2 + 4 * c)
    backward_of(3 + 4 * c)
    up[rows : 2 * rows, :] = (acc[...] * inv_root).astype(jnp.bfloat16)

    for p in range(len(PIECES)):
        for op in band_to_sibling(p):
            op.wait_send()
    for op in started + tops:
        op.wait_send()


def band(docs, tags, queries, column_tag):
    rows, width = docs.shape
    bf, f32 = jnp.bfloat16, jnp.float32
    vmem = pl.BlockSpec(memory_space=pltpu.VMEM)
    return pl.pallas_call(
        band_kernel,
        out_shape=(
            jax.ShapeDtypeStruct((2 * rows, width), bf),
            jax.ShapeDtypeStruct((8, 128), f32),
        ),
        in_specs=[vmem] * 4,
        out_specs=[vmem] * 2,
        scratch_shapes=[
            pltpu.VMEM((SLOTS, rows, width), bf),
            pltpu.VMEM((SLOTS,) + tags.shape, bf),
            pltpu.VMEM((SLOTS, rows, width), bf),
            pltpu.VMEM((2, DETOUR_ROWS, width), bf),
            pltpu.VMEM((SLOTS, rows, rows), f32),
            pltpu.VMEM((rows, SLOTS * rows), bf),
            pltpu.VMEM((SLOTS, 8, rows), f32),
            pltpu.VMEM((8, rows), f32),
            pltpu.VMEM((rows, width), f32),
            pltpu.SemaphoreType.DMA((12, len(PIECES))),
            pltpu.SemaphoreType.DMA((12, len(PIECES))),
            pltpu.SemaphoreType.DMA((2, SLOTS)),
        ],
        compiler_params=pltpu.CompilerParams(
            collective_id=1, has_side_effects=True, vmem_limit_bytes=48 * MIB
        ),
        name="band",
    )(docs, tags, queries, column_tag)


GROUP = 16
CHUNKS = 4


def backward_kernel(
    rows_ref,
    up_ref,
    upt_ref,
    gain_ref,
    loss_ref,
    hid_hbm,
    slope_hbm,
    win_hbm,
    oin_hbm,
    wout_hbm,
    oout_hbm,
    out,
    total,
    grads,
    hid,
    slope,
    win,
    wout,
    s1,
    r1,
    a1,
    r2,
    a2,
    r3,
    a3,
    r4,
    acc,
    s_buf,
    local,
    sems,
):
    x, y, zl, c, r = coords()
    width = up_ref.shape[1]
    half = win_hbm.shape[1]
    cols = 2 * half // CHUNKS
    sibling = device(x, y, zl, 1 - c, r)
    xs = [device(wrap(x + k, NX), y, zl, c, r) for k in range(1, RING)]
    ys = [device(x, wrap(y + k, NY), zl, c, r) for k in range(1, RING)]
    zs = [device(x, y, 1 - zl, c, r), device(x, y, zl, c, 1 - r), device(x, y, 1 - zl, c, 1 - r)]

    loads = []

    def load(src, dst):
        op = pltpu.make_async_copy(src, dst, local.at[len(loads)])
        op.start()
        loads.append(op)

    for j in range(CHUNKS):
        load(hid_hbm.at[j], hid.at[j])
    for j in range(CHUNKS):
        load(slope_hbm.at[j], slope.at[j])
    for k, (inner, outer) in enumerate(((win_hbm, wout_hbm), (oin_hbm, oout_hbm))):
        load(inner, win.at[k])
        load(outer, wout.at[k])

    greet([sibling] + xs + ys + zs)
    state = {"n": 0}
    ops = []

    def send(src, dst, peer):
        n = state["n"]
        state["n"] = n + 1
        op = remote(src, dst, sems.at[0, n], sems.at[1, n], peer)
        op.start()
        ops.append(op)
        return op

    wait1 = []
    for j in range(CHUNKS):
        loads[j].wait()
        s1[j] = nn(upt_ref[1 - c], hid[j]).astype(jnp.bfloat16)
        wait1.append(send(s1.at[j], r1.at[j], sibling))

    wait2 = []
    for j in range(CHUNKS):
        mine = nn(upt_ref[c], hid[j])
        wait1[j].wait_recv()
        mine = mine + r1[j].astype(jnp.float32)
        a1[j] = mine.astype(jnp.bfloat16).reshape(NX, NY, NZ, GROUP, cols)
        waits = []
        for k in range(1, RING):
            slot = RING - 1 - k
            if j % 2 == 0:
                waits.append(send(a1.at[j, wrap(x + k, NX)], r2.at[j, slot], xs[k - 1]))
            else:
                waits.append(send(a1.at[j, :, wrap(y + k, NY)], r2.at[j, slot], ys[k - 1]))
        wait2.append(waits)

    per_half = CHUNKS // 2
    for j in range(CHUNKS):
        loads[CHUNKS + j].wait()
    for k in range(2):
        loads[2 * CHUNKS + 2 * k].wait()
        loads[2 * CHUNKS + 2 * k + 1].wait()
    tile = 512
    for j in range(CHUNKS):
        k = j // per_half

        def tile_step(t, _, j=j, k=k):
            first = pl.multiple_of(t * tile, tile)
            there = pl.multiple_of((j % per_half) * cols + t * tile, tile)
            g_act = nt(up_ref[...], wout[k, pl.ds(there, tile), :])
            g_pre = (g_act * slope[j, :, pl.ds(first, tile)].astype(jnp.float32)).astype(
                jnp.bfloat16
            )
            step = nt(g_pre, win[k, :, pl.ds(there, tile)])
            if j == 0:
                before = jnp.where(t == 0, 0.0, acc[...])
            else:
                before = acc[...]
            acc[...] = before + step
            return 0

        if j == 0:
            acc[...] = jnp.zeros_like(acc)
        lax.fori_loop(0, cols // tile, tile_step, 0)

    values = rows_ref[...].astype(jnp.float32)
    inv_rms = lax.rsqrt(jnp.mean(values * values, axis=1, keepdims=True) + EPSILON)
    unit_rows = values * inv_rms
    g_norm = acc[...]
    weighted = g_norm * unit_rows
    gain_term = jnp.sum(weighted, axis=0, keepdims=True)
    gain = gain_ref[...]
    mean = jnp.mean(weighted * gain, axis=1, keepdims=True)
    d_values = inv_rms * (g_norm * gain - unit_rows * mean)
    grads[...] = (up_ref[...].astype(jnp.float32) + d_values).astype(jnp.bfloat16)

    row = lax.broadcasted_iota(jnp.int32, (8, width), 0)
    s_buf[12] = jnp.where(
        row == 0,
        jnp.broadcast_to(gain_term, (8, width)),
        jnp.broadcast_to(loss_ref[0:1, 0:1], (8, width)),
    )
    small = send(s_buf.at[12], s_buf.at[13], sibling)
    small.wait_recv()
    s_buf[x] = s_buf[12] + s_buf[13]
    small = [send(s_buf.at[x], s_buf.at[x], peer) for peer in xs]

    wait3 = []
    for j in range(CHUNKS):
        for op in wait2[j]:
            op.wait_recv()
        tot = (a1[j, x] if j % 2 == 0 else a1[j, :, y]).astype(jnp.float32)
        for k in range(RING - 1):
            tot = tot + r2[j, k].astype(jnp.float32)
        a2[j] = tot.astype(jnp.bfloat16)
        waits = []
        for k in range(1, RING):
            slot = RING - 1 - k
            if j % 2 == 0:
                waits.append(send(a2.at[j, wrap(y + k, NY)], r3.at[j, slot], ys[k - 1]))
            else:
                waits.append(send(a2.at[j, wrap(x + k, NX)], r3.at[j, slot], xs[k - 1]))
        wait3.append(waits)
        if j == 1:
            for op in small:
                op.wait_recv()
            s_buf[4 + y] = ((s_buf[0] + s_buf[1]) + s_buf[2]) + s_buf[3]
            small = [send(s_buf.at[4 + y], s_buf.at[4 + y], peer) for peer in ys]

    for op in small:
        op.wait_recv()
    here = s_buf.at[8 + 2 * r + zl]
    here[...] = ((s_buf[4] + s_buf[5]) + s_buf[6]) + s_buf[7]
    small = [send(here, here, peer) for peer in zs]

    wait4 = []
    for j in range(CHUNKS):
        for op in wait3[j]:
            op.wait_recv()
        tot = (a2[j, y] if j % 2 == 0 else a2[j, x]).astype(jnp.float32)
        for k in range(RING - 1):
            tot = tot + r3[j, k].astype(jnp.float32)
        a3[j] = tot.astype(jnp.bfloat16)
        if j < per_half:
            wait4.append([send(a3.at[j, 1 - zl], r4.at[0, j], zs[0])])
        else:
            i = j - per_half
            wait4[i].append(send(a3.at[j, zl], r4.at[1, i], zs[1]))
            wait4[i].append(send(a3.at[j, 1 - zl], r4.at[2, i], zs[2]))
    for i in range(per_half):
        for op in wait4[i]:
            op.wait_recv()
        out[:, i * cols : (i + 1) * cols] = (
            a3[i, zl].astype(jnp.float32) + r4[0, i].astype(jnp.float32)
        ) + (r4[1, i].astype(jnp.float32) + r4[2, i].astype(jnp.float32))
    for op in small:
        op.wait_recv()
    total[...] = (s_buf[8] + s_buf[9]) + (s_buf[10] + s_buf[11])
    for op in ops:
        op.wait_send()


def backward(rows_in, upstream, gain, loss_part, hidden, slope, w_in, o_in, w_out, o_out):
    rows, width = rows_in.shape
    half = w_in.shape[1]
    cols = 2 * half // CHUNKS
    groups = NX * NY * NZ
    bf, f32 = jnp.bfloat16, jnp.float32
    upt = upstream.T.reshape(groups, NC, GROUP, rows).transpose(1, 0, 2, 3)
    upt = upt.reshape(NC, groups * GROUP, rows)
    vmem = pl.BlockSpec(memory_space=pltpu.VMEM)
    hbm = pl.BlockSpec(memory_space=pl.ANY)
    return pl.pallas_call(
        backward_kernel,
        out_shape=(
            jax.ShapeDtypeStruct((GROUP, half), f32),
            jax.ShapeDtypeStruct((8, width), f32),
            jax.ShapeDtypeStruct((rows, width), bf),
        ),
        in_specs=[vmem] * 5 + [hbm] * 6,
        out_specs=[vmem] * 3,
        scratch_shapes=[
            pltpu.VMEM((CHUNKS, rows, cols), bf),
            pltpu.VMEM((CHUNKS, rows, cols), bf),
            pltpu.VMEM((2,) + w_in.shape, bf),
            pltpu.VMEM((2,) + w_out.shape, bf),
            pltpu.VMEM((CHUNKS, groups * GROUP, cols), bf),
            pltpu.VMEM((CHUNKS, groups * GROUP, cols), bf),
            pltpu.VMEM((CHUNKS, NX, NY, NZ, GROUP, cols), bf),
            pltpu.VMEM((CHUNKS, RING - 1, RING, NZ, GROUP, cols), bf),
            pltpu.VMEM((CHUNKS, RING, NZ, GROUP, cols), bf),
            pltpu.VMEM((CHUNKS, RING - 1, NZ, GROUP, cols), bf),
            pltpu.VMEM((CHUNKS, NZ, GROUP, cols), bf),
            pltpu.VMEM((3, CHUNKS // 2, GROUP, cols), bf),
            pltpu.VMEM((rows, width), f32),
            pltpu.VMEM((14, 8, width), f32),
            pltpu.SemaphoreType.DMA((2 * CHUNKS + 4,)),
            pltpu.SemaphoreType.DMA((2, 7 * CHUNKS + 16)),
        ],
        compiler_params=pltpu.CompilerParams(
            collective_id=3, has_side_effects=True, vmem_limit_bytes=60 * MIB
        ),
        name="backward",
    )(
        rows_in,
        upstream,
        upt,
        gain.reshape(1, width),
        loss_part,
        hidden,
        slope,
        w_in,
        o_in,
        w_out,
        o_out,
    )


def on_device(query_in, doc_in, cluster, gain, w_in, w_out):
    rows, width = query_in.shape
    queries, docs, hidden, slope, o_in, o_out = forward(query_in, doc_in, gain, w_in, w_out)

    tags = jnp.broadcast_to(cluster.astype(jnp.bfloat16)[None, :], (16, rows))
    column_tag = cluster.astype(jnp.float32)[:, None]
    upstream, loss_part = band(docs, tags, queries, column_tag)

    rows_in = jnp.concatenate([query_in, doc_in], axis=0)
    down_t, total, grad_rows = backward(
        rows_in, upstream, gain, loss_part, hidden, slope, w_in, o_in, w_out, o_out
    )
    loss = total[1, 0] / (rows * 2 * NBLK)
    return (loss, down_t.T, total[0], grad_rows[:rows], grad_rows[rows:])


def solution(mesh):
    in_specs = (
        P(("blk", "rep"), None),
        P(("blk", "rep"), None),
        P(("blk", "rep")),
        P(),
        P(None, "rep"),
        P("rep", None),
    )
    out_specs = (P(), P("rep", "blk"), P(), P(("blk", "rep"), None), P(("blk", "rep"), None))
    return jax.shard_map(
        on_device, mesh=mesh, in_specs=in_specs, out_specs=out_specs, check_vma=False
    )
```

time: 225 us -> 168 us (0.75)
  matrix products: 34.7 us -> 0 us
  Pallas kernels: 162 us -> 152 us
  other arithmetic: 8.61 us -> 3.01 us
  local copies, waits for them, and re-layouts: 16 us -> 11 us
    dot_general x7 -> x0, matrix products: 34.7 us -> none  [the longest x2 14.7 us: on_device(): jnp.dot(normed, w, preferred_element_type=jnp.float32)]
    pallas_call x3 -> x2, Pallas kernels: 113 us -> 105 us  [the longest x1 57.7 us: band(): pl.pallas_call(band_kernel, out_shape=(jax.ShapeDtypeStruct((2 * rows, wi...]
    pallas_call x1, Pallas kernels: 49.4 us -> 46.8 us  [backward(): pl.pallas_call(backward_kernel, out_shape=(jax.ShapeDtypeStruct((GROUP, h...]
where the time goes in v3:
time: 168 us
  Pallas kernels  152 us (90%)
  local copies, waits for them, and re-layouts  11 us (7%)
  other arithmetic  3.01 us (2%)
  between operations  2.48 us (1%)
    pallas_call x1, Pallas kernels, band(): pl.pallas_call(band_kernel, out_shape=(jax.ShapeDtypeStruct((2 * rows, wi...  57.7 us
    pallas_call x1, Pallas kernels, forward(): pl.pallas_call(forward_kernel, out_shape=(jax.ShapeDtypeStruct(q_in.shape...  47 us
    pallas_call x1, Pallas kernels, backward(): pl.pallas_call(backward_kernel, out_shape=(jax.ShapeDtypeStruct((GROUP, h...  46.8 us
    unnamed x9, local copies, waits for them, and re-layouts  4.23 us
    slice x2, local copies, waits for them, and re-layouts, on_device(): return (loss, down_t.T, total[0], grad_rows[:rows], grad_rows[rows:])  3.59 us

profile of v3, /device:TPU:0, one launch (start us, length us, event | category | flops | bytes accessed | tf_op | source)
XLA Modules:
  0.0 168.0 jit_solution(3003378915891083232)
XLA Ops:
  0.6 0.8 fusion.1
  1.4 0.1 copy.12.column_tag
  1.5 2.3 %pad_maximum_fusion.rows_ref = bf16[512,1024]{1,0:T(8,128)(2,1)} fusion(bf16[256,1024]{1,0:T(8,128)(2,1)} %d_in.1, bf16[256,1024]{1,0:T(8,128)(2,1)} %q_in.1), kind=kLoop, calls=%fused_computation | loop fusion | flops 2097152 | bytes 2097152 | tf_op jit(solution)/shard_map/concatenate | solution.py:834
  3.8 47.0 %forward.1 = (bf16[256,1024]{1,0:T(8,128)(2,1)}, bf16[256,1024]{1,0:T(8,128)(2,1)}, bf16[4,512,1024]{2,1,0:T(8,128)(2,1)}, bf16[4,512,1024]{2,1,0:T(8,128)(2,1)}...) custom-call(bf16[256,1024]{1,0:T(8,128)(2,1)} %q_in.1, bf16[256,1024]{1,0:T(8,128)(2,1)} %d_in.1, ...), custom_call_target="tpu_custom_call" | custom-call | tf_op jit(solution)/shard_map/forward/pallas_call | solution.py:263
  50.8 0.0 copy-start.1
  50.8 1.0 copy-done.1
  51.8 0.0 copy-start.2
  51.8 1.0 copy-done.2
  52.9 57.7 %band.1 = (bf16[512,1024]{1,0:T(8,128)(2,1)S(1)}, f32[8,128]{1,0:T(8,128)S(1)}) custom-call(bf16[256,1024]{1,0:T(8,128)(2,1)S(1)} %copy-done.2, bf16[16,256]{1,0:T(8,128)(2,1)S(1)} %broadcast_in_dim.4.tags, bf16[256,1024]{1,0:T(8,128)(2,1)S(1)} %copy-done.1, f32[256,1]{1,0:T(8,128)S(1)} %copy.12.column_tag), custom_call_target="tpu_custom_call" | custom-call | tf_op jit(solution)/shard_map/band/pallas_call | solution.py:542
  110.6 0.0 copy-start.3
  110.6 0.6 copy-done.3
  111.2 0.0 copy-start
  111.2 0.8 copy.13
  111.9 1.1 copy.14
  113.0 0.0 copy-done
  113.0 46.8 %backward.1 = (f32[16,2048]{1,0:T(8,128)}, f32[8,1024]{1,0:T(8,128)}, bf16[512,1024]{1,0:T(8,128)(2,1)}) custom-call(bf16[512,1024]{1,0:T(8,128)(2,1)} %pad_maximum_fusion.rows_ref, bf16[512,1024]{1,0:T(8,128)(2,1)} %copy-done, bf16[2,512,512]{2,1,0:T(8,128)(2,1)} %bitcast.12, f32[1,1024]{1,0:T(1,128)} %bitcast.15, f32[8,128]{1,0:T(8,128)} %copy-done.3, ...), custom_call_target="tpu_custom_call" | custom-call | tf_op jit(solution)/shard_map/backward/pallas_call | solution.py:780
  159.8 1.2 slice.12
  161.7 1.4 slice.13
  163.0 2.2 %fusion = (bf16[256,1024]{1,0:T(8,128)(2,1)}, bf16[256,1024]{1,0:T(8,128)(2,1)}) fusion(bf16[512,1024]{1,0:T(8,128)(2,1)} %get-tuple-element.26), kind=kLoop, calls=%fused_computation.1 | loop fusion | bytes 2097152 | tf_op jit(solution)/shard_map/slice | solution.py:839
  165.3 1.6 copy.16
  (1 shorter events, 0.0 us)
Async XLA Ops:
  50.8 1.0 copy-start.1
  51.8 1.0 copy-start.2
  110.6 0.6 copy-start.3
  111.2 1.8 %copy-start = (bf16[512,1024]{1,0:T(8,128)(2,1)}, bf16[512,1024]{1,0:T(8,128)(2,1)S(1)}, u32[]{:S(2)}) copy-start(bf16[512,1024]{1,0:T(8,128)(2,1)S(1)} %get-tuple-element.18.up_ref) | copy-start | bytes 3145732

commit v4 on v3

--- a/solution.py
+++ b/solution.py
@@ -15,6 +15,7 @@
 EPSILON = 1e-06
 SLOTS = 10
 OWN = 4
+GROUP = 16
 
 
 def coords():
@@ -311,7 +312,28 @@
 
 
 def band_kernel(
-    docs, tags, queries, column_tag, up, loss, gd, gx, gq, transit, s, w, lt, mine, acc, send, recv, tsem
+    docs,
+    tags,
+    queries,
+    column_tag,
+    up,
+    upt,
+    loss,
+    gd,
+    gx,
+    gq,
+    transit,
+    s,
+    w,
+    lt,
+    mine,
+    acc,
+    up_v,
+    upt_v,
+    local,
+    send,
+    recv,
+    tsem,
 ):
     x, y, zl, c, r = coords()
     b = lax.axis_index("blk")
@@ -329,6 +351,10 @@
             if offset or other:
                 rep = 1 - r if other else r
                 peers.append((offset, other, {"blk": wrap(b + offset, NBLK), "rep": rep}))
+    own_docs = pltpu.make_async_copy(docs, gd.at[OWN], local.at[0])
+    own_queries = pltpu.make_async_copy(queries, gq.at[OWN], local.at[1])
+    own_docs.start()
+    own_queries.start()
     greet([peer for _, _, peer in peers] + [onward, source])
 
     def view(slot, p):
@@ -417,12 +443,25 @@
         arrived(7, p, 2 + 4 * c)
         arrived(8, p, 3 + 4 * c)
 
+    def hand_out(k, value):
+        up_v[k] = value
+        turned = jnp.transpose(value).reshape(width // (NC * GROUP), NC, GROUP, rows)
+        for core in range(NC):
+            upt_v[k, core] = turned[:, core].reshape(width // NC, rows)
+        ops = [
+            pltpu.make_async_copy(up_v.at[k], up.at[pl.ds(k * rows, rows)], local.at[2 + 2 * k]),
+            pltpu.make_async_copy(upt_v.at[k], upt.at[k], local.at[3 + 2 * k]),
+        ]
+        for op in ops:
+            op.start()
+        return ops
+
     row = lax.broadcasted_iota(jnp.int32, (rows, rows), 0)
     col = lax.broadcasted_iota(jnp.int32, (rows, rows), 1)
     diagonal = row == col
 
     def masked(a, g, slot):
-        scores = nt(a[...], g[slot]) * inv_root
+        scores = nt(a[OWN], g[slot]) * inv_root
         tag_row = gx[slot].astype(jnp.float32)[0:1, :]
         allowed = tag_row != column_tag[...]
         if isinstance(slot, int) and slot == OWN:
@@ -430,10 +469,10 @@
         return scores, jnp.where(allowed, scores, -jnp.inf)
 
     def score(slot):
-        s[slot] = masked(queries, gd, slot)[1]
+        s[slot] = masked(gq, gd, slot)[1]
 
     def backward_of(slot):
-        m = masked(docs, gq, slot)[1]
+        m = masked(gd, gq, slot)[1]
         wt = jnp.exp(m - lt[slot, 0:1, :])
         if isinstance(slot, int) and slot == OWN:
             wt = wt - diagonal.astype(jnp.float32)
@@ -441,9 +480,9 @@
 
     for p in DOC_PIECES:
         send_own(p)
-    gd[OWN] = docs[...]
-    gq[OWN] = queries[...]
     gx[OWN] = tags[...]
+    own_docs.wait()
+    own_queries.wait()
     for p in DOC_PIECES:
         from_z(p)
     for p in QUERY_PIECES:
@@ -502,7 +541,7 @@
             wt = wt - diagonal.astype(jnp.float32)
         w[:, slot * rows : (slot + 1) * rows] = wt.astype(jnp.bfloat16)
     query_grad = nn(w[...], gd[...].reshape(SLOTS * rows, width))
-    up[0:rows, :] = (query_grad * inv_root).astype(jnp.bfloat16)
+    outs = hand_out(0, (query_grad * inv_root).astype(jnp.bfloat16))
 
     for slot in range(SLOTS):
         if slot != OWN:
@@ -526,27 +565,31 @@
         band_from_sibling(p)
     backward_of(2 + 4 * c)
     backward_of(3 + 4 * c)
-    up[rows : 2 * rows, :] = (acc[...] * inv_root).astype(jnp.bfloat16)
+    outs += hand_out(1, (acc[...] * inv_root).astype(jnp.bfloat16))
 
     for p in range(len(PIECES)):
         for op in band_to_sibling(p):
             op.wait_send()
     for op in started + tops:
         op.wait_send()
+    for op in outs:
+        op.wait()
 
 
 def band(docs, tags, queries, column_tag):
     rows, width = docs.shape
     bf, f32 = jnp.bfloat16, jnp.float32
     vmem = pl.BlockSpec(memory_space=pltpu.VMEM)
+    hbm = pl.BlockSpec(memory_space=pl.ANY)
     return pl.pallas_call(
         band_kernel,
         out_shape=(
             jax.ShapeDtypeStruct((2 * rows, width), bf),
+            jax.ShapeDtypeStruct((2, NC, width // NC, rows), bf),
             jax.ShapeDtypeStruct((8, 128), f32),
         ),
-        in_specs=[vmem] * 4,
-        out_specs=[vmem] * 2,
+        in_specs=[hbm, vmem, hbm, vmem],
+        out_specs=[hbm, hbm, vmem],
         scratch_shapes=[
             pltpu.VMEM((SLOTS, rows, width), bf),
             pltpu.VMEM((SLOTS,) + tags.shape, bf),
@@ -557,25 +600,28 @@
             pltpu.VMEM((SLOTS, 8, rows), f32),
             pltpu.VMEM((8, rows), f32),
             pltpu.VMEM((rows, width), f32),
+            pltpu.VMEM((2, rows, width), bf),
+            pltpu.VMEM((2, NC, width // NC, rows), bf),
+            pltpu.SemaphoreType.DMA((6,)),
             pltpu.SemaphoreType.DMA((12, len(PIECES))),
             pltpu.SemaphoreType.DMA((12, len(PIECES))),
             pltpu.SemaphoreType.DMA((2, SLOTS)),
         ],
         compiler_params=pltpu.CompilerParams(
-            collective_id=1, has_side_effects=True, vmem_limit_bytes=48 * MIB
+            collective_id=1, has_side_effects=True, vmem_limit_bytes=60 * MIB
         ),
         name="band",
     )(docs, tags, queries, column_tag)
 
 
-GROUP = 16
 CHUNKS = 4
 
 
 def backward_kernel(
-    rows_ref,
-    up_ref,
-    upt_ref,
+    q_hbm,
+    d_hbm,
+    up_hbm,
+    upt_hbm,
     gain_ref,
     loss_ref,
     hid_hbm,
@@ -587,6 +633,9 @@
     out,
     total,
     grads,
+    in_v,
+    up_ref,
+    upt_ref,
     hid,
     slope,
     win,
@@ -605,7 +654,7 @@
     sems,
 ):
     x, y, zl, c, r = coords()
-    width = up_ref.shape[1]
+    rows, width = q_hbm.shape
     half = win_hbm.shape[1]
     cols = 2 * half // CHUNKS
     sibling = device(x, y, zl, 1 - c, r)
@@ -614,12 +663,18 @@
     zs = [device(x, y, 1 - zl, c, r), device(x, y, zl, c, 1 - r), device(x, y, 1 - zl, c, 1 - r)]
 
     loads = []
+    n_loads = [0]
 
     def load(src, dst):
-        op = pltpu.make_async_copy(src, dst, local.at[len(loads)])
+        nonlocal loads
+        op = pltpu.make_async_copy(src, dst, local.at[n_loads[0]])
         op.start()
+        n_loads[0] += 1
         loads.append(op)
-
+        return op
+
+    first_loads = [load(upt_hbm.at[k], upt_ref.at[k]) for k in range(2)]
+    loads = []
     for j in range(CHUNKS):
         load(hid_hbm.at[j], hid.at[j])
     for j in range(CHUNKS):
@@ -627,6 +682,11 @@
     for k, (inner, outer) in enumerate(((win_hbm, wout_hbm), (oin_hbm, oout_hbm))):
         load(inner, win.at[k])
         load(outer, wout.at[k])
+    late_loads = [
+        load(up_hbm, up_ref),
+        load(q_hbm, in_v.at[pl.ds(0, rows)]),
+        load(d_hbm, in_v.at[pl.ds(rows, rows)]),
+    ]
 
     greet([sibling] + xs + ys + zs)
     state = {"n": 0}
@@ -640,15 +700,21 @@
         ops.append(op)
         return op
 
+    def down_part(core, j):
+        return nn(upt_ref[0, core], hid[j, 0:rows, :]) + nn(upt_ref[1, core], hid[j, rows:, :])
+
     wait1 = []
     for j in range(CHUNKS):
         loads[j].wait()
-        s1[j] = nn(upt_ref[1 - c], hid[j]).astype(jnp.bfloat16)
+        if j == 0:
+            for op in first_loads:
+                op.wait()
+        s1[j] = down_part(1 - c, j).astype(jnp.bfloat16)
         wait1.append(send(s1.at[j], r1.at[j], sibling))
 
     wait2 = []
     for j in range(CHUNKS):
-        mine = nn(upt_ref[c], hid[j])
+        mine = down_part(c, j)
         wait1[j].wait_recv()
         mine = mine + r1[j].astype(jnp.float32)
         a1[j] = mine.astype(jnp.bfloat16).reshape(NX, NY, NZ, GROUP, cols)
@@ -667,6 +733,8 @@
     for k in range(2):
         loads[2 * CHUNKS + 2 * k].wait()
         loads[2 * CHUNKS + 2 * k + 1].wait()
+    for op in late_loads:
+        op.wait()
     tile = 512
     for j in range(CHUNKS):
         k = j // per_half
@@ -690,7 +758,7 @@
             acc[...] = jnp.zeros_like(acc)
         lax.fori_loop(0, cols // tile, tile_step, 0)
 
-    values = rows_ref[...].astype(jnp.float32)
+    values = in_v[...].astype(jnp.float32)
     inv_rms = lax.rsqrt(jnp.mean(values * values, axis=1, keepdims=True) + EPSILON)
     unit_rows = values * inv_rms
     g_norm = acc[...]
@@ -767,14 +835,12 @@
         op.wait_send()
 
 
-def backward(rows_in, upstream, gain, loss_part, hidden, slope, w_in, o_in, w_out, o_out):
-    rows, width = rows_in.shape
+def backward(q_in, d_in, up, upt, gain, loss_part, hidden, slope, w_in, o_in, w_out, o_out):
+    rows, width = 2 * q_in.shape[0], q_in.shape[1]
     half = w_in.shape[1]
     cols = 2 * half // CHUNKS
     groups = NX * NY * NZ
     bf, f32 = jnp.bfloat16, jnp.float32
-    upt = upstream.T.reshape(groups, NC, GROUP, rows).transpose(1, 0, 2, 3)
-    upt = upt.reshape(NC, groups * GROUP, rows)
     vmem = pl.BlockSpec(memory_space=pltpu.VMEM)
     hbm = pl.BlockSpec(memory_space=pl.ANY)
     return pl.pallas_call(
@@ -784,9 +850,12 @@
             jax.ShapeDtypeStruct((8, width), f32),
             jax.ShapeDtypeStruct((rows, width), bf),
         ),
-        in_specs=[vmem] * 5 + [hbm] * 6,
+        in_specs=[hbm] * 4 + [vmem] * 2 + [hbm] * 6,
         out_specs=[vmem] * 3,
         scratch_shapes=[
+            pltpu.VMEM((rows, width), bf),
+            pltpu.VMEM((rows, width), bf),
+            pltpu.VMEM(upt.shape, bf),
             pltpu.VMEM((CHUNKS, rows, cols), bf),
             pltpu.VMEM((CHUNKS, rows, cols), bf),
             pltpu.VMEM((2,) + w_in.shape, bf),
@@ -801,7 +870,7 @@
             pltpu.VMEM((3, CHUNKS // 2, GROUP, cols), bf),
             pltpu.VMEM((rows, width), f32),
             pltpu.VMEM((14, 8, width), f32),
-            pltpu.SemaphoreType.DMA((2 * CHUNKS + 4,)),
+            pltpu.SemaphoreType.DMA((2 * CHUNKS + 9,)),
             pltpu.SemaphoreType.DMA((2, 7 * CHUNKS + 16)),
         ],
         compiler_params=pltpu.CompilerParams(
@@ -809,8 +878,9 @@
         ),
         name="backward",
     )(
-        rows_in,
-        upstream,
+        q_in,
+        d_in,
+        up,
         upt,
         gain.reshape(1, width),
         loss_part,
@@ -823,20 +893,44 @@
     )
 
 
+def finish_kernel(down, total, grads, down_out, gain_out, loss_out, q_out, d_out):
+    rows = q_out.shape[0]
+    down_out[...] = down[...]
+    gain_out[...] = total[0:1, :]
+    loss_out[...] = total[1:2, 0:1] * (1.0 / (rows * 2 * NBLK))
+    q_out[...] = grads[0:rows, :]
+    d_out[...] = grads[rows : 2 * rows, :]
+
+
+def finish(down, total, grads):
+    rows, width = grads.shape[0] // 2, grads.shape[1]
+    f32 = jnp.float32
+    row_grads = jax.ShapeDtypeStruct((rows, width), grads.dtype)
+    return pl.pallas_call(
+        finish_kernel,
+        out_shape=(
+            jax.ShapeDtypeStruct(down.shape, f32),
+            jax.ShapeDtypeStruct((1, width), f32),
+            jax.ShapeDtypeStruct((1, 1), f32),
+            row_grads,
+            row_grads,
+        ),
+        name="finish",
+    )(down, total, grads)
+
+
 def on_device(query_in, doc_in, cluster, gain, w_in, w_out):
     rows, width = query_in.shape
     queries, docs, hidden, slope, o_in, o_out = forward(query_in, doc_in, gain, w_in, w_out)
 
     tags = jnp.broadcast_to(cluster.astype(jnp.bfloat16)[None, :], (16, rows))
     column_tag = cluster.astype(jnp.float32)[:, None]
-    upstream, loss_part = band(docs, tags, queries, column_tag)
-
-    rows_in = jnp.concatenate([query_in, doc_in], axis=0)
-    down_t, total, grad_rows = backward(
-        rows_in, upstream, gain, loss_part, hidden, slope, w_in, o_in, w_out, o_out
+    up, upt, loss_part = band(docs, tags, queries, column_tag)
+    sums = backward(
+        query_in, doc_in, up, upt, gain, loss_part, hidden, slope, w_in, o_in, w_out, o_out
     )
-    loss = total[1, 0] / (rows * 2 * NBLK)
-    return (loss, down_t.T, total[0], grad_rows[:rows], grad_rows[rows:])
+    down_t, gain_total, loss, q_grads, d_grads = finish(*sums)
+    return (loss.reshape(()), down_t.T, gain_total.reshape(width), q_grads, d_grads)
 
 
 def solution(mesh):

time: 168 us -> 160 us (0.952)
  local copies, waits for them, and re-layouts: 11 us -> 1.4 us
  Pallas kernels: 152 us -> 156 us
  other arithmetic: 3.01 us -> 0.76 us
  between operations: 2.48 us -> 0.66 us
    slice x3 -> x0, local copies, waits for them, and re-layouts: 4.77 us -> none  [the longest x2 3.59 us: on_device(): return (loss, down_t.T, total[0], grad_rows[:rows], grad_rows[rows:])]
    unnamed x9 -> x0, local copies, waits for them, and re-layouts: 4.23 us -> none
    pallas_call x1, Pallas kernels: 57.7 us -> 60.4 us  [band(): pl.pallas_call(band_kernel, out_shape=(jax.ShapeDtypeStruct((2 * rows, wi...]
    pallas_call x0 -> x1, Pallas kernels: none -> 2.37 us  [finish(): pl.pallas_call(finish_kernel, out_shape=(jax.ShapeDtypeStruct(down.shape,...]
    concatenate x1 -> x0, other arithmetic: 2.25 us -> none  [on_device(): rows_in = jnp.concatenate([query_in, doc_in], axis=0)]
    transpose x2 -> x0, local copies, waits for them, and re-layouts: 1.82 us -> none  [backward(): upt = upstream.T.reshape(groups, NC, GROUP, rows).transpose(1, 0, 2, 3)]
where the time goes in v4:
time: 160 us; the launch traced here: 159 us
  Pallas kernels  156 us (98%)
    pallas_call x1, Pallas kernels, band(): pl.pallas_call(band_kernel, out_shape=(jax.ShapeDtypeStruct((2 * rows, wi...  60.4 us
    pallas_call x1, Pallas kernels, forward(): pl.pallas_call(forward_kernel, out_shape=(jax.ShapeDtypeStruct(q_in.shape...  47 us
    pallas_call x1, Pallas kernels, backward(): pl.pallas_call(backward_kernel, out_shape=(jax.ShapeDtypeStruct((GROUP, h...  46.7 us

profile of v4, /device:TPU:0, one launch (start us, length us, event | category | flops | bytes accessed | tf_op | source)
XLA Modules:
  0.0 159.2 jit_solution(1014330414989766375)
XLA Ops:
  0.6 0.8 fusion
  1.4 0.6 broadcast_in_dim.4.tags
  2.0 0.8 copy.11.column_tag
  2.8 47.0 %forward.1 = (bf16[256,1024]{1,0:T(8,128)(2,1)}, bf16[256,1024]{1,0:T(8,128)(2,1)}, bf16[4,512,1024]{2,1,0:T(8,128)(2,1)}, bf16[4,512,1024]{2,1,0:T(8,128)(2,1)}...) custom-call(bf16[256,1024]{1,0:T(8,128)(2,1)} %q_hbm.1, bf16[256,1024]{1,0:T(8,128)(2,1)} %d_hbm.1, ...), custom_call_target="tpu_custom_call" | custom-call | tf_op jit(solution)/shard_map/forward/pallas_call | solution.py:264
  49.8 60.4 %band.1 = (bf16[512,1024]{1,0:T(8,128)(2,1)}, bf16[2,2,512,256]{3,2,1,0:T(8,128)(2,1)}, f32[8,128]{1,0:T(8,128)}) custom-call(bf16[256,1024]{1,0:T(8,128)(2,1)} %get-tuple-element.22.docs, bf16[16,256]{1,0:T(8,128)(2,1)} %broadcast_in_dim.4.tags, bf16[256,1024]{1,0:T(8,128)(2,1)} %get-tuple-element.23.queries, f32[256,1]{1,0:T(8,128)} %copy.11.column_tag), custom_call_target="tpu_custom_call" | custom-call | tf_op jit(solution)/shard_map/band/pallas_call | solution.py:584
  110.2 46.7 %backward.1 = (f32[16,2048]{1,0:T(8,128)}, f32[8,1024]{1,0:T(8,128)}, bf16[512,1024]{1,0:T(8,128)(2,1)}) custom-call(bf16[256,1024]{1,0:T(8,128)(2,1)} %q_hbm.1, bf16[256,1024]{1,0:T(8,128)(2,1)} %d_hbm.1, bf16[512,1024]{1,0:T(8,128)(2,1)} %get-tuple-element.24.up_hbm, bf16[2,2,512,256]{3,2,1,0:T(8,128)(2,1)} %get-tuple-element.25.upt_hbm, ...), custom_call_target="tpu_custom_call" | custom-call | tf_op jit(solution)/shard_map/backward/pallas_call | solution.py:846
  156.9 2.4 %finish.1 = (f32[16,2048]{1,0:T(8,128)}, f32[1,1024]{1,0:T(1,128)}, f32[1,1]{1,0:T(1,128)}, bf16[256,1024]{1,0:T(8,128)(2,1)}, bf16[256,1024]{1,0:T(8,128)(2,1)}) custom-call(f32[16,2048]{1,0:T(8,128)} %get-tuple-element.31.down, f32[8,1024]{1,0:T(8,128)} %get-tuple-element.32.total, bf16[512,1024]{1,0:T(8,128)(2,1)} %get-tuple-element.33.grads), custom_call_target="tpu_custom_call" | custom-call | tf_op jit(solution)/shard_map/finish/pallas_call | solution.py:909

commit v5 on v4

--- a/solution.py
+++ b/solution.py
@@ -614,6 +614,15 @@
     )(docs, tags, queries, column_tag)
 
 
+PARTS = (
+    (0, 0, 768, "x"),
+    (0, 768, 768, "y"),
+    (0, 1536, 512, "z"),
+    (1, 0, 768, "x"),
+    (1, 768, 768, "y"),
+    (1, 1536, 512, "z"),
+)
+WIDE, NARROW = 768, 512
 CHUNKS = 4
 
 
@@ -648,6 +657,11 @@
     r3,
     a3,
     r4,
+    r2z,
+    a2z,
+    r3z,
+    a3z,
+    r4z,
     acc,
     s_buf,
     local,
@@ -657,6 +671,7 @@
     rows, width = q_hbm.shape
     half = win_hbm.shape[1]
     cols = 2 * half // CHUNKS
+    per_half = CHUNKS // 2
     sibling = device(x, y, zl, 1 - c, r)
     xs = [device(wrap(x + k, NX), y, zl, c, r) for k in range(1, RING)]
     ys = [device(x, wrap(y + k, NY), zl, c, r) for k in range(1, RING)]
@@ -676,7 +691,7 @@
     first_loads = [load(upt_hbm.at[k], upt_ref.at[k]) for k in range(2)]
     loads = []
     for j in range(CHUNKS):
-        load(hid_hbm.at[j], hid.at[j])
+        load(hid_hbm.at[j], hid.at[j // per_half, :, pl.ds(j % per_half * cols, cols)])
     for j in range(CHUNKS):
         load(slope_hbm.at[j], slope.at[j])
     for k, (inner, outer) in enumerate(((win_hbm, wout_hbm), (oin_hbm, oout_hbm))):
@@ -700,34 +715,48 @@
         ops.append(op)
         return op
 
-    def down_part(core, j):
-        return nn(upt_ref[0, core], hid[j, 0:rows, :]) + nn(upt_ref[1, core], hid[j, rows:, :])
+    def down_part(core, k, at):
+        return nn(upt_ref[0, core], hid[k, 0:rows, at]) + nn(upt_ref[1, core], hid[k, rows:, at])
 
     wait1 = []
-    for j in range(CHUNKS):
-        loads[j].wait()
-        if j == 0:
-            for op in first_loads:
-                op.wait()
-        s1[j] = down_part(1 - c, j).astype(jnp.bfloat16)
-        wait1.append(send(s1.at[j], r1.at[j], sibling))
+    for op in first_loads:
+        op.wait()
+    n_loaded = 0
+    for k, first, count, _ in PARTS:
+        at = slice(first, first + count)
+        while n_loaded * cols < k * half + first + count:
+            loads[n_loaded].wait()
+            n_loaded += 1
+        s1[k, :, at] = down_part(1 - c, k, at).astype(jnp.bfloat16)
+        view = (k, slice(None), pl.ds(first, count))
+        wait1.append(send(s1.at[view], r1.at[view], sibling))
 
     wait2 = []
-    for j in range(CHUNKS):
-        mine = down_part(c, j)
-        wait1[j].wait_recv()
-        mine = mine + r1[j].astype(jnp.float32)
-        a1[j] = mine.astype(jnp.bfloat16).reshape(NX, NY, NZ, GROUP, cols)
+    waitz = []
+    for p, (k, first, count, axis) in enumerate(PARTS):
+        at = slice(first, first + count)
+        mine = down_part(c, k, at)
+        wait1[p].wait_recv()
+        mine = mine + r1[k, :, at].astype(jnp.float32)
+        a1[k, :, :, :, :, at] = mine.astype(jnp.bfloat16).reshape(NX, NY, NZ, GROUP, count)
+        part = pl.ds(first, count)
         waits = []
-        for k in range(1, RING):
-            slot = RING - 1 - k
-            if j % 2 == 0:
-                waits.append(send(a1.at[j, wrap(x + k, NX)], r2.at[j, slot], xs[k - 1]))
+        if axis == "z":
+            if k == 0:
+                waitz.append(send(a1.at[k, :, :, 1 - zl, :, part], r2z.at[0], zs[0]))
             else:
-                waits.append(send(a1.at[j, :, wrap(y + k, NY)], r2.at[j, slot], ys[k - 1]))
+                waitz.append(send(a1.at[k, :, :, zl, :, part], r2z.at[1], zs[1]))
+                waitz.append(send(a1.at[k, :, :, 1 - zl, :, part], r2z.at[2], zs[2]))
+        for n in range(1, RING):
+            slot = RING - 1 - n
+            if axis == "x":
+                src = a1.at[k, wrap(x + n, NX), :, :, :, part]
+                waits.append(send(src, r2.at[k, 0, slot], xs[n - 1]))
+            elif axis == "y":
+                src = a1.at[k, :, wrap(y + n, NY), :, :, part]
+                waits.append(send(src, r2.at[k, 1, slot], ys[n - 1]))
         wait2.append(waits)
 
-    per_half = CHUNKS // 2
     for j in range(CHUNKS):
         loads[CHUNKS + j].wait()
     for k in range(2):
@@ -780,27 +809,60 @@
     s_buf[x] = s_buf[12] + s_buf[13]
     small = [send(s_buf.at[x], s_buf.at[x], peer) for peer in xs]
 
-    wait3 = []
-    for j in range(CHUNKS):
-        for op in wait2[j]:
+    wait3 = {}
+
+    def second(p):
+        k, first, count, axis = PARTS[p]
+        at = slice(first, first + count)
+        i = 0 if axis == "x" else 1
+        for op in wait2[p]:
             op.wait_recv()
-        tot = (a1[j, x] if j % 2 == 0 else a1[j, :, y]).astype(jnp.float32)
-        for k in range(RING - 1):
-            tot = tot + r2[j, k].astype(jnp.float32)
-        a2[j] = tot.astype(jnp.bfloat16)
-        waits = []
-        for k in range(1, RING):
-            slot = RING - 1 - k
-            if j % 2 == 0:
-                waits.append(send(a2.at[j, wrap(y + k, NY)], r3.at[j, slot], ys[k - 1]))
+        tot = (a1[k, x, :, :, :, at] if i == 0 else a1[k, :, y, :, :, at]).astype(jnp.float32)
+        for n in range(RING - 1):
+            tot = tot + r2[k, i, n].astype(jnp.float32)
+        a2[k, i] = tot.astype(jnp.bfloat16)
+        wait3[p] = []
+        for n in range(1, RING):
+            slot = RING - 1 - n
+            if i == 0:
+                op = send(a2.at[k, i, wrap(y + n, NY)], r3.at[k, i, slot], ys[n - 1])
             else:
-                waits.append(send(a2.at[j, wrap(x + k, NX)], r3.at[j, slot], xs[k - 1]))
-        wait3.append(waits)
-        if j == 1:
-            for op in small:
-                op.wait_recv()
-            s_buf[4 + y] = ((s_buf[0] + s_buf[1]) + s_buf[2]) + s_buf[3]
-            small = [send(s_buf.at[4 + y], s_buf.at[4 + y], peer) for peer in ys]
+                op = send(a2.at[k, i, wrap(x + n, NX)], r3.at[k, i, slot], xs[n - 1])
+            wait3[p].append(op)
+
+    def second_z():
+        k, first, count, _ = PARTS[2]
+        for op in waitz:
+            op.wait_recv()
+        tot = a1[k, :, :, zl, :, first : first + count].astype(jnp.float32)
+        for n in range(RING - 1):
+            tot = tot + r2z[n].astype(jnp.float32)
+        a2z[...] = tot.astype(jnp.bfloat16)
+        return [
+            send(a2z.at[wrap(x + n, NX)], r3z.at[RING - 1 - n], xs[n - 1]) for n in range(1, RING)
+        ]
+
+    def third_z(waits):
+        for op in waits:
+            op.wait_recv()
+        tot = a2z[x].astype(jnp.float32)
+        for n in range(RING - 1):
+            tot = tot + r3z[n].astype(jnp.float32)
+        a3z[...] = tot.astype(jnp.bfloat16)
+        return [
+            send(a3z.at[wrap(y + n, NY)], r4z.at[RING - 1 - n], ys[n - 1]) for n in range(1, RING)
+        ]
+
+    second(0)
+    second(1)
+    for op in small:
+        op.wait_recv()
+    s_buf[4 + y] = ((s_buf[0] + s_buf[1]) + s_buf[2]) + s_buf[3]
+    small = [send(s_buf.at[4 + y], s_buf.at[4 + y], peer) for peer in ys]
+    waitz = second_z()
+    second(3)
+    second(4)
+    waitz = third_z(waitz)
 
     for op in small:
         op.wait_recv()
@@ -808,26 +870,34 @@
     here[...] = ((s_buf[4] + s_buf[5]) + s_buf[6]) + s_buf[7]
     small = [send(here, here, peer) for peer in zs]
 
-    wait4 = []
-    for j in range(CHUNKS):
-        for op in wait3[j]:
+    wait4 = [[], []]
+    for p in (0, 1, 3, 4):
+        k, first, count, axis = PARTS[p]
+        i = 0 if axis == "x" else 1
+        for op in wait3[p]:
             op.wait_recv()
-        tot = (a2[j, y] if j % 2 == 0 else a2[j, x]).astype(jnp.float32)
-        for k in range(RING - 1):
-            tot = tot + r3[j, k].astype(jnp.float32)
-        a3[j] = tot.astype(jnp.bfloat16)
-        if j < per_half:
-            wait4.append([send(a3.at[j, 1 - zl], r4.at[0, j], zs[0])])
+        tot = (a2[k, i, y] if i == 0 else a2[k, i, x]).astype(jnp.float32)
+        for n in range(RING - 1):
+            tot = tot + r3[k, i, n].astype(jnp.float32)
+        a3[k, i] = tot.astype(jnp.bfloat16)
+        if k == 0:
+            wait4[i].append(send(a3.at[k, i, 1 - zl], r4.at[i, 0], zs[0]))
         else:
-            i = j - per_half
-            wait4[i].append(send(a3.at[j, zl], r4.at[1, i], zs[1]))
-            wait4[i].append(send(a3.at[j, 1 - zl], r4.at[2, i], zs[2]))
-    for i in range(per_half):
+            wait4[i].append(send(a3.at[k, i, zl], r4.at[i, 1], zs[1]))
+            wait4[i].append(send(a3.at[k, i, 1 - zl], r4.at[i, 2], zs[2]))
+    for op in waitz:
+        op.wait_recv()
+    first = PARTS[2][1]
+    tot = a3z[y].astype(jnp.float32)
+    for n in range(RING - 1):
+        tot = tot + r4z[n].astype(jnp.float32)
+    out[:, first : first + NARROW] = tot
+    for i in range(2):
         for op in wait4[i]:
             op.wait_recv()
-        out[:, i * cols : (i + 1) * cols] = (
-            a3[i, zl].astype(jnp.float32) + r4[0, i].astype(jnp.float32)
-        ) + (r4[1, i].astype(jnp.float32) + r4[2, i].astype(jnp.float32))
+        out[:, i * WIDE : (i + 1) * WIDE] = (
+            a3[0, i, zl].astype(jnp.float32) + r4[i, 0].astype(jnp.float32)
+        ) + (r4[i, 1].astype(jnp.float32) + r4[i, 2].astype(jnp.float32))
     for op in small:
         op.wait_recv()
     total[...] = (s_buf[8] + s_buf[9]) + (s_buf[10] + s_buf[11])
@@ -856,22 +926,27 @@
             pltpu.VMEM((rows, width), bf),
             pltpu.VMEM((rows, width), bf),
             pltpu.VMEM(upt.shape, bf),
-            pltpu.VMEM((CHUNKS, rows, cols), bf),
+            pltpu.VMEM((2, rows, half), bf),
             pltpu.VMEM((CHUNKS, rows, cols), bf),
             pltpu.VMEM((2,) + w_in.shape, bf),
             pltpu.VMEM((2,) + w_out.shape, bf),
-            pltpu.VMEM((CHUNKS, groups * GROUP, cols), bf),
-            pltpu.VMEM((CHUNKS, groups * GROUP, cols), bf),
-            pltpu.VMEM((CHUNKS, NX, NY, NZ, GROUP, cols), bf),
-            pltpu.VMEM((CHUNKS, RING - 1, RING, NZ, GROUP, cols), bf),
-            pltpu.VMEM((CHUNKS, RING, NZ, GROUP, cols), bf),
-            pltpu.VMEM((CHUNKS, RING - 1, NZ, GROUP, cols), bf),
-            pltpu.VMEM((CHUNKS, NZ, GROUP, cols), bf),
-            pltpu.VMEM((3, CHUNKS // 2, GROUP, cols), bf),
+            pltpu.VMEM((2, groups * GROUP, half), bf),
+            pltpu.VMEM((2, groups * GROUP, half), bf),
+            pltpu.VMEM((2, NX, NY, NZ, GROUP, half), bf),
+            pltpu.VMEM((2, 2, RING - 1, RING, NZ, GROUP, WIDE), bf),
+            pltpu.VMEM((2, 2, RING, NZ, GROUP, WIDE), bf),
+            pltpu.VMEM((2, 2, RING - 1, NZ, GROUP, WIDE), bf),
+            pltpu.VMEM((2, 2, NZ, GROUP, WIDE), bf),
+            pltpu.VMEM((2, RING - 1, GROUP, WIDE), bf),
+            pltpu.VMEM((RING - 1, NX, NY, GROUP, NARROW), bf),
+            pltpu.VMEM((NX, NY, GROUP, NARROW), bf),
+            pltpu.VMEM((RING - 1, NY, GROUP, NARROW), bf),
+            pltpu.VMEM((NY, GROUP, NARROW), bf),
+            pltpu.VMEM((RING - 1, GROUP, NARROW), bf),
             pltpu.VMEM((rows, width), f32),
             pltpu.VMEM((14, 8, width), f32),
             pltpu.SemaphoreType.DMA((2 * CHUNKS + 9,)),
-            pltpu.SemaphoreType.DMA((2, 7 * CHUNKS + 16)),
+            pltpu.SemaphoreType.DMA((2, 64)),
         ],
         compiler_params=pltpu.CompilerParams(
             collective_id=3, has_side_effects=True, vmem_limit_bytes=60 * MIB

time: 160 us -> 156 us (0.975)
  Pallas kernels: 156 us -> 153 us
    pallas_call x1, Pallas kernels: 46.7 us -> 43 us  [backward(): pl.pallas_call(backward_kernel, out_shape=(jax.ShapeDtypeStruct((GROUP, h...]
where the time goes in v5:
time: 156 us
  Pallas kernels  153 us (98%)
    pallas_call x1, Pallas kernels, band(): pl.pallas_call(band_kernel, out_shape=(jax.ShapeDtypeStruct((2 * rows, wi...  60.4 us
    pallas_call x1, Pallas kernels, forward(): pl.pallas_call(forward_kernel, out_shape=(jax.ShapeDtypeStruct(q_in.shape...  47 us
    pallas_call x1, Pallas kernels, backward(): pl.pallas_call(backward_kernel, out_shape=(jax.ShapeDtypeStruct((GROUP, h...  43 us

profile of v5, /device:TPU:0, one launch (start us, length us, event | category | flops | bytes accessed | tf_op | source)
XLA Modules:
  0.0 155.5 jit_solution(13995364015477544142)
XLA Ops:
  0.6 0.8 fusion
  1.4 0.6 broadcast_in_dim.4.tags
  2.0 0.8 copy.11.column_tag
  2.8 47.0 %forward.1 = (bf16[256,1024]{1,0:T(8,128)(2,1)}, bf16[256,1024]{1,0:T(8,128)(2,1)}, bf16[4,512,1024]{2,1,0:T(8,128)(2,1)}, bf16[4,512,1024]{2,1,0:T(8,128)(2,1)}...) custom-call(bf16[256,1024]{1,0:T(8,128)(2,1)} %q_hbm.1, bf16[256,1024]{1,0:T(8,128)(2,1)} %d_hbm.1, ...), custom_call_target="tpu_custom_call" | custom-call | tf_op jit(solution)/shard_map/forward/pallas_call | solution.py:264
  49.8 60.4 %band.1 = (bf16[512,1024]{1,0:T(8,128)(2,1)}, bf16[2,2,512,256]{3,2,1,0:T(8,128)(2,1)}, f32[8,128]{1,0:T(8,128)}) custom-call(bf16[256,1024]{1,0:T(8,128)(2,1)} %get-tuple-element.22.docs, bf16[16,256]{1,0:T(8,128)(2,1)} %broadcast_in_dim.4.tags, bf16[256,1024]{1,0:T(8,128)(2,1)} %get-tuple-element.23.queries, f32[256,1]{1,0:T(8,128)} %copy.11.column_tag), custom_call_target="tpu_custom_call" | custom-call | tf_op jit(solution)/shard_map/band/pallas_call | solution.py:584
  110.2 43.0 %backward.1 = (f32[16,2048]{1,0:T(8,128)}, f32[8,1024]{1,0:T(8,128)}, bf16[512,1024]{1,0:T(8,128)(2,1)}) custom-call(bf16[256,1024]{1,0:T(8,128)(2,1)} %q_hbm.1, bf16[256,1024]{1,0:T(8,128)(2,1)} %d_hbm.1, bf16[512,1024]{1,0:T(8,128)(2,1)} %get-tuple-element.24.up_hbm, bf16[2,2,512,256]{3,2,1,0:T(8,128)(2,1)} %get-tuple-element.25.upt_hbm, ...), custom_call_target="tpu_custom_call" | custom-call | tf_op jit(solution)/shard_map/backward/pallas_call | solution.py:916
  153.1 2.4 %finish.1 = (f32[16,2048]{1,0:T(8,128)}, f32[1,1024]{1,0:T(1,128)}, f32[1,1]{1,0:T(1,128)}, bf16[256,1024]{1,0:T(8,128)(2,1)}, bf16[256,1024]{1,0:T(8,128)(2,1)}) custom-call(f32[16,2048]{1,0:T(8,128)} %get-tuple-element.31.down, f32[8,1024]{1,0:T(8,128)} %get-tuple-element.32.total, bf16[512,1024]{1,0:T(8,128)(2,1)} %get-tuple-element.33.grads), custom_call_target="tpu_custom_call" | custom-call | tf_op jit(solution)/shard_map/finish/pallas_call | solution.py:984

commit v6 on v5

--- a/solution.py
+++ b/solution.py
@@ -83,14 +83,12 @@
     return out_ref.at[pl.ds(pl.multiple_of(first, rows), rows)]
 
 
-def forward_kernel(
+def forward_part(
     q_in,
     d_in,
     gain_ref,
     win_hbm,
     wout_hbm,
-    q_emb,
-    d_emb,
     hid_hbm,
     slope_hbm,
     oin_hbm,
@@ -108,6 +106,7 @@
     stores,
     send,
     recv,
+    meet,
 ):
     x, y, zl, c, r = coords()
     cross = device(x, y, 1 - zl, c, 1 - r)
@@ -121,7 +120,7 @@
     load_out = pltpu.make_async_copy(wout_hbm, wout, local.at[1])
     load_in.start()
     load_out.start()
-    greet([cross, near, ahead, behind, sibling])
+    meet([ahead, behind])
     color = lax.rem(x + 2 * zl, 4)
     started = []
 
@@ -241,58 +240,18 @@
     second_hop(7)
     down_own(2)
     down_own(3)
-    for shift in (0, 3, 1, 2):
+    for shift in (0, 3, 1):
         down_other(shift)
-    for k, (ref, emb) in enumerate(((q_in, q_emb), (d_in, d_emb))):
-        emb[...] = (ref[...].astype(jnp.float32) + acc[k * rows : (k + 1) * rows, :]).astype(
-            jnp.bfloat16
-        )
-    for op in started:
-        op.wait_send()
-    for op in stored:
-        op.wait()
-
-
-def forward(q_in, d_in, gain, w_in, w_out):
-    rows, width = q_in.shape
-    half = w_in.shape[1]
-    bf, f32 = jnp.bfloat16, jnp.float32
-    tile = 2 * WBLK
-    vmem = pl.BlockSpec(memory_space=pltpu.VMEM)
-    hbm = pl.BlockSpec(memory_space=pl.ANY)
-    per_chunk = jax.ShapeDtypeStruct((CHUNKS, 2 * rows, 2 * half // CHUNKS), bf)
-    return pl.pallas_call(
-        forward_kernel,
-        out_shape=(
-            jax.ShapeDtypeStruct(q_in.shape, bf),
-            jax.ShapeDtypeStruct(d_in.shape, bf),
-            per_chunk,
-            per_chunk,
-            jax.ShapeDtypeStruct(w_in.shape, bf),
-            jax.ShapeDtypeStruct(w_out.shape, bf),
-        ),
-        in_specs=[vmem] * 3 + [hbm] * 2,
-        out_specs=[vmem] * 2 + [hbm] * 4,
-        scratch_shapes=[
-            pltpu.VMEM(w_in.shape, bf),
-            pltpu.VMEM(w_out.shape, bf),
-            pltpu.VMEM(w_in.shape, bf),
-            pltpu.VMEM(w_out.shape, bf),
-            pltpu.VMEM((2 * rows, width), bf),
-            pltpu.VMEM((2 * half // tile, 2 * rows, tile), bf),
-            pltpu.VMEM((2 * half // tile, 2 * rows, tile), bf),
-            pltpu.VMEM((2 * rows, tile), f32),
-            pltpu.VMEM((2 * rows, width), f32),
-            pltpu.SemaphoreType.DMA((2,)),
-            pltpu.SemaphoreType.DMA((2 * 2 * half // tile + 8,)),
-            pltpu.SemaphoreType.DMA((8, W_CHUNKS)),
-            pltpu.SemaphoreType.DMA((8, W_CHUNKS)),
-        ],
-        compiler_params=pltpu.CompilerParams(
-            collective_id=0, has_side_effects=True, vmem_limit_bytes=56 * MIB
-        ),
-        name="forward",
-    )(q_in, d_in, gain.reshape(1, width), w_in, w_out)
+    from_sibling(2, range(W_CHUNKS // 2, W_CHUNKS))
+    last = pl.ds(pl.multiple_of(color_at(2) * tile, tile), tile)
+    store(oout.at[last, :], oout_hbm.at[last, :])
+
+    def embed(k):
+        at = slice(k * rows, (k + 1) * rows)
+        mixed = acc[at, :] + nn(hid[half // tile + color_at(2), at, :], oout[last, :])
+        return ((q_in, d_in)[k][...].astype(jnp.float32) + mixed).astype(jnp.bfloat16)
+
+    return embed, started, stored
 
 
 PIECES = (
@@ -311,10 +270,49 @@
 DETOUR_ROWS = 48
 
 
-def band_kernel(
-    docs,
+def layer_kernel(*refs):
+    ins, outs, scratch = refs[:7], refs[7:14], refs[14:]
+    q_in, d_in, gain_ref, tags, column_tag, win_hbm, wout_hbm = ins
+    up, upt, loss, hid_hbm, slope_hbm, oin_hbm, oout_hbm = outs
+    forward_scratch, band_scratch = scratch[:13], scratch[13:]
+    b = lax.axis_index("blk")
+    zl = coords()[2]
+    r = lax.axis_index("rep")
+    step = NZ * NC * (1 - 2 * zl)
+    onward = {"blk": wrap(b + step, NBLK), "rep": r}
+    source = {"blk": wrap(b - step, NBLK), "rep": r}
+    peers = []
+    for offset in range(-2, 3):
+        for other in range(2):
+            if offset or other:
+                rep = 1 - r if other else r
+                peers.append((offset, other, {"blk": wrap(b + offset, NBLK), "rep": rep}))
+
+    def meet(more):
+        greet([peer for _, _, peer in peers] + [onward, source] + more)
+
+    embed, started, stored = forward_part(
+        q_in,
+        d_in,
+        gain_ref,
+        win_hbm,
+        wout_hbm,
+        hid_hbm,
+        slope_hbm,
+        oin_hbm,
+        oout_hbm,
+        *forward_scratch,
+        meet,
+    )
+    band_part(tags, column_tag, up, upt, loss, *band_scratch, embed, peers, onward, source)
+    for op in started:
+        op.wait_send()
+    for op in stored:
+        op.wait()
+
+
+def band_part(
     tags,
-    queries,
     column_tag,
     up,
     upt,
@@ -334,36 +332,24 @@
     send,
     recv,
     tsem,
+    embed,
+    peers,
+    onward,
+    source,
 ):
     x, y, zl, c, r = coords()
-    b = lax.axis_index("blk")
-    rows, width = docs.shape
+    rows, width = gd.shape[1:]
     inv_root = 1.0 / math.sqrt(width)
     cross = device(x, y, 1 - zl, c, 1 - r)
     near = device(x, y, 1 - zl, c, r)
     sibling = device(x, y, zl, 1 - c, r)
-    step = NZ * NC * (1 - 2 * zl)
-    onward = {"blk": wrap(b + step, NBLK), "rep": r}
-    source = {"blk": wrap(b - step, NBLK), "rep": r}
-    peers = []
-    for offset in range(-2, 3):
-        for other in range(2):
-            if offset or other:
-                rep = 1 - r if other else r
-                peers.append((offset, other, {"blk": wrap(b + offset, NBLK), "rep": rep}))
-    own_docs = pltpu.make_async_copy(docs, gd.at[OWN], local.at[0])
-    own_queries = pltpu.make_async_copy(queries, gq.at[OWN], local.at[1])
-    own_docs.start()
-    own_queries.start()
-    greet([peer for _, _, peer in peers] + [onward, source])
 
     def view(slot, p):
         kind, first, count = PIECES[p][:3]
         return (gd, gx, gq)[kind].at[slot, pl.ds(first, count)]
 
     def own(p):
-        kind, first, count = PIECES[p][:3]
-        return (docs, tags, queries)[kind].at[pl.ds(first, count)]
+        return view(OWN, p)
 
     z_slot = 8 - 8 * zl
     far_slot = 8 * zl
@@ -449,8 +435,8 @@
         for core in range(NC):
             upt_v[k, core] = turned[:, core].reshape(width // NC, rows)
         ops = [
-            pltpu.make_async_copy(up_v.at[k], up.at[pl.ds(k * rows, rows)], local.at[2 + 2 * k]),
-            pltpu.make_async_copy(upt_v.at[k], upt.at[k], local.at[3 + 2 * k]),
+            pltpu.make_async_copy(up_v.at[k], up.at[pl.ds(k * rows, rows)], local.at[2 * k]),
+            pltpu.make_async_copy(upt_v.at[k], upt.at[k], local.at[1 + 2 * k]),
         ]
         for op in ops:
             op.start()
@@ -478,11 +464,11 @@
             wt = wt - diagonal.astype(jnp.float32)
         acc[...] += nn(wt.astype(jnp.bfloat16), gq[slot])
 
+    gx[OWN] = tags[...]
+    gd[OWN] = embed(1)
     for p in DOC_PIECES:
         send_own(p)
-    gx[OWN] = tags[...]
-    own_docs.wait()
-    own_queries.wait()
+    gq[OWN] = embed(0)
     for p in DOC_PIECES:
         from_z(p)
     for p in QUERY_PIECES:
@@ -576,21 +562,41 @@
         op.wait()
 
 
-def band(docs, tags, queries, column_tag):
-    rows, width = docs.shape
+def layer(q_in, d_in, gain, tags, column_tag, w_in, w_out):
+    rows, width = q_in.shape
+    half = w_in.shape[1]
     bf, f32 = jnp.bfloat16, jnp.float32
+    tile = 2 * WBLK
     vmem = pl.BlockSpec(memory_space=pltpu.VMEM)
     hbm = pl.BlockSpec(memory_space=pl.ANY)
+    per_chunk = jax.ShapeDtypeStruct((CHUNKS, 2 * rows, 2 * half // CHUNKS), bf)
     return pl.pallas_call(
-        band_kernel,
+        layer_kernel,
         out_shape=(
             jax.ShapeDtypeStruct((2 * rows, width), bf),
             jax.ShapeDtypeStruct((2, NC, width // NC, rows), bf),
             jax.ShapeDtypeStruct((8, 128), f32),
+            per_chunk,
+            per_chunk,
+            jax.ShapeDtypeStruct(w_in.shape, bf),
+            jax.ShapeDtypeStruct(w_out.shape, bf),
         ),
-        in_specs=[hbm, vmem, hbm, vmem],
-        out_specs=[hbm, hbm, vmem],
+        in_specs=[vmem] * 5 + [hbm] * 2,
+        out_specs=[hbm, hbm, vmem] + [hbm] * 4,
         scratch_shapes=[
+            pltpu.VMEM(w_in.shape, bf),
+            pltpu.VMEM(w_out.shape, bf),
+            pltpu.VMEM(w_in.shape, bf),
+            pltpu.VMEM(w_out.shape, bf),
+            pltpu.VMEM((2 * rows, width), bf),
+            pltpu.VMEM((2 * half // tile, 2 * rows, tile), bf),
+            pltpu.VMEM((2 * half // tile, 2 * rows, tile), bf),
+            pltpu.VMEM((2 * rows, tile), f32),
+            pltpu.VMEM((2 * rows, width), f32),
+            pltpu.SemaphoreType.DMA((2,)),
+            pltpu.SemaphoreType.DMA((2 * 2 * half // tile + 8,)),
+            pltpu.SemaphoreType.DMA((8, W_CHUNKS)),
+            pltpu.SemaphoreType.DMA((8, W_CHUNKS)),
             pltpu.VMEM((SLOTS, rows, width), bf),
             pltpu.VMEM((SLOTS,) + tags.shape, bf),
             pltpu.VMEM((SLOTS, rows, width), bf),
@@ -602,16 +608,16 @@
             pltpu.VMEM((rows, width), f32),
             pltpu.VMEM((2, rows, width), bf),
             pltpu.VMEM((2, NC, width // NC, rows), bf),
-            pltpu.SemaphoreType.DMA((6,)),
+            pltpu.SemaphoreType.DMA((4,)),
             pltpu.SemaphoreType.DMA((12, len(PIECES))),
             pltpu.SemaphoreType.DMA((12, len(PIECES))),
             pltpu.SemaphoreType.DMA((2, SLOTS)),
         ],
         compiler_params=pltpu.CompilerParams(
-            collective_id=1, has_side_effects=True, vmem_limit_bytes=60 * MIB
+            collective_id=0, has_side_effects=True, vmem_limit_bytes=60 * MIB
         ),
-        name="band",
-    )(docs, tags, queries, column_tag)
+        name="layer",
+    )(q_in, d_in, gain.reshape(1, width), tags, column_tag, w_in, w_out)
 
 
 PARTS = (
@@ -996,11 +1002,11 @@
 
 def on_device(query_in, doc_in, cluster, gain, w_in, w_out):
     rows, width = query_in.shape
-    queries, docs, hidden, slope, o_in, o_out = forward(query_in, doc_in, gain, w_in, w_out)
-
     tags = jnp.broadcast_to(cluster.astype(jnp.bfloat16)[None, :], (16, rows))
     column_tag = cluster.astype(jnp.float32)[:, None]
-    up, upt, loss_part = band(docs, tags, queries, column_tag)
+    up, upt, loss_part, hidden, slope, o_in, o_out = layer(
+        query_in, doc_in, gain, tags, column_tag, w_in, w_out
+    )
     sums = backward(
         query_in, doc_in, up, upt, gain, loss_part, hidden, slope, w_in, o_in, w_out, o_out
     )

time: 156 us -> 150 us (0.962)
  Pallas kernels: 153 us -> 147 us
    pallas_call x2 -> x1, Pallas kernels: 107 us -> 100 us  [layer(): pl.pallas_call(layer_kernel, out_shape=(jax.ShapeDtypeStruct((2 * rows, w...]
where the time goes in v6:
time: 150 us
  Pallas kernels  147 us (98%)
    pallas_call x1, Pallas kernels, layer(): pl.pallas_call(layer_kernel, out_shape=(jax.ShapeDtypeStruct((2 * rows, w...  100 us
    pallas_call x1, Pallas kernels, backward(): pl.pallas_call(backward_kernel, out_shape=(jax.ShapeDtypeStruct((GROUP, h...  44.1 us

profile of v6, /device:TPU:0, one launch (start us, length us, event | category | flops | bytes accessed | tf_op | source)
XLA Modules:
  0.0 149.6 jit_solution(4712975584830358750)
XLA Ops:
  0.6 0.8 fusion
  1.4 0.6 broadcast_in_dim.4.refs_3_
  2.0 0.8 copy.11.refs_4_
  2.8 100.4 %layer.1 = (bf16[512,1024]{1,0:T(8,128)(2,1)}, bf16[2,2,512,256]{3,2,1,0:T(8,128)(2,1)}, f32[8,128]{1,0:T(8,128)}, bf16[4,512,1024]{2,1,0:T(8,128)(2,1)}, bf16[4...) custom-call(bf16[256,1024]{1,0:T(8,128)(2,1)} %q_hbm.1, bf16[256,1024]{1,0:T(8,128)(2,1)} %d_hbm.1, ...), custom_call_target="tpu_custom_call" | custom-call | tf_op jit(solution)/shard_map/layer/pallas_call | solution.py:573
  103.2 44.1 %backward.1 = (f32[16,2048]{1,0:T(8,128)}, f32[8,1024]{1,0:T(8,128)}, bf16[512,1024]{1,0:T(8,128)(2,1)}) custom-call(bf16[256,1024]{1,0:T(8,128)(2,1)} %q_hbm.1, bf16[256,1024]{1,0:T(8,128)(2,1)} %d_hbm.1, bf16[512,1024]{1,0:T(8,128)(2,1)} %get-tuple-element.20.up_hbm, bf16[2,2,512,256]{3,2,1,0:T(8,128)(2,1)} %get-tuple-element.21.upt_hbm, ...), custom_call_target="tpu_custom_call" | custom-call | tf_op jit(solution)/shard_map/backward/pallas_call | solution.py:922
  147.3 2.4 %finish.1 = (f32[16,2048]{1,0:T(8,128)}, f32[1,1024]{1,0:T(1,128)}, f32[1,1]{1,0:T(1,128)}, bf16[256,1024]{1,0:T(8,128)(2,1)}, bf16[256,1024]{1,0:T(8,128)(2,1)}) custom-call(f32[16,2048]{1,0:T(8,128)} %get-tuple-element.27.down, f32[8,1024]{1,0:T(8,128)} %get-tuple-element.28.total, bf16[512,1024]{1,0:T(8,128)(2,1)} %get-tuple-element.29.grads), custom_call_target="tpu_custom_call" | custom-call | tf_op jit(solution)/shard_map/finish/pallas_call | solution.py:990

commit v7 on v6

--- a/solution.py
+++ b/solution.py
@@ -271,8 +271,8 @@
 
 
 def layer_kernel(*refs):
-    ins, outs, scratch = refs[:7], refs[7:14], refs[14:]
-    q_in, d_in, gain_ref, tags, column_tag, win_hbm, wout_hbm = ins
+    ins, outs, scratch = refs[:6], refs[6:13], refs[13:]
+    q_in, d_in, gain_ref, cluster, win_hbm, wout_hbm = ins
     up, upt, loss, hid_hbm, slope_hbm, oin_hbm, oout_hbm = outs
     forward_scratch, band_scratch = scratch[:13], scratch[13:]
     b = lax.axis_index("blk")
@@ -304,7 +304,7 @@
         *forward_scratch,
         meet,
     )
-    band_part(tags, column_tag, up, upt, loss, *band_scratch, embed, peers, onward, source)
+    band_part(cluster, up, upt, loss, *band_scratch, embed, peers, onward, source)
     for op in started:
         op.wait_send()
     for op in stored:
@@ -312,8 +312,7 @@
 
 
 def band_part(
-    tags,
-    column_tag,
+    cluster,
     up,
     upt,
     loss,
@@ -326,6 +325,7 @@
     lt,
     mine,
     acc,
+    column_tag,
     up_v,
     upt_v,
     local,
@@ -339,6 +339,8 @@
 ):
     x, y, zl, c, r = coords()
     rows, width = gd.shape[1:]
+    tag = cluster[...].astype(jnp.float32)
+    column_tag[...] = jnp.transpose(jnp.broadcast_to(tag, (128, rows)))
     inv_root = 1.0 / math.sqrt(width)
     cross = device(x, y, 1 - zl, c, 1 - r)
     near = device(x, y, 1 - zl, c, r)
@@ -449,7 +451,7 @@
     def masked(a, g, slot):
         scores = nt(a[OWN], g[slot]) * inv_root
         tag_row = gx[slot].astype(jnp.float32)[0:1, :]
-        allowed = tag_row != column_tag[...]
+        allowed = tag_row != column_tag[:, 0:1]
         if isinstance(slot, int) and slot == OWN:
             allowed = allowed | diagonal
         return scores, jnp.where(allowed, scores, -jnp.inf)
@@ -464,7 +466,7 @@
             wt = wt - diagonal.astype(jnp.float32)
         acc[...] += nn(wt.astype(jnp.bfloat16), gq[slot])
 
-    gx[OWN] = tags[...]
+    gx[OWN] = jnp.broadcast_to(tag, gx.shape[1:]).astype(jnp.bfloat16)
     gd[OWN] = embed(1)
     for p in DOC_PIECES:
         send_own(p)
@@ -562,7 +564,7 @@
         op.wait()
 
 
-def layer(q_in, d_in, gain, tags, column_tag, w_in, w_out):
+def layer(q_in, d_in, gain, cluster, w_in, w_out):
     rows, width = q_in.shape
     half = w_in.shape[1]
     bf, f32 = jnp.bfloat16, jnp.float32
@@ -581,7 +583,7 @@
             jax.ShapeDtypeStruct(w_in.shape, bf),
             jax.ShapeDtypeStruct(w_out.shape, bf),
         ),
-        in_specs=[vmem] * 5 + [hbm] * 2,
+        in_specs=[vmem] * 4 + [hbm] * 2,
         out_specs=[hbm, hbm, vmem] + [hbm] * 4,
         scratch_shapes=[
             pltpu.VMEM(w_in.shape, bf),
@@ -598,7 +600,7 @@
             pltpu.SemaphoreType.DMA((8, W_CHUNKS)),
             pltpu.SemaphoreType.DMA((8, W_CHUNKS)),
             pltpu.VMEM((SLOTS, rows, width), bf),
-            pltpu.VMEM((SLOTS,) + tags.shape, bf),
+            pltpu.VMEM((SLOTS, 16, rows), bf),
             pltpu.VMEM((SLOTS, rows, width), bf),
             pltpu.VMEM((2, DETOUR_ROWS, width), bf),
             pltpu.VMEM((SLOTS, rows, rows), f32),
@@ -606,6 +608,7 @@
             pltpu.VMEM((SLOTS, 8, rows), f32),
             pltpu.VMEM((8, rows), f32),
             pltpu.VMEM((rows, width), f32),
+            pltpu.VMEM((rows, 128), f32),
             pltpu.VMEM((2, rows, width), bf),
             pltpu.VMEM((2, NC, width // NC, rows), bf),
             pltpu.SemaphoreType.DMA((4,)),
@@ -617,7 +620,7 @@
             collective_id=0, has_side_effects=True, vmem_limit_bytes=60 * MIB
         ),
         name="layer",
-    )(q_in, d_in, gain.reshape(1, width), tags, column_tag, w_in, w_out)
+    )(q_in, d_in, gain.reshape(1, width), cluster.reshape(1, rows), w_in, w_out)
 
 
 PARTS = (
@@ -1001,11 +1004,9 @@
 
 
 def on_device(query_in, doc_in, cluster, gain, w_in, w_out):
-    rows, width = query_in.shape
-    tags = jnp.broadcast_to(cluster.astype(jnp.bfloat16)[None, :], (16, rows))
-    column_tag = cluster.astype(jnp.float32)[:, None]
+    width = query_in.shape[1]
     up, upt, loss_part, hidden, slope, o_in, o_out = layer(
-        query_in, doc_in, gain, tags, column_tag, w_in, w_out
+        query_in, doc_in, gain, cluster, w_in, w_out
     )
     sums = backward(
         query_in, doc_in, up, upt, gain, loss_part, hidden, slope, w_in, o_in, w_out, o_out

time: 150 us -> 148 us (0.987)
  no operation moved by 1% of the time
where the time goes in v7:
time: 148 us; the launch traced here: 147 us
  Pallas kernels  147 us (99%)
    pallas_call x1, Pallas kernels, layer(): pl.pallas_call(layer_kernel, out_shape=(jax.ShapeDtypeStruct((2 * rows, w...  100 us
    pallas_call x1, Pallas kernels, backward(): pl.pallas_call(backward_kernel, out_shape=(jax.ShapeDtypeStruct((GROUP, h...  44 us

profile of v7, /device:TPU:0, one launch (start us, length us, event | category | flops | bytes accessed | tf_op | source)
XLA Modules:
  0.0 147.5 jit_solution(16327768931923237855)
XLA Ops:
  0.6 100.5 %layer.1 = (bf16[512,1024]{1,0:T(8,128)(2,1)}, bf16[2,2,512,256]{3,2,1,0:T(8,128)(2,1)}, f32[8,128]{1,0:T(8,128)}, bf16[4,512,1024]{2,1,0:T(8,128)(2,1)}, bf16[4...) custom-call(bf16[256,1024]{1,0:T(8,128)(2,1)} %q_hbm.1, bf16[256,1024]{1,0:T(8,128)(2,1)} %d_hbm.1, ...), custom_call_target="tpu_custom_call" | custom-call | tf_op jit(solution)/shard_map/layer/pallas_call | solution.py:575
  101.1 44.0 %backward.1 = (f32[16,2048]{1,0:T(8,128)}, f32[8,1024]{1,0:T(8,128)}, bf16[512,1024]{1,0:T(8,128)(2,1)}) custom-call(bf16[256,1024]{1,0:T(8,128)(2,1)} %q_hbm.1, bf16[256,1024]{1,0:T(8,128)(2,1)} %d_hbm.1, bf16[512,1024]{1,0:T(8,128)(2,1)} %get-tuple-element.20.up_hbm, bf16[2,2,512,256]{3,2,1,0:T(8,128)(2,1)} %get-tuple-element.21.upt_hbm, ...), custom_call_target="tpu_custom_call" | custom-call | tf_op jit(solution)/shard_map/backward/pallas_call | solution.py:925
  145.1 2.4 %finish.1 = (f32[16,2048]{1,0:T(8,128)}, f32[1,1024]{1,0:T(1,128)}, f32[1,1]{1,0:T(1,128)}, bf16[256,1024]{1,0:T(8,128)(2,1)}, bf16[256,1024]{1,0:T(8,128)(2,1)}) custom-call(f32[16,2048]{1,0:T(8,128)} %get-tuple-element.27.down, f32[8,1024]{1,0:T(8,128)} %get-tuple-element.28.total, bf16[512,1024]{1,0:T(8,128)(2,1)} %get-tuple-element.29.grads), custom_call_target="tpu_custom_call" | custom-call | tf_op jit(solution)/shard_map/finish/pallas_call | solution.py:993

commit v8 on v7

--- a/solution.py
+++ b/solution.py
@@ -730,19 +730,23 @@
     wait1 = []
     for op in first_loads:
         op.wait()
-    n_loaded = 0
-    for k, first, count, _ in PARTS:
+    loaded = []
+
+    def for_sibling(p):
+        k, first, count, _ = PARTS[p]
         at = slice(first, first + count)
-        while n_loaded * cols < k * half + first + count:
-            loads[n_loaded].wait()
-            n_loaded += 1
+        while len(loaded) * cols < k * half + first + count:
+            loads[len(loaded)].wait()
+            loaded.append(1)
         s1[k, :, at] = down_part(1 - c, k, at).astype(jnp.bfloat16)
         view = (k, slice(None), pl.ds(first, count))
         wait1.append(send(s1.at[view], r1.at[view], sibling))
 
     wait2 = []
     waitz = []
-    for p, (k, first, count, axis) in enumerate(PARTS):
+
+    def for_links(p):
+        k, first, count, axis = PARTS[p]
         at = slice(first, first + count)
         mine = down_part(c, k, at)
         wait1[p].wait_recv()
@@ -765,6 +769,13 @@
                 src = a1.at[k, :, wrap(y + n, NY), :, :, part]
                 waits.append(send(src, r2.at[k, 1, slot], ys[n - 1]))
         wait2.append(waits)
+
+    ahead = 3
+    for p in range(len(PARTS) + ahead):
+        if p < len(PARTS):
+            for_sibling(p)
+        if p >= ahead:
+            for_links(p - ahead)
 
     for j in range(CHUNKS):
         loads[CHUNKS + j].wait()

time: 148 us -> 148 us (level)
  no operation moved by 1% of the time
where the time goes in v8:
time: 148 us; the launch traced here: 147 us
  Pallas kernels  146 us (99%)
    pallas_call x1, Pallas kernels, layer(): pl.pallas_call(layer_kernel, out_shape=(jax.ShapeDtypeStruct((2 * rows, w...  100 us
    pallas_call x1, Pallas kernels, backward(): pl.pallas_call(backward_kernel, out_shape=(jax.ShapeDtypeStruct((GROUP, h...  43.5 us

profile of v8, /device:TPU:0, one launch (start us, length us, event | category | flops | bytes accessed | tf_op | source)
XLA Modules:
  0.0 147.0 jit_solution(9670707921105745815)
XLA Ops:
  0.6 100.5 %layer.1 = (bf16[512,1024]{1,0:T(8,128)(2,1)}, bf16[2,2,512,256]{3,2,1,0:T(8,128)(2,1)}, f32[8,128]{1,0:T(8,128)}, bf16[4,512,1024]{2,1,0:T(8,128)(2,1)}, bf16[4...) custom-call(bf16[256,1024]{1,0:T(8,128)(2,1)} %q_hbm.1, bf16[256,1024]{1,0:T(8,128)(2,1)} %d_hbm.1, ...), custom_call_target="tpu_custom_call" | custom-call | tf_op jit(solution)/shard_map/layer/pallas_call | solution.py:575
  101.1 43.5 %backward.1 = (f32[16,2048]{1,0:T(8,128)}, f32[8,1024]{1,0:T(8,128)}, bf16[512,1024]{1,0:T(8,128)(2,1)}) custom-call(bf16[256,1024]{1,0:T(8,128)(2,1)} %q_hbm.1, bf16[256,1024]{1,0:T(8,128)(2,1)} %d_hbm.1, bf16[512,1024]{1,0:T(8,128)(2,1)} %get-tuple-element.20.up_hbm, bf16[2,2,512,256]{3,2,1,0:T(8,128)(2,1)} %get-tuple-element.21.upt_hbm, ...), custom_call_target="tpu_custom_call" | custom-call | tf_op jit(solution)/shard_map/backward/pallas_call | solution.py:936
  144.6 2.4 %finish.1 = (f32[16,2048]{1,0:T(8,128)}, f32[1,1024]{1,0:T(1,128)}, f32[1,1]{1,0:T(1,128)}, bf16[256,1024]{1,0:T(8,128)(2,1)}, bf16[256,1024]{1,0:T(8,128)(2,1)}) custom-call(f32[16,2048]{1,0:T(8,128)} %get-tuple-element.27.down, f32[8,1024]{1,0:T(8,128)} %get-tuple-element.28.total, bf16[512,1024]{1,0:T(8,128)(2,1)} %get-tuple-element.29.grads), custom_call_target="tpu_custom_call" | custom-call | tf_op jit(solution)/shard_map/finish/pallas_call | solution.py:1004
